TPU v7x, 32 devices: a whole 2x2x4 slice. The times are simulated.
32 devices in a mesh: grp: 4 (over x, core), fs: 8 (over z, y).
Axes of the slice: x: 2, y: 2, z: 4, core: 2. Of those that a mesh axis runs over, the one named last changes fastest.
Arguments:
- image_patches: bfloat16 [32, 24, 24, 384], P(('grp', 'fs')), may hold values from -6 to 6
- cotangent: bfloat16 [32, 24, 24, 384], P(('grp', 'fs')), may hold values from -6 to 6
- image_count: int32 [4, 8], P('grp', 'fs'), may hold values from 0 to 1, as said below
- resolution: int32 [32], P(('grp', 'fs')), may hold values from 14 to 24, as said below
- owner_list: int32 [6], replicated, may hold values from 0 to 3, as said below
- focal_weight: float32 [4, 384, 768], P('grp', 'fs'), may hold values from -0.3125 to 0.3125
- focal_first: float32 [4, 384, 768], P('grp', 'fs'), may hold values from -96 to 96
- focal_second: float32 [4, 384, 768], P('grp', 'fs'), may hold values from 480 to 7520
- modulate_weight: float32 [4, 384, 384], P('grp', 'fs'), may hold values from -0.3125 to 0.3125
- modulate_first: float32 [4, 384, 384], P('grp', 'fs'), may hold values from -112 to 112
- modulate_second: float32 [4, 384, 384], P('grp', 'fs'), may hold values from 768 to 12320
- project_weight: float32 [4, 384, 384], P('grp', 'fs'), may hold values from -0.3125 to 0.3125
- project_first: float32 [4, 384, 384], P('grp', 'fs'), may hold values from -112 to 112
- project_second: float32 [4, 384, 384], P('grp', 'fs'), may hold values from 768 to 12320
- expand_weight: float32 [4, 384, 1536], P('grp', 'fs'), may hold values from -0.3125 to 0.3125
- expand_first: float32 [4, 384, 1536], P('grp', 'fs'), may hold values from -40 to 40
- expand_second: float32 [4, 384, 1536], P('grp', 'fs'), may hold values from 86.4 to 1376
- shrink_weight: float32 [4, 1536, 384], P('grp', 'fs'), may hold values from -0.15625 to 0.15625
- shrink_first: float32 [4, 1536, 384], P('grp', 'fs'), may hold values from -64 to 64
- shrink_second: float32 [4, 1536, 384], P('grp', 'fs'), may hold values from 288 to 4608
- vector_weight: float32 [4, 102, 384], P('grp', None, 'fs'), as said below
- vector_first: float32 [4, 102, 384], P('grp', None, 'fs'), may hold values from -80 to 80
- vector_second: float32 [4, 102, 384], P('grp', None, 'fs'), may hold values from 384 to 6560
Outputs:
- block_output: bfloat16 [32, 24, 24, 384], P(('grp', 'fs'))
- input_grad: float32 [32, 24, 24, 384], P(('grp', 'fs'))
- focal_new: float32 [4, 384, 768], P('grp', 'fs')
- focal_first_new: float32 [4, 384, 768], P('grp', 'fs')
- focal_second_new: float32 [4, 384, 768], P('grp', 'fs')
- modulate_new: float32 [4, 384, 384], P('grp', 'fs')
- modulate_first_new: float32 [4, 384, 384], P('grp', 'fs')
- modulate_second_new: float32 [4, 384, 384], P('grp', 'fs')
- project_new: float32 [4, 384, 384], P('grp', 'fs')
- project_first_new: float32 [4, 384, 384], P('grp', 'fs')
- project_second_new: float32 [4, 384, 384], P('grp', 'fs')
- expand_new: float32 [4, 384, 1536], P('grp', 'fs')
- expand_first_new: float32 [4, 384, 1536], P('grp', 'fs')
- expand_second_new: float32 [4, 384, 1536], P('grp', 'fs')
- shrink_new: float32 [4, 1536, 384], P('grp', 'fs')
- shrink_first_new: float32 [4, 1536, 384], P('grp', 'fs')
- shrink_second_new: float32 [4, 1536, 384], P('grp', 'fs')
- vector_new: float32 [4, 102, 384], P('grp', None, 'fs')
- vector_first_new: float32 [4, 102, 384], P('grp', None, 'fs')
- vector_second_new: float32 [4, 102, 384], P('grp', None, 'fs')
Inputs may be any that keep to these rules, and one draw needn't show every extreme that they name: A device's first image_count slots hold images, the others are padding. The device at the head of both axes holds none, and in every draw some devices hold 1. `resolution`: each image is 14, 16 or 24 patches on a side (images of 224, 256 and 384 pixels); both 14 and 24 occur in every draw. `owner_list`: owners in the order focal, modulate, project, expand, shrink, vector; group 0 and group 4 - 1 own something in every draw. `vector_weight`: rows 0 and 7 lie in 0.5 to 1.5, rows 6 and 10 in 1 to 2.5.
All inputs are finite; a program needn't handle non-finite values.
Results may differ from a plain program's by a relative error of at most 0.0097.
Values may be sent and summed in bfloat16 or wider, within the bound.
A program may use at most 128 MiB of HBM per device.

v0:
```python
import math

import jax
import jax.numpy as jnp
from jax import lax
from jax.sharding import PartitionSpec as P

C = 384
HID = 1536
LEVELS = 3
GATES = 4
STEP = 10
TENSORS = 6


highest = lax.Precision.HIGHEST
beta_one = 0.9
beta_two = 0.95
adam_eps = 1e-08
weight_decay = 0.05
norm_eps = 1e-05


def from_root(array, axis, root):
    mine = lax.axis_index(axis) == root
    return lax.psum(jnp.where(mine, array, jnp.zeros_like(array)), axis)


def layer_norm(values, norm_gain, norm_shift):
    row_mean = jnp.mean(values, axis=-1, keepdims=True)
    centred = values - row_mean
    row_var = jnp.mean(centred * centred, axis=-1, keepdims=True)
    return centred * lax.rsqrt(row_var + norm_eps) * norm_gain + norm_shift


def gelu_exact(values):
    return jax.nn.gelu(values, approximate=False)


def depthwise(feature_map, kernel):
    return lax.conv_general_dilated(
        feature_map,
        kernel,
        (1, 1),
        "SAME",
        dimension_numbers=("NHWC", "HWIO", "NHWC"),
        feature_group_count=feature_map.shape[-1],
        precision=highest,
    )


def focal_context(context, gate_values, kernel_rows, live_mask, live_area):
    current = context * live_mask
    combined = jnp.zeros_like(context)
    offset = 0
    for number in range(LEVELS):
        kernel_side = 2 * number + 3
        kernel = kernel_rows[offset : offset + kernel_side * kernel_side].reshape(
            kernel_side, kernel_side, 1, -1
        )
        offset = offset + kernel_side * kernel_side
        current = gelu_exact(depthwise(current, kernel)) * live_mask
        combined = combined + current * gate_values[..., number : number + 1]
    pooled = gelu_exact(jnp.sum(current, axis=(1, 2)) / live_area[:, None])
    return combined + pooled[:, None, None, :] * gate_values[..., LEVELS : LEVELS + 1]


def split_vector(vector):
    channels = vector.shape[1]
    bias_rows = HID // channels
    single_rows = [vector[row_index] for row_index in range(11)]
    expand_bias = vector[11 : 11 + bias_rows].reshape(-1)
    gate_rows = vector[11 + bias_rows : 11 + bias_rows + GATES]
    kernel_rows = vector[11 + bias_rows + GATES :]
    return (single_rows, expand_bias, gate_rows, kernel_rows)


def image_mask(live_count, resolution, grid_side):
    slot_index = jnp.arange(resolution.shape[0])
    cell_index = jnp.arange(grid_side)
    inside = cell_index[None, :] < resolution[:, None]
    is_live = slot_index < live_count
    joint_mask = is_live[:, None, None] & inside[:, :, None] & inside[:, None, :]
    live_area = (resolution * resolution).astype(jnp.float32)
    return (joint_mask.astype(jnp.float32)[..., None], live_area)


def tensor_rates():
    wide_rate = 1.5 / math.sqrt(C)
    return (wide_rate, wide_rate, wide_rate, wide_rate, 1.5 / math.sqrt(HID), 0.2)


def adam_step(weight, first_moment, second_moment, gradient, step_rate):
    first_new = beta_one * first_moment + (1.0 - beta_one) * gradient
    second_new = beta_two * second_moment + (1.0 - beta_two) * gradient * gradient
    first_hat = first_new / (1.0 - beta_one**STEP)
    second_hat = second_new / (1.0 - beta_two**STEP)
    weight_new = weight - step_rate * (
        first_hat / (jnp.sqrt(second_hat) + adam_eps) + weight_decay * weight
    )
    return (weight_new, first_new, second_new)


def matmul_plain(left_side, right_side):
    return jnp.dot(left_side, right_side, preferred_element_type=jnp.float32)


def matmul_left(left_side, right_side):
    return lax.dot_general(
        left_side, right_side, (((0,), (0,)), ((), ())), preferred_element_type=jnp.float32
    )


def matmul_right(left_side, right_side):
    return lax.dot_general(
        left_side, right_side, (((1,), (1,)), ((), ())), preferred_element_type=jnp.float32
    )


def shards(
    image_patches,
    cotangent,
    image_count,
    resolution,
    owner_list,
    focal_weight,
    focal_first,
    focal_second,
    modulate_weight,
    modulate_first,
    modulate_second,
    project_weight,
    project_first,
    project_second,
    expand_weight,
    expand_first,
    expand_second,
    shrink_weight,
    shrink_first,
    shrink_second,
    vector_weight,
    vector_first,
    vector_second,
):
    matrices = (focal_weight, modulate_weight, project_weight, expand_weight, shrink_weight)
    old_weights = matrices + (vector_weight,)
    all_firsts = (
        focal_first,
        modulate_first,
        project_first,
        expand_first,
        shrink_first,
        vector_first,
    )
    all_seconds = (
        focal_second,
        modulate_second,
        project_second,
        expand_second,
        shrink_second,
        vector_second,
    )
    shares = tuple(
        (
            from_root(stacked[0].astype(jnp.bfloat16), "grp", owner_list[row_index])
            for row_index, stacked in enumerate(matrices)
        )
    )
    vector_share = from_root(vector_weight[0], "grp", owner_list[5])
    weights = (
        lax.all_gather(shares[0], "fs", axis=0, tiled=True),
        lax.all_gather(shares[1], "fs", axis=0, tiled=True),
        lax.all_gather(shares[2], "fs", axis=0, tiled=True),
        lax.all_gather(shares[3], "fs", axis=0, tiled=True),
        lax.all_gather(shares[4], "fs", axis=0, tiled=True),
    )
    vector = lax.all_gather(vector_share, "fs", axis=1, tiled=True)
    single_rows, expand_bias, gate_rows, kernel_rows = split_vector(vector)
    (
        first_gain,
        first_shift,
        query_bias,
        context_bias,
        modulate_bias,
        project_bias,
        first_scale,
        second_gain,
        second_shift,
        shrink_bias,
        second_scale,
    ) = single_rows
    channels = image_patches.shape[-1]
    grid_shape = image_patches.shape[:3]
    live_mask, live_area = image_mask(image_count[0, 0], resolution, image_patches.shape[1])
    flat_mask = live_mask.reshape(-1, 1)
    inputs = image_patches.astype(jnp.float32).reshape(-1, channels)
    normed, first_pull = jax.vjp(layer_norm, inputs, first_gain, first_shift)
    normed_low = normed.astype(jnp.bfloat16)
    pre_focal = matmul_plain(normed_low, weights[0])
    query_rows = pre_focal[:, :channels] + query_bias
    context = pre_focal[:, channels:] + context_bias
    gate_values = jnp.dot(normed, gate_rows.T, precision=highest)

    def context_map(context_rows, gate_input, kernel_input):
        return focal_context(
            context_rows.reshape(grid_shape + (channels,)),
            gate_input.reshape(grid_shape + (GATES,)),
            kernel_input,
            live_mask,
            live_area,
        ).reshape(-1, channels)

    summed, focal_pull = jax.vjp(context_map, context, gate_values, kernel_rows)
    summed_low = summed.astype(jnp.bfloat16)
    modulator = matmul_plain(summed_low, weights[1]) + modulate_bias
    mixed_rows = query_rows * modulator
    mixed_low = mixed_rows.astype(jnp.bfloat16)
    projected = matmul_plain(mixed_low, weights[2]) + project_bias
    middle = inputs + first_scale * projected
    second, second_pull = jax.vjp(layer_norm, middle, second_gain, second_shift)
    second_low = second.astype(jnp.bfloat16)
    hidden = matmul_plain(second_low, weights[3]) + expand_bias
    active, gelu_pull = jax.vjp(gelu_exact, hidden)
    active_low = active.astype(jnp.bfloat16)
    shrunk = matmul_plain(active_low, weights[4]) + shrink_bias
    block_output = (
        ((middle + second_scale * shrunk) * flat_mask)
        .astype(jnp.bfloat16)
        .reshape(image_patches.shape)
    )
    backward_weights = (
        lax.all_gather(shares[0], "fs", axis=0, tiled=True),
        lax.all_gather(shares[1], "fs", axis=0, tiled=True),
        lax.all_gather(shares[2], "fs", axis=0, tiled=True),
        lax.all_gather(shares[3], "fs", axis=0, tiled=True),
        lax.all_gather(shares[4], "fs", axis=0, tiled=True),
    )
    upstream = cotangent.astype(jnp.float32).reshape(-1, channels) * flat_mask
    grad_scale_two = jnp.sum(upstream * shrunk, axis=0)
    back_shrunk = upstream * second_scale
    grad_shrink_bias = jnp.sum(back_shrunk, axis=0)
    back_shrunk_low = back_shrunk.astype(jnp.bfloat16)
    grad_shrink = matmul_left(active_low, back_shrunk_low)
    back_active = matmul_right(back_shrunk_low, backward_weights[4])
    (back_hidden,) = gelu_pull(back_active)
    grad_expand_bias = jnp.sum(back_hidden, axis=0)
    back_hidden_low = back_hidden.astype(jnp.bfloat16)
    grad_expand = matmul_left(second_low, back_hidden_low)
    back_second = matmul_right(back_hidden_low, backward_weights[3])
    back_middle, grad_second_gain, grad_second_shift = second_pull(back_second)
    back_middle = back_middle + upstream
    grad_scale_one = jnp.sum(back_middle * projected, axis=0)
    back_projected = back_middle * first_scale
    grad_project_bias = jnp.sum(back_projected, axis=0)
    back_projected_low = back_projected.astype(jnp.bfloat16)
    grad_project = matmul_left(mixed_low, back_projected_low)
    back_mixed = matmul_right(back_projected_low, backward_weights[2])
    back_query = back_mixed * modulator
    back_modulator = back_mixed * query_rows
    grad_modulate_bias = jnp.sum(back_modulator, axis=0)
    back_modulator_low = back_modulator.astype(jnp.bfloat16)
    grad_modulate = matmul_left(summed_low, back_modulator_low)
    back_summed = matmul_right(back_modulator_low, backward_weights[1])
    back_context, back_gates, grad_kernels = focal_pull(back_summed)
    grad_query_bias = jnp.sum(back_query, axis=0)
    grad_context_bias = jnp.sum(back_context, axis=0)
    back_pre_low = jnp.concatenate([back_query, back_context], axis=1).astype(jnp.bfloat16)
    grad_focal = matmul_left(normed_low, back_pre_low)
    grad_gates = jnp.dot(back_gates.T, normed, precision=highest)
    back_normed = matmul_right(back_pre_low, backward_weights[0]) + jnp.dot(
        back_gates, gate_rows, precision=highest
    )
    back_inputs, grad_first_gain, grad_first_shift = first_pull(back_normed)
    input_grad = (back_inputs + back_middle).reshape(image_patches.shape)
    grad_vector = jnp.concatenate(
        [
            jnp.stack(
                [
                    grad_first_gain,
                    grad_first_shift,
                    grad_query_bias,
                    grad_context_bias,
                    grad_modulate_bias,
                    grad_project_bias,
                    grad_scale_one,
                    grad_second_gain,
                    grad_second_shift,
                    grad_shrink_bias,
                    grad_scale_two,
                ]
            ),
            grad_expand_bias.reshape(-1, channels),
            grad_gates,
            grad_kernels,
        ],
        axis=0,
    )
    reduced = (
        lax.psum_scatter(grad_focal, "fs", scatter_dimension=0, tiled=True),
        lax.psum_scatter(grad_modulate, "fs", scatter_dimension=0, tiled=True),
        lax.psum_scatter(grad_project, "fs", scatter_dimension=0, tiled=True),
        lax.psum_scatter(grad_expand, "fs", scatter_dimension=0, tiled=True),
        lax.psum_scatter(grad_shrink, "fs", scatter_dimension=0, tiled=True),
        lax.psum_scatter(grad_vector, "fs", scatter_dimension=1, tiled=True),
    )
    totals = lax.psum(
        (reduced[0], reduced[1], reduced[2], reduced[3], reduced[4], reduced[5]), "grp"
    )
    group_index = lax.axis_index("grp")
    step_rates = tensor_rates()
    outputs = [block_output, input_grad]
    for row_index in range(TENSORS):
        is_owner = group_index == owner_list[row_index]
        updated = adam_step(
            old_weights[row_index][0],
            all_firsts[row_index][0],
            all_seconds[row_index][0],
            totals[row_index],
            step_rates[row_index],
        )
        for new_value in updated:
            outputs.append(jnp.where(is_owner, new_value, 0.0)[None])
    return tuple(outputs)


def solution(mesh):
    placed = (
        P(("grp", "fs"), None, None, None),
        P(("grp", "fs"), None, None, None),
        P("grp", "fs"),
        P(("grp", "fs")),
        P(),
        P("grp", "fs", None),
        P("grp", "fs", None),
        P("grp", "fs", None),
        P("grp", "fs", None),
        P("grp", "fs", None),
        P("grp", "fs", None),
        P("grp", "fs", None),
        P("grp", "fs", None),
        P("grp", "fs", None),
        P("grp", "fs", None),
        P("grp", "fs", None),
        P("grp", "fs", None),
        P("grp", "fs", None),
        P("grp", "fs", None),
        P("grp", "fs", None),
        P("grp", None, "fs"),
        P("grp", None, "fs"),
        P("grp", None, "fs"),
    )
    return jax.shard_map(
        shards,
        mesh=mesh,
        in_specs=placed,
        out_specs=(
            P(("grp", "fs"), None, None, None),
            P(("grp", "fs"), None, None, None),
            P("grp", "fs", None),
            P("grp", "fs", None),
            P("grp", "fs", None),
            P("grp", "fs", None),
            P("grp", "fs", None),
            P("grp", "fs", None),
            P("grp", "fs", None),
            P("grp", "fs", None),
            P("grp", "fs", None),
            P("grp", "fs", None),
            P("grp", "fs", None),
            P("grp", "fs", None),
            P("grp", "fs", None),
            P("grp", "fs", None),
            P("grp", "fs", None),
            P("grp", None, "fs"),
            P("grp", None, "fs"),
            P("grp", None, "fs"),
        ),
        check_vma=False,
    )
```

profile of v0, /device:TPU:0, one launch (start us, length us, event | category | flops | bytes accessed | tf_op | source)
XLA Modules:
  0.0 725.5 jit_solution(6624341218473402930)
XLA Ops:
  7.3 1.5 fusion.189
  10.0 1.6 fusion.151
  13.6 1.6 fusion.134
  15.3 1.6 fusion.133
  18.9 12.9 %psum.84 = f32[102,48]{0,1:T(8,128)S(1)} all-reduce(f32[102,48]{0,1:T(8,128)S(1)} %bitcast_select_fusion), channel_id=1, replica_groups=mesh['grp'=4,'fs'=8] {'grp'}, use_global_device_ids=true, to_apply=%region_0.1 | all-reduce | flops 4896 | bytes 39168 | tf_op jit(solution)/shard_map/psum | solution.py:26
  31.9 31.1 %all_gather.23 = f32[102,384]{0,1:T(8,128)S(1)} all-gather(f32[102,48]{0,1:T(8,128)S(1)} %psum.84), channel_id=1, replica_groups=mesh['grp'=4,'fs'=8] {'fs'}, dimensions={1}, use_global_device_ids=true | all-gather | bytes 176256 | tf_op jit(solution)/shard_map/all_gather | solution.py:177
  62.9 1.7 slice_reduce_fusion.3
  70.7 3.2 convolution_bitcast_fusion
  77.3 31.1 %all_gather.25 = bf16[384,384]{1,0:T(8,128)(2,1)S(1)} all-gather(bf16[48,384]{1,0:T(8,128)(2,1)} %get-tuple-element.91), channel_id=1, replica_groups=mesh['grp'=4,'fs'=8] {'fs'}, dimensions={0}, use_global_device_ids=true | all-gather | bytes 331776 | tf_op jit(solution)/shard_map/all_gather | solution.py:172
  108.4 33.0 %all_gather.26 = bf16[384,384]{1,0:T(8,128)(2,1)} all-gather(bf16[48,384]{1,0:T(8,128)(2,1)} %get-tuple-element.92), channel_id=1, replica_groups=mesh['grp'=4,'fs'=8] {'fs'}, dimensions={0}, use_global_device_ids=true | all-gather | bytes 331776 | tf_op jit(solution)/shard_map/all_gather | solution.py:173
  141.4 32.1 %all_gather.24 = bf16[384,768]{1,0:T(8,128)(2,1)S(1)} all-gather(bf16[48,768]{1,0:T(8,128)(2,1)} %get-tuple-element.93), channel_id=1, replica_groups=mesh['grp'=4,'fs'=8] {'fs'}, dimensions={0}, use_global_device_ids=true | all-gather | bytes 663552 | tf_op jit(solution)/shard_map/all_gather | solution.py:171
  176.9 3.2 broadcast_multiply_fusion.1
  182.8 4.8 broadcast_multiply_fusion
  189.6 4.5 fusion.104
  194.1 3.5 fusion.185
  200.0 1.0 slice.168
  201.7 1.0 slice.169
  203.3 1.0 slice.163
  205.0 1.0 slice.164
  206.8 1.0 slice.165
  209.1 1.4 multiply_convert_fusion.3
  210.5 1.4 multiply_add_fusion.2
  215.4 11.6 %multiply_convert_fusion = (bf16[576,1536]{1,0:T(8,128)(2,1)}, f32[576,1536]{1,0:T(8,128)}, f32[576,1536]{1,0:T(8,128)}) fusion(f32[1536]{0:T(1024)} %add.295, bf16[384,1536]{1,0:T(8,128)(2,1)} %all-gather.3.cloned.1.call-done, f32[576,384]{1,0:T(8,128)S(1)} %get-tuple-element.163, f32[384]{0:T(512)} %get-tuple-element.77, f32[384]{0:T(512)} %get-tuple-element.78, ...), kind=kOutput, calls=%fused_computation.3 | convolution fusion | flops 738975744 | bytes 10925568 | tf_op jit(solution)/shard_map/dot_general | solution.py:105
  227.0 29.8 %all-gather.5.cloned.1.call-done = bf16[1536,384]{1,0:T(8,128)(2,1)} async-done(((bf16[192,384]{1,0:T(8,128)(2,1)}), bf16[1536,384]{1,0:T(8,128)(2,1)}) %all-gather.5.cloned.1.call-update) | async-done | bytes 1179664 | tf_op jit(solution)/shard_map/all_gather | solution.py:175
  256.8 6.2 fusion.190
  263.1 1.8 multiply_reduce_fusion.2
  265.6 2.6 multiply_reduce_fusion
  269.2 1.3 fusion.130
  270.5 3.5 fusion.124
  274.3 2.3 multiply_reduce_fusion.10
  276.7 2.0 multiply_add_fusion.1
  279.7 4.6 fusion.101
  285.9 1.2 pad.32
  287.1 2.6 reshape.665
  289.7 1.3 copy.230
  291.8 2.2 fusion.35
  294.8 1.0 slice.167
  296.2 1.3 fusion.192
  297.6 4.6 multiply_reduce_fusion.8
  303.2 1.2 pad.34
  304.4 1.6 reshape.670
  309.8 1.7 fusion.99
  311.6 1.1 copy-done.8
  312.7 4.1 fusion.85
  318.0 1.1 broadcast_multiply_fusion.2
  319.1 1.1 fusion.225
  320.3 2.8 fusion.193
  324.2 18.2 %convolution_reduce_fusion = f32[5,5,384]{2,1,0:T(8,128)S(1)} fusion(f32[1,24,24,384]{3,2,1,0:T(8,128)S(1)} %copy-done.24, f32[1,24,24,384]{3,2,1,0:T(8,128)} %fusion.225), kind=kOutput, calls=%fused_computation.84 | convolution fusion | flops 59885568 | bytes 1807872 | tf_op jit(solution)/shard_map/transpose(jvp())/conv_general_dilated | solution.py:41
  347.1 34.6 %convolution_reduce_fusion.1 = f32[7,7,384]{2,1,0:T(8,128)S(1)} fusion(f32[1,24,24,384]{3,2,1,0:T(8,128)} %copy-done.37, f32[1,24,24,384]{3,2,1,0:T(8,128)S(1)} %copy-done.36), kind=kOutput, calls=%fused_computation.85 | convolution fusion | flops 112140288 | bytes 1844736 | tf_op jit(solution)/shard_map/transpose(jvp())/conv_general_dilated | solution.py:41
  382.5 8.1 %convolution_reduce_fusion.2 = f32[3,3,384]{2,1,0:T(4,128)S(1)} fusion(f32[1,24,24,384]{3,2,1,0:T(8,128)S(1)} %copy-done.16, f32[1,24,24,384]{3,2,1,0:T(8,128)} %broadcast_multiply_fusion.2), kind=kOutput, calls=%fused_computation.87 | convolution fusion | flops 22579200 | bytes 1783296 | tf_op jit(solution)/shard_map/transpose(jvp())/conv_general_dilated | solution.py:41
  392.6 1.4 fusion.128
  394.1 2.6 multiply_reduce_fusion.4
  399.8 66.4 %reduce-scatter.9.cloned.1.call-done = f32[48,768]{1,0:T(8,128)} async-done(((f32[384,768]{1,0:T(8,128)}), f32[48,768]{1,0:T(8,128)}) %reduce-scatter.9.cloned.1.call-update) | async-done | bytes 147472 | tf_op jit(solution)/shard_map/reduce_scatter | solution.py:299
  466.2 71.5 %reduce-scatter.15.cloned.1.call-done = f32[48,1536]{1,0:T(8,128)} async-done(((f32[384,1536]{1,0:T(8,128)}), f32[48,1536]{1,0:T(8,128)}) %reduce-scatter.15.cloned.1.call-update) | async-done | bytes 294928 | tf_op jit(solution)/shard_map/reduce_scatter | solution.py:302
  537.7 71.6 %reduce-scatter.17.cloned.1.call-done = f32[192,384]{1,0:T(8,128)} async-done(((f32[1536,384]{1,0:T(8,128)}), f32[192,384]{1,0:T(8,128)}) %reduce-scatter.17.cloned.1.call-update) | async-done | bytes 294928 | tf_op jit(solution)/shard_map/reduce_scatter | solution.py:303
  609.4 1.1 add_add_fusion.2
  610.5 62.6 %reduce-scatter.19.cloned.1.call-done = f32[48,102]{1,0:T(8,128)} async-done(((f32[384,102]{1,0:T(8,128)}), f32[48,102]{1,0:T(8,128)}) %reduce-scatter.19.cloned.1.call-update) | async-done | bytes 19600
  673.1 11.2 %psum.95 = f32[102,48]{0,1:T(8,128)S(1)} all-reduce(f32[102,48]{0,1:T(8,128)} %bitcast.448), channel_id=1, replica_groups=mesh['grp'=4,'fs'=8] {'grp'}, use_global_device_ids=true, to_apply=%region_43.44 | all-reduce | flops 4896 | bytes 39168 | tf_op jit(solution)/shard_map/psum | solution.py:306
  685.0 26.1 %all-reduce.14.cloned.1.call-done = (f32[48,768]{1,0:T(8,128)}, f32[48,384]{1,0:T(8,128)}, f32[48,384]{1,0:T(8,128)}, f32[48,1536]{1,0:T(8,128)}, f32[192,384]{1,0:T(8,128)}) async-done(((f32[48,768]{1,0:T(8,128)}, f32[48,384]{1,0:T(8,128)}, f32[48,384]{1,0:T(8,128)}, f32[48,1536]{1,0:T(8,128)}, f32[192,384]{1,0:T(8,128)}), (f32[48,768]{1,0:T(8,128)}, f32[48,384]{1,0:T(8,128)}, f32[48,384]{1,0:T(8,128)}, ...) | async-done | bytes 884752 | tf_op jit(solution)/shard_map/psum | solution.py:306
  711.1 1.7 select_bitcast_fusion.8
  712.8 1.6 select_bitcast_fusion.6
  714.4 1.8 select_bitcast_fusion.4
  716.3 1.2 select_bitcast_fusion.2
  717.5 1.2 select_bitcast_fusion
  (429 shorter events, 51.6 us)
Async XLA Ops:
  7.2 9.7 %copy-start.38 = (f32[1,48,768]{2,1,0:T(8,128)S(1)}, f32[1,48,768]{2,1,0:T(8,128)}, u32[]{:S(2)}) copy-start(f32[1,48,768]{2,1,0:T(8,128)} %param.28) | copy-start | bytes 442372
  7.2 10.4 %copy-start.2 = (bf16[1,24,24,384]{3,2,1,0:T(8,128)(2,1)S(1)}, bf16[1,24,24,384]{3,2,1,0:T(8,128)(2,1)}, u32[]{:S(2)}) copy-start(bf16[1,24,24,384]{3,2,1,0:T(8,128)(2,1)} %param.23) | copy-start | bytes 1327108
  7.2 70.1 %all-reduce.16.cloned.1.call-start = ((), (), s32[]{:S(2)}) async-start(), calls=%async_computation.15 | async-start | bytes 147456 | tf_op jit(solution)/shard_map/psum | solution.py:26
  11.6 129.7 %all-reduce.18.cloned.1.call-start = ((), (), s32[]{:S(2)}) async-start(), calls=%async_computation.16 | async-start | bytes 737280 | tf_op jit(solution)/shard_map/psum | solution.py:26
  17.6 197.8 %all-gather.3.cloned.1.call-start = ((), (), s32[]{:S(2)}) async-start(), calls=%async_computation.6 | async-start | bytes 1327104 | tf_op jit(solution)/shard_map/all_gather | solution.py:174
  17.8 52.8 %copy-start.59 = (f32[24,24]{1,0:T(8,128)}, f32[24,24]{1,0:T(8,128)S(1)}, u32[]{:S(2)}) copy-start(f32[24,24]{1,0:T(8,128)S(1)} %broadcast_multiply_fusion.3) | copy-start | bytes 6916
  17.9 58.0 %copy-start.83 = (f32[576]{0:T(1024)}, f32[576]{0:T(1024)S(1)}, u32[]{:S(2)}) copy-start(f32[576]{0:T(1024)S(1)} %div.144) | copy-start | bytes 6916
  62.9 7.7 %copy-start = (f32[102,384]{0,1:T(8,128)}, f32[102,384]{0,1:T(8,128)S(1)}, u32[]{:S(2)}) copy-start(f32[102,384]{0,1:T(8,128)S(1)} %all_gather.23) | copy-start | bytes 470020
  64.6 11.3 %copy-start.91 = (f32[384]{0:T(512)}, f32[384]{0:T(512)S(1)}, u32[]{:S(2)}) copy-start(f32[384]{0:T(512)S(1)} %get-tuple-element.84) | copy-start | bytes 4612
  64.6 11.3 %copy-start.107 = (f32[384]{0:T(512)}, f32[384]{0:T(512)S(1)}, u32[]{:S(2)}) copy-start(f32[384]{0:T(512)S(1)} %get-tuple-element.83) | copy-start | bytes 4612
  64.6 11.7 %copy-start.96 = (f32[384]{0:T(512)}, f32[384]{0:T(512)S(1)}, u32[]{:S(2)}) copy-start(f32[384]{0:T(512)S(1)} %get-tuple-element.75) | copy-start | bytes 4612
  70.5 5.7 copy-start.105
  70.6 5.6 copy-start.87
  70.7 5.6 copy-start.79
  76.3 97.2 %copy-start.29 = (bf16[576,384]{1,0:T(8,128)(2,1)}, bf16[576,384]{1,0:T(8,128)(2,1)S(1)}, u32[]{:S(2)}) copy-start(bf16[576,384]{1,0:T(8,128)(2,1)S(1)} %add_convert_fusion.2) | copy-start | bytes 1327108
  108.4 100.6 %copy-start.34 = (bf16[384,384]{1,0:T(8,128)(2,1)}, bf16[384,384]{1,0:T(8,128)(2,1)S(1)}, u32[]{:S(2)}) copy-start(bf16[384,384]{1,0:T(8,128)(2,1)S(1)} %all_gather.25) | copy-start | bytes 884740
  141.4 115.4 %all-gather.5.cloned.1.call-start = ((), (), s32[]{:S(2)}) async-start(), calls=%async_computation.7 | async-start | bytes 1327104 | tf_op jit(solution)/shard_map/all_gather | solution.py:175
  174.4 34.6 %copy-start.3 = (f32[576,768]{1,0:T(8,128)}, f32[576,768]{1,0:T(8,128)S(1)}, u32[]{:S(2)}) copy-start(f32[576,768]{1,0:T(8,128)S(1)} %fusion.191) | copy-start | bytes 5308420
  197.7 10.1 %copy-start.99 = (f32[384]{0:T(512)}, f32[384]{0:T(512)S(1)}, u32[]{:S(2)}) copy-start(f32[384]{0:T(512)S(1)} %get-tuple-element.103) | copy-start | bytes 4612
  197.7 10.7 %copy-start.4 = (f32[1,24,24,384]{3,2,1,0:T(8,128)}, f32[1,24,24,384]{3,2,1,0:T(8,128)S(1)}, u32[]{:S(2)}) copy-start(f32[1,24,24,384]{3,2,1,0:T(8,128)S(1)} %get-tuple-element.104) | copy-start | bytes 2654212
  211.9 53.0 %copy-start.7 = (f32[576,384]{1,0:T(8,128)}, f32[576,384]{1,0:T(8,128)S(1)}, u32[]{:S(2)}) copy-start(f32[576,384]{1,0:T(8,128)S(1)} %get-tuple-element.163) | copy-start | bytes 2654212
  215.0 184.8 %reduce-scatter.13.cloned.1.call-start = ((), (), s32[]{:S(2)}) async-start(), calls=%async_computation.10 | async-start | bytes 663552 | tf_op jit(solution)/shard_map/reduce_scatter | solution.py:301
  256.8 6.3 copy-start.102
  256.8 6.3 copy-start.131
  256.8 6.3 copy-start.136
  256.8 6.3 copy-start.142
  274.1 125.7 %reduce-scatter.11.cloned.1.call-start = ((), (), s32[]{:S(2)}) async-start(), calls=%async_computation.9 | async-start | bytes 663552 | tf_op jit(solution)/shard_map/reduce_scatter | solution.py:300
  276.7 7.6 %copy-start.9 = (f32[576,384]{1,0:T(8,128)}, f32[576,384]{1,0:T(8,128)S(1)}, u32[]{:S(2)}) copy-start(f32[576,384]{1,0:T(8,128)S(1)} %get-tuple-element.167) | copy-start | bytes 2654212
  297.6 168.7 %reduce-scatter.9.cloned.1.call-start = ((), (), s32[]{:S(2)}) async-start(), calls=%async_computation.8 | async-start | bytes 1327104 | tf_op jit(solution)/shard_map/reduce_scatter | solution.py:299
  311.5 226.1 %reduce-scatter.15.cloned.1.call-start = ((), (), s32[]{:S(2)}) async-start(), calls=%async_computation.11 | async-start | bytes 2654208 | tf_op jit(solution)/shard_map/reduce_scatter | solution.py:302
  316.8 292.5 %reduce-scatter.17.cloned.1.call-start = ((), (), s32[]{:S(2)}) async-start(), calls=%async_computation.12 | async-start | bytes 2654208 | tf_op jit(solution)/shard_map/reduce_scatter | solution.py:303
  323.1 19.4 %copy-start.112 = (f32[1536]{0:T(1024)S(1)}, f32[1536]{0:T(1024)}, u32[]{:S(2)}) copy-start(f32[1536]{0:T(1024)} %get-tuple-element.169) | copy-start | bytes 18436
  323.1 19.4 %copy-start.140 = (f32[384]{0:T(512)S(1)}, f32[384]{0:T(512)}, u32[]{:S(2)}) copy-start(f32[384]{0:T(512)} %get-tuple-element.60) | copy-start | bytes 4612
  323.1 20.0 %copy-start.141 = (f32[384]{0:T(512)S(1)}, f32[384]{0:T(512)}, u32[]{:S(2)}) copy-start(f32[384]{0:T(512)} %get-tuple-element.122) | copy-start | bytes 4612
  323.1 20.5 %copy-start.139 = (f32[384]{0:T(512)S(1)}, f32[384]{0:T(512)}, u32[]{:S(2)}) copy-start(f32[384]{0:T(512)} %get-tuple-element.64) | copy-start | bytes 4612
  323.1 21.1 %copy-start.110 = (f32[384]{0:T(512)S(1)}, f32[384]{0:T(512)}, u32[]{:S(2)}) copy-start(f32[384]{0:T(512)} %get-tuple-element.67) | copy-start | bytes 4612
  323.1 21.7 %copy-start.118 = (f32[384]{0:T(512)S(1)}, f32[384]{0:T(512)}, u32[]{:S(2)}) copy-start(f32[384]{0:T(512)} %get-tuple-element.65) | copy-start | bytes 4612
  323.2 22.2 %copy-start.117 = (f32[384]{0:T(512)S(1)}, f32[384]{0:T(512)}, u32[]{:S(2)}) copy-start(f32[384]{0:T(512)} %get-tuple-element.66) | copy-start | bytes 4612
  323.2 22.8 %copy-start.109 = (f32[384]{0:T(512)S(1)}, f32[384]{0:T(512)}, u32[]{:S(2)}) copy-start(f32[384]{0:T(512)} %get-tuple-element.68) | copy-start | bytes 4612
  323.2 24.0 %copy-start.36 = (f32[1,24,24,384]{3,2,1,0:T(8,128)S(1)}, f32[1,24,24,384]{3,2,1,0:T(8,128)}, u32[]{:S(2)}) copy-start(f32[1,24,24,384]{3,2,1,0:T(8,128)} %copy-done.35) | copy-start | bytes 2654212
  323.2 349.9 %reduce-scatter.19.cloned.1.call-start = ((), (), s32[]{:S(2)}) async-start(), calls=%async_computation.13 | async-start | bytes 221184
  347.1 35.2 %copy-start.134 = (f32[576]{0:T(1024)S(1)}, f32[576]{0:T(1024)}, u32[]{:S(2)}) copy-start(f32[576]{0:T(1024)} %get-tuple-element.71) | copy-start | bytes 6916
  347.1 35.3 %copy-start.16 = (f32[1,24,24,384]{3,2,1,0:T(8,128)S(1)}, f32[1,24,24,384]{3,2,1,0:T(8,128)}, u32[]{:S(2)}) copy-start(f32[1,24,24,384]{3,2,1,0:T(8,128)} %copy-done.15) | copy-start | bytes 2654212
  382.5 8.8 %copy-start.73 = (f32[24,24]{1,0:T(8,128)S(1)}, f32[24,24]{1,0:T(8,128)}, u32[]{:S(2)}) copy-start(f32[24,24]{1,0:T(8,128)} %get-tuple-element.72) | copy-start | bytes 6916
  382.5 8.8 %copy-start.74 = (f32[24,24]{1,0:T(8,128)S(1)}, f32[24,24]{1,0:T(8,128)}, u32[]{:S(2)}) copy-start(f32[24,24]{1,0:T(8,128)} %get-tuple-element.73) | copy-start | bytes 6916
  382.5 8.8 %copy-start.75 = (f32[24,24]{1,0:T(8,128)S(1)}, f32[24,24]{1,0:T(8,128)}, u32[]{:S(2)}) copy-start(f32[24,24]{1,0:T(8,128)} %get-tuple-element.74) | copy-start | bytes 6916
  382.5 9.5 %copy-start.111 = (f32[384]{0:T(512)S(1)}, f32[384]{0:T(512)}, u32[]{:S(2)}) copy-start(f32[384]{0:T(512)} %get-tuple-element.120) | copy-start | bytes 4612
  382.5 10.0 %copy-start.1 = (f32[102,384]{0,1:T(8,128)S(1)}, f32[102,384]{0,1:T(8,128)}, u32[]{:S(2)}) copy-start(f32[102,384]{0,1:T(8,128)} %copy-done) | copy-start | bytes 470020
  399.1 311.9 %all-reduce.14.cloned.1.call-start = ((), (), s32[]{:S(2)}) async-start(), calls=%async_computation.14 | async-start | bytes 1769472 | tf_op jit(solution)/shard_map/psum | solution.py:306
  609.3 75.0 %copy-start.65 = (f32[1,102,48]{1,2,0:T(8,128)S(1)}, f32[1,102,48]{1,2,0:T(8,128)}, u32[]{:S(2)}) copy-start(f32[1,102,48]{1,2,0:T(8,128)} %param.43) | copy-start | bytes 58756
  609.3 75.0 %copy-start.89 = (f32[1,102,48]{1,2,0:T(8,128)S(1)}, f32[1,102,48]{1,2,0:T(8,128)}, u32[]{:S(2)}) copy-start(f32[1,102,48]{1,2,0:T(8,128)} %param.45) | copy-start | bytes 58756
  609.3 75.0 %copy-start.90 = (f32[1,102,48]{1,2,0:T(8,128)S(1)}, f32[1,102,48]{1,2,0:T(8,128)}, u32[]{:S(2)}) copy-start(f32[1,102,48]{1,2,0:T(8,128)} %param.44) | copy-start | bytes 58756
  609.3 101.7 %copy-start.51 = (f32[1,48,384]{2,1,0:T(8,128)S(1)}, f32[1,48,384]{2,1,0:T(8,128)}, u32[]{:S(2)}) copy-start(f32[1,48,384]{2,1,0:T(8,128)} %param.31) | copy-start | bytes 221188
  609.4 101.7 %copy-start.68 = (f32[1,48,384]{2,1,0:T(8,128)S(1)}, f32[1,48,384]{2,1,0:T(8,128)}, u32[]{:S(2)}) copy-start(f32[1,48,384]{2,1,0:T(8,128)} %param.33) | copy-start | bytes 221188
  609.4 101.7 %copy-start.69 = (f32[1,48,384]{2,1,0:T(8,128)S(1)}, f32[1,48,384]{2,1,0:T(8,128)}, u32[]{:S(2)}) copy-start(f32[1,48,384]{2,1,0:T(8,128)} %param.32) | copy-start | bytes 221188
  609.4 103.4 %copy-start.52 = (f32[1,48,384]{2,1,0:T(8,128)S(1)}, f32[1,48,384]{2,1,0:T(8,128)}, u32[]{:S(2)}) copy-start(f32[1,48,384]{2,1,0:T(8,128)} %param.34) | copy-start | bytes 221188
  609.4 103.4 %copy-start.70 = (f32[1,48,384]{2,1,0:T(8,128)S(1)}, f32[1,48,384]{2,1,0:T(8,128)}, u32[]{:S(2)}) copy-start(f32[1,48,384]{2,1,0:T(8,128)} %param.36) | copy-start | bytes 221188
  609.4 103.3 %copy-start.71 = (f32[1,48,384]{2,1,0:T(8,128)S(1)}, f32[1,48,384]{2,1,0:T(8,128)}, u32[]{:S(2)}) copy-start(f32[1,48,384]{2,1,0:T(8,128)} %param.35) | copy-start | bytes 221188
  609.4 105.0 %copy-start.55 = (f32[1,48,768]{2,1,0:T(8,128)S(1)}, f32[1,48,768]{2,1,0:T(8,128)}, u32[]{:S(2)}) copy-start(f32[1,48,768]{2,1,0:T(8,128)} %param.29) | copy-start | bytes 442372
  610.5 103.9 %copy-start.39 = (f32[1,48,768]{2,1,0:T(8,128)S(1)}, f32[1,48,768]{2,1,0:T(8,128)}, u32[]{:S(2)}) copy-start(f32[1,48,768]{2,1,0:T(8,128)} %param.28) | copy-start | bytes 442372
  610.5 103.9 %copy-start.54 = (f32[1,48,768]{2,1,0:T(8,128)S(1)}, f32[1,48,768]{2,1,0:T(8,128)}, u32[]{:S(2)}) copy-start(f32[1,48,768]{2,1,0:T(8,128)} %param.30) | copy-start | bytes 442372
  610.5 105.7 %copy-start.32 = (f32[1,48,1536]{2,1,0:T(8,128)S(1)}, f32[1,48,1536]{2,1,0:T(8,128)}, u32[]{:S(2)}) copy-start(f32[1,48,1536]{2,1,0:T(8,128)} %param.37) | copy-start | bytes 884740
  610.5 105.7 %copy-start.45 = (f32[1,48,1536]{2,1,0:T(8,128)S(1)}, f32[1,48,1536]{2,1,0:T(8,128)}, u32[]{:S(2)}) copy-start(f32[1,48,1536]{2,1,0:T(8,128)} %param.39) | copy-start | bytes 884740
  610.5 105.7 %copy-start.46 = (f32[1,48,1536]{2,1,0:T(8,128)S(1)}, f32[1,48,1536]{2,1,0:T(8,128)}, u32[]{:S(2)}) copy-start(f32[1,48,1536]{2,1,0:T(8,128)} %param.38) | copy-start | bytes 884740
  (96 other events, 188.3 us)
Sparse Core Ops, SparseCore 0:
  11.8 32.2 all-reduce.15
  47.9 33.8 all-reduce.17
  141.5 41.9 all-gather.2
  215.1 41.6 all-gather.4
  274.2 60.8 reduce-scatter.12
  338.6 61.1 reduce-scatter.10
  403.2 62.9 reduce-scatter.8
  469.7 67.9 reduce-scatter.14
  541.2 68.0 reduce-scatter.16
  613.0 60.1 reduce-scatter.18
  675.8 35.1 all-reduce.13
where the time goes:
time: 732 us; the launch traced here: 726 us
  waiting for transfers between devices  328 us (45%)
  blocking collectives  151 us (21%)
  matrix products  132 us (18%)
  local copies, waits for them, and re-layouts  55 us (8%)
  other arithmetic  36.7 us (5%)
  between operations  21.1 us (3%)
    conv_general_dilated x9, matrix products, depthwise(): lax.conv_general_dilated(feature_map, kernel, (1, 1), 'SAME', dimension_n...  81 us
    reduce_scatter x1, waiting for transfers between devices, shards(): lax.psum_scatter(grad_shrink, 'fs', scatter_dimension=0, tiled=True)  71.6 us
    reduce_scatter x1, waiting for transfers between devices, shards(): lax.psum_scatter(grad_expand, 'fs', scatter_dimension=0, tiled=True)  71.5 us
    reduce_scatter x1, waiting for transfers between devices, shards(): lax.psum_scatter(grad_focal, 'fs', scatter_dimension=0, tiled=True)  66.4 us
    unnamed x12, waiting for transfers between devices  62.8 us
    all_gather x1, blocking collectives, shards(): lax.all_gather(shares[2], 'fs', axis=0, tiled=True)  33 us
    all_gather x1, blocking collectives, shards(): lax.all_gather(shares[0], 'fs', axis=0, tiled=True)  32.1 us
    all_gather x1, blocking collectives, shards(): lax.all_gather(shares[1], 'fs', axis=0, tiled=True)  31.1 us
  transfers between devices with their start and end apart: 11, of which 7 were waited for; matrix products, arithmetic and copies ran while one was open for 25% of the time, Pallas kernels for 0%

commit v1 on v0

v1 whole, which is shorter than its diff:
```python
import math

import jax
import jax.numpy as jnp
from jax import lax
from jax.experimental import pallas as pl
from jax.experimental.pallas import tpu as pltpu
from jax.sharding import PartitionSpec as P

f32 = jnp.float32
b16 = jnp.bfloat16
LEVELS = 3
GATES = 4
LANE = 128
norm_eps = 1e-05
PAD = 3
EDGE = 8
SQRT_HALF = math.sqrt(0.5)
INV_SQRT_2PI = 1.0 / math.sqrt(2.0 * math.pi)
BLK = 48


def gelu_parts(z):
    az = jnp.abs(z)
    t = 1.0 / (1.0 + (0.3275911 * SQRT_HALF) * az)
    e = jnp.exp(z * z * -0.5)
    poly = t * (
        0.5 * 0.254829592
        + t * (0.5 * -0.284496736 + t * (0.5 * 1.421413741 + t * (0.5 * -1.453152027 + t * (0.5 * 1.061405429))))
    )
    tail = poly * e
    phi = jnp.where(z >= 0.0, 1.0 - tail, tail)
    return z * phi, phi + z * e * INV_SQRT_2PI


def mm(a, b):
    return jnp.dot(a, b, preferred_element_type=f32)


def mm_t(a, b):
    return lax.dot_general(a, b, (((1,), (1,)), ((), ())), preferred_element_type=f32)


def mm_g(a, b):
    return lax.dot_general(a, b, (((0,), (0,)), ((), ())), preferred_element_type=f32)


def tall(values):
    rows, cols = values.shape
    return jnp.sum(values.reshape(rows // 8, 8, cols), axis=0)


def lane_sum(values):
    parts = values[:, :LANE]
    for start in range(LANE, values.shape[1], LANE):
        parts = parts + values[:, start : start + LANE]
    return jnp.sum(parts, axis=1, keepdims=True)


class Shape:
    def __init__(self, side, channels, hid):
        self.side = side
        self.rows = side * side
        self.c = channels
        self.nc = channels // LANE
        self.hid = hid
        self.bias_rows = hid // channels
        self.gate_at = 11 + self.bias_rows
        self.kernel_at = self.gate_at + GATES
        self.taps = [(2 * n + 3) ** 2 for n in range(LEVELS)]
        self.nvec = self.kernel_at + sum(self.taps)
        self.padded = (self.nc, side + 2 * PAD, side + 2 * EDGE, LANE)


def compute_scratch(s):
    flat = (s.rows, s.c)
    split = (s.nc, s.rows, LANE)
    grid = (s.nc, s.side, s.side, LANE)
    return dict(
        vc=pltpu.VMEM((s.nc, s.nvec, LANE), f32),
        mask=pltpu.VMEM((s.rows, LANE), f32),
        xh1=pltpu.VMEM(flat, f32),
        r1=pltpu.VMEM((s.rows, LANE), f32),
        n1b=pltpu.VMEM(flat, b16),
        gate=pltpu.VMEM((GATES, s.rows, LANE), f32),
        q=pltpu.VMEM(flat, f32),
        pads=[pltpu.VMEM(s.padded, f32) for _ in range(LEVELS + 1)],
        gd=[pltpu.VMEM(grid, f32) for _ in range(LEVELS)],
        summed=pltpu.VMEM(grid, f32),
        sumb=pltpu.VMEM(flat, b16),
        mod=pltpu.VMEM(flat, f32),
        mixb=pltpu.VMEM(flat, b16),
        proj=pltpu.VMEM(flat, f32),
        mid=pltpu.VMEM(flat, f32),
        xh2=pltpu.VMEM(flat, f32),
        r2=pltpu.VMEM((s.rows, LANE), f32),
        n2b=pltpu.VMEM(flat, b16),
        dshrb=pltpu.VMEM(flat, b16),
        actb=pltpu.VMEM((s.rows, s.hid), b16),
        dhidb=pltpu.VMEM((s.rows, s.hid), b16),
        shr=pltpu.VMEM(flat, f32),
        dn=pltpu.VMEM(flat, f32),
        dqb=pltpu.VMEM(flat, b16),
        dsum=pltpu.VMEM(split, f32),
        dgate=pltpu.VMEM((GATES, s.rows, LANE), f32),
        dctxb=pltpu.VMEM(flat, b16),
        gacc=pltpu.VMEM((s.nc, sum(s.taps), 8, LANE), f32),
        pool=pltpu.VMEM((2, 8, s.c), f32),
    )


class Compute:
    def __init__(self, s, refs, scratch):
        self.s = s
        self.__dict__.update(refs)
        self.__dict__.update(scratch)
        self.dmid, self.dprojb, self.dmodb = self.mid, self.dshrb, self.n2b

    def row(self, index):
        return self.v[index : index + 1, :]

    def wide_mask(self, at):
        m = self.mask[at, :]
        return jnp.concatenate([m] * self.s.nc, axis=1)

    def wide(self, ref, at):
        m = ref[at, :]
        return jnp.concatenate([m] * self.s.nc, axis=1)

    def blocks(self, body, sums=0):
        s = self.s
        start = tuple(jnp.zeros((8, s.c), f32) for _ in range(sums))

        def step(index, carry):
            at = pl.ds(pl.multiple_of(index * BLK, BLK), BLK)
            parts = body(at, pl.ds(index * (BLK // s.side), BLK // s.side))
            if not sums:
                return carry
            return tuple(total + tall(part) for total, part in zip(carry, parts))

        return lax.fori_loop(0, s.rows // BLK, step, start)

    def image(self, ref, lines):
        return ref[0, lines].astype(f32).reshape(BLK, self.s.c)

    def store(self, ref, lines, values):
        ref[0, lines] = values.reshape(BLK // self.s.side, self.s.side, self.s.c).astype(ref.dtype)

    def put(self, index, total):
        self.gv[index : index + 1, :] = jnp.sum(total, axis=0, keepdims=True)

    def prepare(self):
        s = self.s
        shape = (s.side, s.side, LANE)
        side = jnp.where(self.count > 0, self.sides, 0)
        inside = (lax.broadcasted_iota(jnp.int32, shape, 0) < side) & (
            lax.broadcasted_iota(jnp.int32, shape, 1) < side
        )
        self.mask[...] = jnp.where(inside, 1.0, 0.0).astype(f32).reshape(s.rows, LANE)

        def zero_plane(index, carry):
            for pad in self.pads:
                for ch in range(s.nc):
                    pad[ch, index, 0:EDGE, :] = jnp.zeros((EDGE, LANE), f32)
                    pad[ch, index, EDGE + s.side :, :] = jnp.zeros((EDGE, LANE), f32)
            return carry

        lax.fori_loop(0, s.side + 2 * PAD, zero_plane, 0)
        for pad in self.pads:
            for ch in range(s.nc):
                for edge in list(range(PAD)) + list(range(PAD + s.side, s.side + 2 * PAD)):
                    pad[ch, edge, EDGE : EDGE + s.side, :] = jnp.zeros((s.side, LANE), f32)

        def norm(at, lines):
            x = self.image(self.x, lines)
            centred = x - lane_sum(x) * (1.0 / s.c)
            r = lax.rsqrt(lane_sum(centred * centred) * (1.0 / s.c) + norm_eps)
            self.xh1[at, :] = centred * r
            self.r1[at, :] = jnp.broadcast_to(r, (BLK, LANE))

        self.blocks(norm)

        def clear(index, carry):
            for ch in range(s.nc):
                self.gacc[ch, index] = jnp.zeros((8, LANE), f32)
            return carry

        lax.fori_loop(0, sum(s.taps), clear, 0)

    def first(self):
        s = self.s
        for ch in range(s.nc):
            self.vc[ch] = self.v[: s.nvec, ch * LANE : (ch + 1) * LANE]
        gain, shift = self.row(0), self.row(1)
        weights = [self.row(s.gate_at + l) for l in range(GATES)]

        def step(at, lines):
            n1 = self.xh1[at, :] * gain + shift
            self.n1b[at, :] = n1.astype(b16)
            for l in range(GATES):
                self.gate[l, at, :] = jnp.broadcast_to(lane_sum(n1 * weights[l]), (BLK, LANE))

        self.blocks(step)
        n1b = self.n1b[...]
        self.q[...] = mm(n1b, self.wf(0)) + self.row(2)
        ctx = mm(n1b, self.wf(1)) + self.row(3)
        m = self.mask[...]
        for ch in range(s.nc):
            part = ctx[:, ch * LANE : (ch + 1) * LANE] * m
            self.pads[0][ch, PAD : PAD + s.side, EDGE : EDGE + s.side, :] = part.reshape(
                s.side, s.side, LANE
            )

    def level(self, l, block=4):
        s = self.s
        k = 2 * l + 3
        p = l + 1
        offset = s.kernel_at + sum(s.taps[:l])
        source = self.pads[l]
        per = s.side // block

        def step(index, carry):
            ch = lax.div(index, per)
            r0 = lax.rem(index, per) * block
            acc = [None] * block
            for dc in range(-p, p + 1):
                taps = [
                    self.vc[ch, pl.ds(offset + (dr + p) * k + dc + p, 1), :]
                    for dr in range(-p, p + 1)
                ]
                for a in range(-p, block + p):
                    x = source[ch, r0 + PAD + a, pl.ds(EDGE + dc, s.side), :]
                    for o in range(max(0, a - p), min(block, a + p + 1)):
                        term = x * taps[a - o + p]
                        acc[o] = term if acc[o] is None else acc[o] + term
            for o in range(block):
                at = pl.ds(pl.multiple_of((r0 + o) * s.side, s.side), s.side)
                m = self.mask[at, :]
                value, slope = gelu_parts(acc[o])
                value = value * m
                self.gd[l][ch, r0 + o] = slope * m
                self.pads[l + 1][ch, r0 + o + PAD, EDGE : EDGE + s.side, :] = value
                term = value * self.gate[l, at, :]
                if l:
                    term = term + self.summed[ch, r0 + o]
                self.summed[ch, r0 + o] = term
            return carry

        lax.fori_loop(0, s.nc * per, step, 0)

    def pooling(self):
        s = self.s
        area = (self.sides * self.sides).astype(f32)
        for ch in range(s.nc):
            last = self.pads[LEVELS][ch, PAD : PAD + s.side, EDGE : EDGE + s.side, :]
            total = jnp.sum(tall(last.reshape(s.rows, LANE)), axis=0, keepdims=True)
            value, slope = gelu_parts(total / area)
            cols = slice(ch * LANE, (ch + 1) * LANE)
            self.pool[0, :, cols] = jnp.broadcast_to(value, (8, LANE))
            self.pool[1, :, cols] = jnp.broadcast_to(slope / area, (8, LANE))

        def step(index, carry):
            at = pl.ds(pl.multiple_of(index * s.side * 2, s.side * 2), s.side * 2)
            gate = self.gate[LEVELS, at, :]
            for ch in range(s.nc):
                cols = slice(ch * LANE, (ch + 1) * LANE)
                part = self.summed[ch, pl.ds(index * 2, 2)].reshape(2 * s.side, LANE)
                self.sumb[at, cols] = (part + gate * self.pool[0, 0:1, cols]).astype(b16)
            return carry

        lax.fori_loop(0, s.side // 2, step, 0)

    def modulate(self):
        s = self.s
        self.mod[...] = mm(self.sumb[...], self.wh()) + self.row(4)

        def mix(at, lines):
            self.mixb[at, :] = (self.q[at, :] * self.mod[at, :]).astype(b16)

        self.blocks(mix)
        self.proj[...] = mm(self.mixb[...], self.wp()) + self.row(5)
        scale, gain, shift = self.row(6), self.row(7), self.row(8)
        upscale = self.row(10)

        def norm(at, lines):
            mid = self.image(self.x, lines) + scale * self.proj[at, :]
            self.mid[at, :] = mid
            centred = mid - lane_sum(mid) * (1.0 / s.c)
            r = lax.rsqrt(lane_sum(centred * centred) * (1.0 / s.c) + norm_eps)
            xh = centred * r
            self.xh2[at, :] = xh
            self.r2[at, :] = jnp.broadcast_to(r, (BLK, LANE))
            self.n2b[at, :] = (xh * gain + shift).astype(b16)
            d_shr = self.image(self.cot, lines) * self.wide_mask(at) * upscale
            self.dshrb[at, :] = d_shr.astype(b16)
            return (d_shr,)

        (g_b2,) = self.blocks(norm, 1)
        self.put(9, g_b2)

    def feed(self, wide=256):
        s = self.s
        half = s.hid // 2
        per = half // wide
        for j in range(s.hid // wide):
            h, at = j // per, (j % per) * wide
            cols = slice(j * wide, (j + 1) * wide)
            first_row, first_col = divmod(j * wide, s.c)
            bias = []
            for start in range(j * wide, (j + 1) * wide, LANE):
                r, c = divmod(start, s.c)
                bias.append(self.v[11 + r : 12 + r, c : c + LANE])
            bias = jnp.concatenate(bias, axis=1)
            w1 = self.w1(h, at, wide)
            hid = mm(self.n2b[...], w1) + bias
            act, slope = gelu_parts(hid)
            self.actb[:, cols] = act.astype(b16)
            d_hid = mm_t(self.dshrb[...], self.w2(j * wide, wide)) * slope
            self.dhidb[:, cols] = d_hid.astype(b16)
            g_bias = jnp.sum(tall(d_hid), axis=0, keepdims=True)
            for i, start in enumerate(range(j * wide, (j + 1) * wide, LANE)):
                r, c = divmod(start, s.c)
                self.gv[11 + r : 12 + r, c : c + LANE] = g_bias[:, i * LANE : (i + 1) * LANE]

    def feed_grads(self, wide=256):
        s = self.s
        half = s.hid // 2
        for j in range(s.hid // wide):
            cols = slice(j * wide, (j + 1) * wide)
            h, at = divmod(j * wide, half)
            self.put_g2(j * wide, wide, mm_g(self.actb[:, cols], self.dshrb[...]))
            self.put_g1(h, at, wide, mm_g(self.n2b[...], self.dhidb[:, cols]))

    def feed_out(self):
        s = self.s
        half = s.hid // 2
        self.shr[...] = mm(self.actb[...], self.w2(0, s.hid)) + self.row(9)
        self.dn[...] = mm_t(self.dhidb[:, :half], self.w1(0, 0, half)) + mm_t(
            self.dhidb[:, half:], self.w1(1, 0, half)
        )

    def middle(self):
        s = self.s
        gain, scale, upscale = self.row(7), self.row(6), self.row(10)

        def step(at, lines):
            shr, mid, proj, xh = self.shr[at, :], self.mid[at, :], self.proj[at, :], self.xh2[at, :]
            m = self.wide_mask(at)
            u = self.image(self.cot, lines) * m
            self.store(self.out, lines, (mid + upscale * shr) * m)
            d = self.dn[at, :]
            e = d * gain
            mean_e = lane_sum(e) * (1.0 / s.c)
            mean_x = lane_sum(e * xh) * (1.0 / s.c)
            d_mid = u + self.wide(self.r2, at) * (e - mean_e - xh * mean_x)
            self.dmid[at, :] = d_mid
            d_proj = scale * d_mid
            self.dprojb[at, :] = d_proj.astype(b16)
            return u * shr, d * xh, d, d_mid * proj, d_proj

        sums = self.blocks(step, 5)
        for index, total in zip((10, 7, 8, 6, 5), sums):
            self.put(index, total)
        self.dn[...] = mm_t(self.dprojb[...], self.wp())

        def split(at, lines):
            d = self.dn[at, :]
            d_q = d * self.mod[at, :]
            d_mod = d * self.q[at, :]
            self.dqb[at, :] = d_q.astype(b16)
            self.dmodb[at, :] = d_mod.astype(b16)
            return d_q, d_mod

        g_bq, g_bh = self.blocks(split, 2)
        self.put(2, g_bq)
        self.put(4, g_bh)
        d_sum = mm_t(self.dmodb[...], self.wh())
        for ch in range(s.nc):
            self.dsum[ch] = d_sum[:, ch * LANE : (ch + 1) * LANE]

    def middle_grads(self):
        self.put_gp(mm_g(self.mixb[...], self.dprojb[...]))
        self.put_gh(mm_g(self.sumb[...], self.dmodb[...]))

    def focal_top(self):
        s = self.s

        def step(index, carry):
            at = pl.ds(pl.multiple_of(index * s.side * 2, s.side * 2), s.side * 2)
            gate = self.gate[LEVELS, at, :]
            sums = [jnp.zeros((2 * s.side, LANE), f32) for _ in range(GATES)]
            out = []
            for ch in range(s.nc):
                cols = slice(ch * LANE, (ch + 1) * LANE)
                d = self.dsum[ch, at, :]
                values = [
                    self.pads[l][ch, pl.ds(index * 2 + PAD, 2), EDGE : EDGE + s.side, :]
                    for l in range(1, LEVELS + 1)
                ]
                for l in range(LEVELS):
                    sums[l] = sums[l] + d * values[l].reshape(2 * s.side, LANE)
                sums[LEVELS] = sums[LEVELS] + d * self.pool[0, 0:1, cols]
                out.append(carry[ch] + tall(d * gate))
            for l in range(GATES):
                self.dgate[l, at, :] = jnp.broadcast_to(
                    jnp.sum(sums[l], axis=1, keepdims=True), (2 * s.side, LANE)
                )
            return tuple(out)

        zero = jnp.zeros((8, LANE), f32)
        totals = lax.fori_loop(0, s.side // 2, step, (zero,) * s.nc)
        for ch in range(s.nc):
            cols = slice(ch * LANE, (ch + 1) * LANE)
            total = jnp.sum(totals[ch], axis=0, keepdims=True)
            self.pool[1, :, cols] = self.pool[1, :, cols] * total

        def last(index, carry):
            at = pl.ds(pl.multiple_of(index * s.side * 2, s.side * 2), s.side * 2)
            gate = self.gate[LEVELS - 1, at, :]
            for ch in range(s.nc):
                cols = slice(ch * LANE, (ch + 1) * LANE)
                e = self.dsum[ch, at, :] * gate + self.pool[1, 0:1, cols]
                d = e.reshape(2, s.side, LANE) * self.gd[LEVELS - 1][ch, pl.ds(index * 2, 2)]
                self.pads[LEVELS][ch, pl.ds(index * 2 + PAD, 2), EDGE : EDGE + s.side, :] = d
            return carry

        lax.fori_loop(0, s.side // 2, last, 0)

    def level_back(self, l, block=4):
        s = self.s
        k = 2 * l + 3
        p = l + 1
        base = sum(s.taps[:l])
        offset = s.kernel_at + base
        source = self.pads[l + 1]
        inputs = self.pads[l]
        per = s.side // block

        def step(index, carry):
            ch = lax.div(index, per)
            r0 = lax.rem(index, per) * block
            acc = [None] * block
            xs = [
                inputs[ch, r0 + PAD + o, EDGE : EDGE + s.side, :] for o in range(block)
            ]
            for dc in range(-p, p + 1):
                taps = [
                    self.vc[ch, pl.ds(offset + (dr + p) * k + dc + p, 1), :]
                    for dr in range(-p, p + 1)
                ]
                sums = [None] * k
                for a in range(-p, block + p):
                    d = source[ch, r0 + PAD + a, pl.ds(EDGE - dc, s.side), :]
                    for o in range(max(0, a - p), min(block, a + p + 1)):
                        dr = o - a
                        term = d * taps[dr + p]
                        acc[o] = term if acc[o] is None else acc[o] + term
                        part = tall(d * xs[o])
                        sums[dr + p] = part if sums[dr + p] is None else sums[dr + p] + part
                for dr in range(-p, p + 1):
                    tap = base + (dr + p) * k + dc + p
                    self.gacc[ch, tap] = self.gacc[ch, tap] + sums[dr + p]
            total = None
            for o in range(block):
                at = pl.ds(pl.multiple_of((r0 + o) * s.side, s.side), s.side)
                if l:
                    e = acc[o] + self.dsum[ch, at, :] * self.gate[l - 1, at, :]
                    self.pads[l][ch, r0 + o + PAD, EDGE : EDGE + s.side, :] = (
                        e * self.gd[l - 1][ch, r0 + o]
                    )
                else:
                    self.summed[ch, r0 + o] = acc[o] * self.mask[at, :]
            return carry

        lax.fori_loop(0, s.nc * per, step, 0)

    def focal_end(self):
        s = self.s

        def step(index, carry):
            at = pl.ds(pl.multiple_of(index * s.side * 2, s.side * 2), s.side * 2)
            out = []
            for ch in range(s.nc):
                cols = slice(ch * LANE, (ch + 1) * LANE)
                d = self.summed[ch, pl.ds(index * 2, 2)].reshape(2 * s.side, LANE)
                self.dctxb[at, cols] = d.astype(b16)
                out.append(carry[ch] + tall(d))
            return tuple(out)

        zero = jnp.zeros((8, LANE), f32)
        totals = lax.fori_loop(0, s.side // 2, step, (zero,) * s.nc)
        for ch in range(s.nc):
            cols = slice(ch * LANE, (ch + 1) * LANE)
            self.gv[3:4, cols] = jnp.sum(totals[ch], axis=0, keepdims=True)
            self.gv[s.kernel_at : s.nvec, cols] = jnp.sum(self.gacc[ch], axis=1)

    def last_grads(self):
        n1b = self.n1b[...]
        self.put_gf(0, mm_g(n1b, self.dqb[...]))
        self.put_gf(1, mm_g(n1b, self.dctxb[...]))

    def last_back(self):
        s = self.s
        self.dn[...] = mm_t(self.dqb[...], self.wf(0)) + mm_t(self.dctxb[...], self.wf(1))
        gain, shift = self.row(0), self.row(1)
        weights = [self.row(s.gate_at + l) for l in range(GATES)]

        def step(at, lines):
            xh = self.xh1[at, :]
            n1 = xh * gain + shift
            d = self.dn[at, :]
            sums = []
            for l in range(GATES):
                dg = self.wide(self.dgate.at[l], at)
                d = d + dg * weights[l]
                sums.append(dg * n1)
            e = d * gain
            mean_e = lane_sum(e) * (1.0 / s.c)
            mean_x = lane_sum(e * xh) * (1.0 / s.c)
            d_in = self.dmid[at, :] + self.wide(self.r1, at) * (e - mean_e - xh * mean_x)
            self.store(self.grad, lines, d_in)
            return (d * xh, d) + tuple(sums)

        sums = self.blocks(step, 2 + GATES)
        for index, total in zip((0, 1) + tuple(s.gate_at + l for l in range(GATES)), sums):
            self.put(index, total)

    def run(self):
        self.prepare()
        self.first()
        for l in range(LEVELS):
            self.level(l)
        self.pooling()
        self.modulate()
        self.feed()
        self.feed_grads()
        self.feed_out()
        self.middle()
        self.middle_grads()
        self.focal_top()
        for l in reversed(range(LEVELS)):
            self.level_back(l)
        self.focal_end()
        self.last_grads()
        self.last_back()


MESH = pl.DeviceIdType.MESH
STEP = 10
TENSORS = 6
beta_one = 0.9
beta_two = 0.95
adam_eps = 1e-08
weight_decay = 0.05
VMEM_BYTES = 63 * 2**20 + 2**19


class Plan:
    def __init__(self, n_grp, n_fs, s):
        self.X = n_grp // 2
        self.Y = 2 ** (int(math.log2(n_fs)) // 2)
        self.Z = n_fs // self.Y
        self.fs = n_fs
        self.s = s
        self.rows = s.c // n_fs
        self.rp = -(-self.rows // 16) * 16
        self.rows2 = s.hid // n_fs // 2
        self.rp2 = -(-self.rows2 // 16) * 16
        self.rv = self.rp // 2
        half = s.c
        self.pieces = {
            "f": (self.rp, half, b16),
            "v": (self.rv, LANE, f32),
            "m": (self.rp, half, b16),
            "e": (self.rp, s.hid // 2, b16),
            "s": (self.rp2, s.c, b16),
        }

    def whole(self, name):
        rows, cols, kind = self.pieces[name]
        if name in "sv":
            return (self.Z, self.Y, 2, rows, cols)
        return (2, self.Z, self.Y, rows, cols)


def comm_scratch(p):
    out = {}
    for name, (rows, cols, kind) in p.pieces.items():
        out[name] = dict(
            cand=pltpu.VMEM((2, rows, cols), kind),
            rx1=pltpu.VMEM((rows, cols), kind),
            sel=pltpu.VMEM((rows, cols), kind),
            rx2=pltpu.VMEM((p.X - 1, rows, cols), kind),
            full=pltpu.VMEM(p.whole(name), kind),
            grad=pltpu.VMEM(p.whole(name), kind),
            r1=pltpu.VMEM((p.Z, p.Y, rows, cols), kind),
            r2=pltpu.VMEM((p.Y - 1, p.Z, rows, cols), kind),
            a2=pltpu.VMEM((p.Z, rows, cols), kind),
            r3=pltpu.VMEM((p.Z - 1, rows, cols), kind),
            a3=pltpu.VMEM((rows, cols), kind),
            r4=pltpu.VMEM((p.X - 1, rows, cols), kind),
            a4=pltpu.VMEM((rows, cols), f32),
            r5=pltpu.VMEM((rows, cols), f32),
        )
    return out


def sem_count(p):
    per = 1 + (p.X - 1) + (p.Z - 1) + p.Z * (p.Y - 1) + p.fs
    per += 1 + (p.Y - 1) + (p.Z - 1) + (p.X - 1) + 1
    return per * len(p.pieces)


class Links:
    def __init__(self, p, send_sem, recv_sem):
        self.p = p
        self.send_sem, self.recv_sem = send_sem, recv_sem
        self.used = 0
        self.sent = []
        self.g, self.f = lax.axis_index("grp"), lax.axis_index("fs")
        self.x, self.c = lax.div(self.g, 2), lax.rem(self.g, 2)
        self.z, self.y = lax.div(self.f, p.Y), lax.rem(self.f, p.Y)

    def sibling(self):
        return (self.x * 2 + 1 - self.c, self.f)

    def by_x(self, d):
        return (lax.rem(self.x + d, self.p.X) * 2 + self.c, self.f)

    def by_z(self, d):
        return (self.g, lax.rem(self.z + d, self.p.Z) * self.p.Y + self.y)

    def by_y(self, d):
        return (self.g, self.z * self.p.Y + lax.rem(self.y + d, self.p.Y))

    def partners(self):
        p = self.p
        return (
            [self.sibling()]
            + [self.by_x(d) for d in range(1, p.X)]
            + [self.by_z(d) for d in range(1, p.Z)]
            + [self.by_y(d) for d in range(1, p.Y)]
        )

    def barrier(self):
        sem = pltpu.get_barrier_semaphore()
        partners = self.partners()
        for partner in partners:
            pl.semaphore_signal(sem, inc=1, device_id=partner, device_id_type=MESH)
        pl.semaphore_wait(sem, len(partners))

    def send(self, source, target, partner, arriving=None):
        index = self.used
        self.used += 1

        def copy(src, dst):
            return pltpu.make_async_remote_copy(
                src_ref=src,
                dst_ref=dst,
                send_sem=self.send_sem.at[index],
                recv_sem=self.recv_sem.at[index],
                device_id=partner,
                device_id_type=MESH,
            )

        started = copy(source, target)
        started.start()
        self.sent.append(started)
        coming = copy(source, target if arriving is None else arriving)
        return coming.wait_recv

    def finish(self):
        for copy in self.sent:
            copy.wait_send()


class Gather:
    def __init__(self, name, links, refs):
        self.name, self.links, self.p = name, links, links.p
        self.__dict__.update(refs)

    def piece(self, half, z, y):
        return self.full.at[z, y, half] if self.name in "sv" else self.full.at[half, z, y]

    def core_send(self, z, y):
        k = self.links
        here = self.piece(k.c, z, y)
        return k.send(here, here, k.sibling(), self.piece(1 - k.c, z, y))

    def one(self):
        k = self.links
        self.wait1 = k.send(self.cand.at[1 - k.c], self.rx1, k.sibling())

    def two(self):
        k, p = self.links, self.p
        self.wait1()
        self.sel[...] = self.cand[k.c] + self.rx1[...]
        self.wait2 = [
            k.send(self.sel, self.rx2.at[d - 1], k.by_x(d)) for d in range(1, p.X)
        ]

    def y_sends(self, z):
        k, p = self.links, self.p
        here = self.piece(k.c, z, k.y)
        for d in range(1, p.Y):
            other = lax.rem(k.y + p.Y - d, p.Y)
            wait = k.send(here, here, k.by_y(d), self.piece(k.c, z, other))
            self.wait4.append((wait, z, other))

    def three(self):
        k, p = self.links, self.p
        for wait in self.wait2:
            wait()
        total = self.sel[...]
        for d in range(p.X - 1):
            total = total + self.rx2[d]
        self.piece(k.c, k.z, k.y)[...] = total
        here = self.piece(k.c, k.z, k.y)
        self.wait3, self.wait4, self.wait5 = [], [], []
        for d in range(1, p.Z):
            other = lax.rem(k.z + p.Z - d, p.Z)
            wait = k.send(here, here, k.by_z(d), self.piece(k.c, other, k.y))
            self.wait3.append((wait, other))
        self.y_sends(k.z)
        self.wait5.append(self.core_send(k.z, k.y))

    def four(self):
        k = self.links
        for wait, z in self.wait3:
            wait()
            self.y_sends(z)
            self.wait5.append(self.core_send(z, k.y))

    def five(self):
        for wait, z, y in self.wait4:
            wait()
            self.wait5.append(self.core_send(z, y))

    def six(self):
        for wait in self.wait5:
            wait()


class Reduce:
    def __init__(self, name, links, refs, result):
        self.name, self.links, self.p = name, links, links.p
        self.__dict__.update(refs)
        self.result = result

    def half(self, h):
        return self.grad.at[:, :, h] if self.name in "sv" else self.grad.at[h]

    def one(self):
        k = self.links
        self.wait1 = k.send(self.half(1 - k.c), self.r1, k.sibling())

    def two(self):
        k, p = self.links, self.p
        self.wait1()
        mine = self.half(k.c)

        def add(index, carry):
            z, y = lax.div(index, p.Y), lax.rem(index, p.Y)
            self.r1[z, y] = self.r1[z, y] + mine[z, y]
            return carry

        lax.fori_loop(0, p.fs, add, 0)
        self.wait2 = [
            k.send(self.r1.at[:, lax.rem(k.y + d, p.Y)], self.r2.at[d - 1], k.by_y(d))
            for d in range(1, p.Y)
        ]

    def three(self):
        k, p = self.links, self.p
        for wait in self.wait2:
            wait()

        def add(z, carry):
            total = self.r1[z, k.y].astype(f32)
            for d in range(p.Y - 1):
                total = total + self.r2[d, z].astype(f32)
            self.a2[z] = total.astype(self.a2.dtype)
            return carry

        lax.fori_loop(0, p.Z, add, 0)
        self.wait3 = [
            k.send(self.a2.at[lax.rem(k.z + d, p.Z)], self.r3.at[d - 1], k.by_z(d))
            for d in range(1, p.Z)
        ]

    def four(self):
        k, p = self.links, self.p
        for wait in self.wait3:
            wait()
        total = self.a2[k.z].astype(f32)
        for d in range(p.Z - 1):
            total = total + self.r3[d].astype(f32)
        self.a3[...] = total.astype(self.a3.dtype)
        self.wait4 = [
            k.send(self.a3, self.r4.at[d - 1], k.by_x(d)) for d in range(1, p.X)
        ]

    def five(self):
        k, p = self.links, self.p
        for wait in self.wait4:
            wait()
        total = self.a3[...].astype(f32)
        for d in range(p.X - 1):
            total = total + self.r4[d].astype(f32)
        self.a4[...] = total
        self.result[k.c] = total
        self.wait5 = k.send(self.a4, self.r5, k.sibling())

    def six(self):
        k = self.links
        self.wait5()
        self.result[1 - k.c] = self.r5[...]


def spread_matrix(rows, rp, count):
    bits = int(math.log2(rp))
    shape = (count * rows, count * rp)
    a = lax.broadcasted_iota(jnp.int32, shape, 0)
    b = lax.broadcasted_iota(jnp.int32, shape, 1)
    i = lax.bitwise_and(b, rp - 1)
    hit = (a == lax.shift_right_logical(b, bits) * rows + i) & (i < rows)
    return jnp.where(hit, 1.0, 0.0).astype(b16)


def block_kernel(p, tree, *refs):
    s = p.s
    (count, sides, owners, x, cot, wf, wh, wp, w1, w2, v_own) = refs[:11]
    (out, grad, fin_f, fin_v, fin_m, fin_e, fin_s) = refs[11:18]
    own = jax.tree.unflatten(tree, refs[18:])
    comm = own["comm"]
    k = Links(p, own["send_sem"], own["recv_sem"])
    even = p.rp == p.rows and p.rp2 == p.rows2

    def mine(index):
        return jnp.where(owners[index] == k.g, 1.0, 0.0).astype(f32)

    def cut(values, rows, rp):
        if rows == rp:
            return values
        return jnp.concatenate([values, jnp.zeros((rp - rows, values.shape[1]), f32)], axis=0)

    half, wide = s.c, s.hid // 2
    for name, parts in (
        ("f", ((0, wf, 0, 0), (0, wf, 0, half))),
        ("m", ((1, wh, 0, 0), (2, wp, 0, 0))),
        ("e", ((3, w1, 0, 0), (3, w1, 0, wide))),
        ("s", ((4, w2, 0, 0), (4, w2, p.rows2, 0))),
    ):
        rp, cols, kind = p.pieces[name]
        rows = p.rows2 if name == "s" else p.rows
        for h, (index, ref, row, col) in enumerate(parts):
            values = ref[0, row : row + rows, col : col + cols] * mine(index)
            comm[name]["cand"][h] = cut(values, rows, rp).astype(kind)
    values = cut(v_own[0] * mine(5), p.rows, p.rp)
    values = jnp.concatenate([values, jnp.zeros((p.rp, LANE - s.nvec), f32)], axis=1)
    for h in range(2):
        comm["v"]["cand"][h] = values[h * p.rv : (h + 1) * p.rv]

    k.barrier()
    order = ("f", "v", "m", "e", "s")
    gathers = [Gather(name, k, comm[name]) for name in order]
    for stage in ("one", "two", "three", "four", "five", "six"):
        for gather in gathers:
            getattr(gather, stage)()

    full = {name: comm[name]["full"] for name in order}
    if not even:
        own["map"][...] = spread_matrix(p.rows, p.rp, p.fs)

    vector = full["v"][...].reshape(p.fs * p.rp, LANE)
    if not even:
        vector = jnp.dot(own["map"][...].astype(f32), vector, precision=lax.Precision.HIGHEST)
    own["v"][...] = vector.T

    def compact(values):
        return values if even else mm(own["map"][...], values).astype(b16)

    def spread(values):
        values = values.astype(b16)
        return values if even else mm_g(own["map"][...], values).astype(b16)

    def matrix(name, h, at, cols):
        part = full[name][h, :, :, :, at : at + cols]
        return compact(part.reshape(p.fs * p.rp, cols))

    if even:
        shrink = full["s"]

        def take_shrink(at, rows):
            return shrink[...].reshape(s.hid, s.c)[at : at + rows]
    else:
        def close(f, carry):
            z, y = lax.div(f, p.Y), lax.rem(f, p.Y)
            parts = [full["s"][z, y, h].astype(f32)[: p.rows2] for h in range(2)]
            at = pl.ds(pl.multiple_of(f * 2 * p.rows2, 2 * p.rows2), 2 * p.rows2)
            own["w2n"][at, :] = jnp.concatenate(parts, axis=0).astype(b16)
            return carry

        lax.fori_loop(0, p.fs, close, 0)

        def take_shrink(at, rows):
            return own["w2n"][at : at + rows, :]

    def put(name, h, at, values):
        cols = values.shape[1]
        grads = spread(values).reshape(p.Z, p.Y, p.rp, cols)
        comm[name]["grad"][h, :, :, :, at : at + cols] = grads

    def put_shrink(at, rows, values):
        if even:
            low = values.astype(b16)
            start = at
            while start < at + rows:
                piece = start // p.rp2
                inner = start - piece * p.rp2
                size = min(p.rp2 - inner, at + rows - start)
                f, h = piece // 2, piece % 2
                comm["s"]["grad"][f // p.Y, f % p.Y, h, inner : inner + size, :] = low[
                    start - at : start - at + size
                ]
                start += size
        else:
            own["g2n"][at : at + rows, :] = values.astype(b16)

    refs = dict(
        x=x,
        cot=cot,
        v=own["v"],
        count=count[0, 0],
        sides=sides[0],
        out=out,
        grad=grad,
        gv=own["gv"],
        wf=lambda h: matrix("f", h, 0, half),
        wh=lambda: matrix("m", 0, 0, s.c),
        wp=lambda: matrix("m", 1, 0, s.c),
        w1=lambda h, at, cols: matrix("e", h, at, cols),
        w2=take_shrink,
        put_gf=lambda h, values: put("f", h, 0, values),
        put_gh=lambda values: put("m", 0, 0, values),
        put_gp=lambda values: put("m", 1, 0, values),
        put_g1=lambda h, at, cols, values: put("e", h, at, values),
        put_g2=put_shrink,
    )
    own["gv"][s.nvec :, :] = jnp.zeros((LANE - s.nvec, s.c), f32)
    block = Compute(s, refs, own["compute"])
    block.run()

    if not even:

        def open_up(f, carry):
            z, y = lax.div(f, p.Y), lax.rem(f, p.Y)
            at = pl.ds(pl.multiple_of(f * 2 * p.rows2, 2 * p.rows2), 2 * p.rows2)
            both = own["g2n"][at, :].astype(f32)
            for h in range(2):
                part = cut(both[h * p.rows2 : (h + 1) * p.rows2], p.rows2, p.rp2)
                comm["s"]["grad"][z, y, h] = part.astype(b16)
            return carry

        lax.fori_loop(0, p.fs, open_up, 0)
    grads = own["gv"][...].T
    if not even:
        grads = lax.dot_general(
            own["map"][...].astype(f32),
            grads,
            (((0,), (0,)), ((), ())),
            precision=lax.Precision.HIGHEST,
        )
    comm["v"]["grad"][...] = grads.reshape(p.whole("v"))
    results = dict(f=fin_f, v=fin_v, m=fin_m, e=fin_e, s=fin_s)
    reduces = [Reduce(name, k, comm[name], results[name]) for name in ("s", "e", "m", "f", "v")]
    for stage in ("one", "two", "three", "four", "five", "six"):
        for reduce in reduces:
            getattr(reduce, stage)()
    k.finish()


def adam_kernel(p, rates, *refs):
    s = p.s
    owners = refs[0]
    fins = dict(zip("fvmes", refs[1:6]))
    olds, news = refs[6:24], refs[24:42]
    g = lax.axis_index("grp")
    half, wide = s.c, s.hid // 2
    parts = (
        [("f", h, 0, p.rows, h * half, half) for h in range(2)],
        [("m", 0, 0, p.rows, 0, s.c)],
        [("m", 1, 0, p.rows, 0, s.c)],
        [("e", h, 0, p.rows, h * wide, wide) for h in range(2)],
        [("s", h, h * p.rows2, p.rows2, 0, s.c) for h in range(2)],
        [
            ("v", h, h * p.rv, min(p.rows - h * p.rv, p.rv), 0, s.nvec)
            for h in range(2)
        ],
    )
    for index, pieces in enumerate(parts):
        keep = owners[index] == g
        scale = jnp.where(keep, 1.0, 0.0).astype(f32)
        for name, h, row, rows, col, cols in pieces:
            at = (0, slice(row, row + rows), slice(col, col + cols))
            gradient = fins[name][h, :rows, :cols]
            weight, first, second = (olds[3 * index + i][at] for i in range(3))
            first_new = beta_one * first + (1.0 - beta_one) * gradient
            second_new = beta_two * second + (1.0 - beta_two) * gradient * gradient
            first_hat = first_new / (1.0 - beta_one**STEP)
            second_hat = second_new / (1.0 - beta_two**STEP)
            weight_new = weight - rates[index] * (
                first_hat / (jnp.sqrt(second_hat) + adam_eps) + weight_decay * weight
            )
            for i, value in enumerate((weight_new, first_new, second_new)):
                news[3 * index + i][at] = value * scale


def solution(mesh):
    n_grp, n_fs = mesh.shape["grp"], mesh.shape["fs"]

    def shards(image_patches, cotangent, image_count, resolution, owner_list, *tensors):
        side, channels = image_patches.shape[1], image_patches.shape[3]
        hid = tensors[9].shape[2]
        s = Shape(side, channels, hid)
        p = Plan(n_grp, n_fs, s)
        even = p.rp == p.rows and p.rp2 == p.rows2
        scratch = dict(
            comm=comm_scratch(p),
            compute=compute_scratch(s),
            v=pltpu.VMEM((LANE, s.c), f32),
            gv=pltpu.VMEM((LANE, s.c), f32),
            send_sem=pltpu.SemaphoreType.DMA((sem_count(p),)),
            recv_sem=pltpu.SemaphoreType.DMA((sem_count(p),)),
        )
        if not even:
            scratch["map"] = pltpu.VMEM((s.c, p.fs * p.rp), b16)
            scratch["w2n"] = pltpu.VMEM((s.hid, s.c), b16)
            scratch["g2n"] = pltpu.VMEM((s.hid, s.c), b16)
        leaves, tree = jax.tree.flatten(scratch, is_leaf=lambda v: not isinstance(v, (dict, list)))
        vmem = pl.BlockSpec(memory_space=pltpu.VMEM)
        smem = pl.BlockSpec(memory_space=pltpu.SMEM)
        shape = jax.ShapeDtypeStruct
        fins = [shape((2,) + p.pieces[name][:2], f32) for name in "fvmes"]
        tensors = tensors[:15] + tuple(t.transpose(0, 2, 1) for t in tensors[15:])
        results = pl.pallas_call(
            lambda *refs: block_kernel(p, tree, *refs),
            out_shape=[shape(image_patches.shape, b16), shape(image_patches.shape, f32)] + fins,
            in_specs=[smem] * 3 + [vmem] * 8,
            out_specs=[vmem] * 7,
            scratch_shapes=leaves,
            compiler_params=pltpu.CompilerParams(
                collective_id=0, has_side_effects=True, vmem_limit_bytes=VMEM_BYTES
            ),
            name="block",
        )(
            image_count,
            resolution,
            owner_list,
            image_patches,
            cotangent,
            tensors[0],
            tensors[3],
            tensors[6],
            tensors[9],
            tensors[12],
            tensors[15],
        )
        wide_rate = 1.5 / math.sqrt(channels)
        rates = (wide_rate,) * 4 + (1.5 / math.sqrt(hid), 0.2)
        news = pl.pallas_call(
            lambda *refs: adam_kernel(p, rates, *refs),
            out_shape=[shape(t.shape, f32) for t in tensors],
            in_specs=[smem] + [vmem] * 23,
            out_specs=[vmem] * 18,
            compiler_params=pltpu.CompilerParams(vmem_limit_bytes=VMEM_BYTES),
            name="adam",
        )(owner_list, *results[2:], *tensors)
        news = tuple(news[:15]) + tuple(t.transpose(0, 2, 1) for t in news[15:])
        return tuple(results[:2]) + news

    images = P(("grp", "fs"), None, None, None)
    weights = (P("grp", "fs", None),) * 15 + (P("grp", None, "fs"),) * 3
    return jax.shard_map(
        shards,
        mesh=mesh,
        in_specs=(images, images, P("grp", "fs"), P(("grp", "fs")), P()) + weights,
        out_specs=(images, images) + weights,
        check_vma=False,
    )
```

time: 732 us -> 132 us (0.18)
  waiting for transfers between devices: 328 us -> 0 us
  blocking collectives: 151 us -> 0 us
  matrix products: 132 us -> 0 us
  Pallas kernels: 0 us -> 127 us
  local copies, waits for them, and re-layouts: 55 us -> 2.23 us
  other arithmetic: 36.7 us -> 0 us
  between operations: 21.1 us -> 1.99 us
    reduce_scatter x5 -> x0, waiting for transfers between devices: 210 us -> none  [the longest x1 71.6 us: shards(): lax.psum_scatter(grad_shrink, 'fs', scatter_dimension=0, tiled=True)]
    pallas_call x0 -> x2, Pallas kernels: none -> 127 us  [the longest x1 123 us: shards(): pl.pallas_call(lambda *refs: block_kernel(p, tree, *refs), out_shape=[sha...]
    all_gather x4 -> x0, blocking collectives: 127 us -> none  [the longest x1 33 us: shards(): lax.all_gather(shares[2], 'fs', axis=0, tiled=True)]
    conv_general_dilated x9 -> x0, matrix products: 81 us -> none  [depthwise(): lax.conv_general_dilated(feature_map, kernel, (1, 1), 'SAME', dimension_n...]
    unnamed x12 -> x0, waiting for transfers between devices: 62.8 us -> none
    dot_general x18 -> x0, matrix products: 50.8 us -> none  [the longest x5 17.6 us: matmul_plain(): return jnp.dot(left_side, right_side, preferred_element_type=jnp.float32)]
    all_gather x2 -> x0, waiting for transfers between devices: 29.8 us -> none  [the longest x1 29.8 us: shards(): lax.all_gather(shares[4], 'fs', axis=0, tiled=True)]
    psum x3 -> x0, waiting for transfers between devices: 26.1 us -> none  [the longest x1 26.1 us: shards(): lax.psum((reduced[0], reduced[1], reduced[2], reduced[3], reduced[4], red...]
  transfers between devices with their start and end apart: 11 -> 0, of which waited for: 7 -> 0; matrix products, arithmetic and copies ran while one was open for 25% -> 0% of each run, Pallas kernels for 0% -> 0%
where the time goes in v1:
time: 132 us; the launch traced here: 131 us
  Pallas kernels  127 us (96%)
  local copies, waits for them, and re-layouts  2.23 us (2%)
  between operations  1.99 us (2%)
    pallas_call x1, Pallas kernels, shards(): pl.pallas_call(lambda *refs: block_kernel(p, tree, *refs), out_shape=[sha...  123 us
    pallas_call x1, Pallas kernels, shards(): pl.pallas_call(lambda *refs: adam_kernel(p, rates, *refs), out_shape=[sha...  4.08 us

profile of v1, /device:TPU:0, one launch (start us, length us, event | category | flops | bytes accessed | tf_op | source)
XLA Modules:
  0.0 131.5 jit_solution(15842503323186141511)
XLA Ops:
  1.9 123.2 %block.1 = (bf16[1,24,24,384]{3,2,1,0:T(8,128)(2,1)}, f32[1,24,24,384]{3,2,1,0:T(8,128)}, f32[2,48,384]{2,1,0:T(8,128)}, f32[2,24,128]{2,1,0:T(8,128)}, f32[2,48...) custom-call(s32[1,1]{1,0:T(1,128)S(6)} %copy.45.refs_0_, s32[1]{0:T(128)S(6)} %copy.46.refs_1_, ...), custom_call_target="tpu_custom_call" | custom-call | tf_op jit(solution)/shard_map/block/pallas_call | solution.py:1046
  125.1 0.0 copy-start.1
  125.1 4.1 %adam.1 = (f32[1,48,768]{2,1,0:T(8,128)}, f32[1,48,768]{2,1,0:T(8,128)}, f32[1,48,768]{2,1,0:T(8,128)}, f32[1,48,384]{2,1,0:T(8,128)}, f32[1,48,384]{2,1,0:T(8,1...) custom-call(s32[6]{0:T(128)} %refs_0_.2, ...), custom_call_target="tpu_custom_call" | custom-call | tf_op jit(solution)/shard_map/adam/pallas_call | solution.py:1071
  129.2 0.0 copy-start
  129.2 0.0 copy-done.1
  129.2 0.8 copy.47
  130.0 0.5 copy-done
  130.6 0.9 copy.48
Async XLA Ops:
  125.1 4.1 %copy-start.1 = (bf16[1,24,24,384]{3,2,1,0:T(8,128)(2,1)S(1)}, bf16[1,24,24,384]{3,2,1,0:T(8,128)(2,1)}, u32[]{:S(2)}) copy-start(bf16[1,24,24,384]{3,2,1,0:T(8,128)(2,1)} %get-tuple-element.90) | copy-start | bytes 1327108
  129.2 1.3 %copy-start = (f32[1,24,24,384]{3,2,1,0:T(8,128)S(1)}, f32[1,24,24,384]{3,2,1,0:T(8,128)}, u32[]{:S(2)}) copy-start(f32[1,24,24,384]{3,2,1,0:T(8,128)} %get-tuple-element.91) | copy-start | bytes 2654212

commit v2 on v1

v2 whole, which is shorter than its diff:
```python
import math

import jax
import jax.numpy as jnp
from jax import lax
from jax.experimental import pallas as pl
from jax.experimental.pallas import tpu as pltpu
from jax.sharding import PartitionSpec as P

f32 = jnp.float32
b16 = jnp.bfloat16
LEVELS = 3
GATES = 4
LANE = 128
norm_eps = 1e-05
PAD = 3
EDGE = 8
SQRT_HALF = math.sqrt(0.5)
INV_SQRT_2PI = 1.0 / math.sqrt(2.0 * math.pi)
BLK = 192


def gelu_parts(z):
    az = jnp.abs(z)
    t = 1.0 / (1.0 + (0.3275911 * SQRT_HALF) * az)
    e = jnp.exp(z * z * -0.5)
    poly = t * (
        0.5 * 0.254829592
        + t * (0.5 * -0.284496736 + t * (0.5 * 1.421413741 + t * (0.5 * -1.453152027 + t * (0.5 * 1.061405429))))
    )
    tail = poly * e
    phi = jnp.where(z >= 0.0, 1.0 - tail, tail)
    return z * phi, phi + z * e * INV_SQRT_2PI


def mm(a, b):
    return jnp.dot(a, b, preferred_element_type=f32)


def mm_t(a, b):
    return lax.dot_general(a, b, (((1,), (1,)), ((), ())), preferred_element_type=f32)


def mm_g(a, b):
    return lax.dot_general(a, b, (((0,), (0,)), ((), ())), preferred_element_type=f32)


def tall(values):
    rows, cols = values.shape
    return jnp.sum(values.reshape(rows // 8, 8, cols), axis=0)


def lane_sum(values):
    parts = values[:, :LANE]
    for start in range(LANE, values.shape[1], LANE):
        parts = parts + values[:, start : start + LANE]
    return jnp.sum(parts, axis=1, keepdims=True)


class Shape:
    def __init__(self, side, channels, hid):
        self.side = side
        self.rows = side * side
        self.c = channels
        self.nc = channels // LANE
        self.hid = hid
        self.bias_rows = hid // channels
        self.gate_at = 11 + self.bias_rows
        self.kernel_at = self.gate_at + GATES
        self.taps = [(2 * n + 3) ** 2 for n in range(LEVELS)]
        self.nvec = self.kernel_at + sum(self.taps)
        self.padded = (self.nc, side + 2 * PAD, side + 2 * EDGE, LANE)


def compute_scratch(s):
    flat = (s.rows, s.c)
    split = (s.nc, s.rows, LANE)
    grid = (s.nc, s.side, s.side, LANE)
    return dict(
        vc=pltpu.VMEM((s.nc, s.nvec, LANE), f32),
        mask=pltpu.VMEM((s.rows, LANE), f32),
        xh1=pltpu.VMEM(flat, f32),
        r1=pltpu.VMEM((s.rows, LANE), f32),
        n1b=pltpu.VMEM(flat, b16),
        gate=pltpu.VMEM((GATES, s.rows, LANE), f32),
        q=pltpu.VMEM(flat, f32),
        pads=[pltpu.VMEM(s.padded, f32) for _ in range(LEVELS + 1)],
        gd=[pltpu.VMEM(grid, f32) for _ in range(LEVELS)],
        summed=pltpu.VMEM(grid, f32),
        sumb=pltpu.VMEM(flat, b16),
        mod=pltpu.VMEM(flat, f32),
        mixb=pltpu.VMEM(flat, b16),
        proj=pltpu.VMEM(flat, f32),
        mid=pltpu.VMEM(flat, f32),
        xh2=pltpu.VMEM(flat, f32),
        r2=pltpu.VMEM((s.rows, LANE), f32),
        n2b=pltpu.VMEM(flat, b16),
        dshrb=pltpu.VMEM(flat, b16),
        actb=pltpu.VMEM((s.rows, s.hid), b16),
        dhidb=pltpu.VMEM((s.rows, s.hid), b16),
        shr=pltpu.VMEM(flat, f32),
        dn=pltpu.VMEM(flat, f32),
        dqb=pltpu.VMEM(flat, b16),
        dsum=pltpu.VMEM(split, f32),
        dgate=pltpu.VMEM((GATES, s.rows, LANE), f32),
        dctxb=pltpu.VMEM(flat, b16),
        gacc=pltpu.VMEM((s.nc, sum(s.taps), 8, LANE), f32),
        pool=pltpu.VMEM((2, 8, s.c), f32),
    )


class Compute:
    def __init__(self, s, refs, scratch):
        self.s = s
        self.__dict__.update(refs)
        self.__dict__.update(scratch)
        self.dmid, self.dprojb, self.dmodb = self.mid, self.dshrb, self.n2b

    def row(self, index):
        return self.v[index : index + 1, :]

    def wide_mask(self, at):
        m = self.mask[at, :]
        return jnp.concatenate([m] * self.s.nc, axis=1)

    def wide(self, ref, at):
        m = ref[at, :]
        return jnp.concatenate([m] * self.s.nc, axis=1)

    def blocks(self, body, sums=0):
        s = self.s
        start = tuple(jnp.zeros((8, s.c), f32) for _ in range(sums))

        def step(index, carry):
            at = pl.ds(pl.multiple_of(index * BLK, BLK), BLK)
            parts = body(at, pl.ds(index * (BLK // s.side), BLK // s.side))
            if not sums:
                return carry
            return tuple(total + tall(part) for total, part in zip(carry, parts))

        return lax.fori_loop(0, s.rows // BLK, step, start)

    def image(self, ref, lines):
        return ref[lines].astype(f32).reshape(BLK, self.s.c)

    def store(self, ref, lines, values):
        ref[lines] = values.reshape(BLK // self.s.side, self.s.side, self.s.c).astype(ref.dtype)

    def put(self, index, total):
        self.gv[index : index + 1, :] = jnp.sum(total, axis=0, keepdims=True)

    def prepare(self):
        s = self.s
        shape = (s.side, s.side, LANE)
        side = jnp.where(self.count > 0, self.sides, 0)
        inside = (lax.broadcasted_iota(jnp.int32, shape, 0) < side) & (
            lax.broadcasted_iota(jnp.int32, shape, 1) < side
        )
        self.mask[...] = jnp.where(inside, 1.0, 0.0).astype(f32).reshape(s.rows, LANE)

        def zero_plane(index, carry):
            for pad in self.pads:
                for ch in range(s.nc):
                    pad[ch, index, 0:EDGE, :] = jnp.zeros((EDGE, LANE), f32)
                    pad[ch, index, EDGE + s.side :, :] = jnp.zeros((EDGE, LANE), f32)
            return carry

        lax.fori_loop(0, s.side + 2 * PAD, zero_plane, 0)
        for pad in self.pads:
            for ch in range(s.nc):
                for edge in list(range(PAD)) + list(range(PAD + s.side, s.side + 2 * PAD)):
                    pad[ch, edge, EDGE : EDGE + s.side, :] = jnp.zeros((s.side, LANE), f32)

        def norm(at, lines):
            x = self.image(self.x, lines)
            centred = x - lane_sum(x) * (1.0 / s.c)
            r = lax.rsqrt(lane_sum(centred * centred) * (1.0 / s.c) + norm_eps)
            self.xh1[at, :] = centred * r
            self.r1[at, :] = jnp.broadcast_to(r, (BLK, LANE))

        self.blocks(norm)

        def clear(index, carry):
            for ch in range(s.nc):
                self.gacc[ch, index] = jnp.zeros((8, LANE), f32)
            return carry

        lax.fori_loop(0, sum(s.taps), clear, 0)

    def first(self):
        s = self.s
        for ch in range(s.nc):
            self.vc[ch] = self.v[: s.nvec, ch * LANE : (ch + 1) * LANE]
        gain, shift = self.row(0), self.row(1)
        weights = [self.row(s.gate_at + l) for l in range(GATES)]

        def step(at, lines):
            n1 = self.xh1[at, :] * gain + shift
            self.n1b[at, :] = n1.astype(b16)
            for l in range(GATES):
                self.gate[l, at, :] = jnp.broadcast_to(lane_sum(n1 * weights[l]), (BLK, LANE))

        self.blocks(step)

    def context(self, chunks):
        s = self.s
        lanes = slice(chunks[0] * LANE, (chunks[-1] + 1) * LANE)
        ctx = mm(self.n1b[...], self.wc(chunks)) + self.v[3:4, lanes]
        m = self.mask[...]
        for i, ch in enumerate(chunks):
            part = ctx[:, i * LANE : (i + 1) * LANE] * m
            self.pads[0][ch, PAD : PAD + s.side, EDGE : EDGE + s.side, :] = part.reshape(
                s.side, s.side, LANE
            )

    def query(self):
        self.q[...] = mm(self.n1b[...], self.wq()) + self.row(2)

    def level(self, l, chunks, block=6):
        s = self.s
        k = 2 * l + 3
        p = l + 1
        offset = s.kernel_at + sum(s.taps[:l])
        source = self.pads[l]
        per = s.side // block

        def step(index, carry):
            ch = chunks[0] + lax.div(index, per)
            r0 = lax.rem(index, per) * block
            acc = [None] * block
            for dc in range(-p, p + 1):
                taps = [
                    self.vc[ch, pl.ds(offset + (dr + p) * k + dc + p, 1), :]
                    for dr in range(-p, p + 1)
                ]
                for a in range(-p, block + p):
                    x = source[ch, r0 + PAD + a, pl.ds(EDGE + dc, s.side), :]
                    for o in range(max(0, a - p), min(block, a + p + 1)):
                        term = x * taps[a - o + p]
                        acc[o] = term if acc[o] is None else acc[o] + term
            for o in range(block):
                at = pl.ds(pl.multiple_of((r0 + o) * s.side, s.side), s.side)
                m = self.mask[at, :]
                value, slope = gelu_parts(acc[o])
                value = value * m
                self.gd[l][ch, r0 + o] = slope * m
                self.pads[l + 1][ch, r0 + o + PAD, EDGE : EDGE + s.side, :] = value
                term = value * self.gate[l, at, :]
                if l:
                    term = term + self.summed[ch, r0 + o]
                self.summed[ch, r0 + o] = term
            return carry

        lax.fori_loop(0, len(chunks) * per, step, 0)

    def pooling(self):
        s = self.s
        area = (self.sides * self.sides).astype(f32)
        for ch in range(s.nc):
            last = self.pads[LEVELS][ch, PAD : PAD + s.side, EDGE : EDGE + s.side, :]
            total = jnp.sum(tall(last.reshape(s.rows, LANE)), axis=0, keepdims=True)
            value, slope = gelu_parts(total / area)
            cols = slice(ch * LANE, (ch + 1) * LANE)
            self.pool[0, :, cols] = jnp.broadcast_to(value, (8, LANE))
            self.pool[1, :, cols] = jnp.broadcast_to(slope / area, (8, LANE))

        def step(index, carry):
            at = pl.ds(pl.multiple_of(index * BLK, BLK), BLK)
            gate = self.gate[LEVELS, at, :]
            for ch in range(s.nc):
                cols = slice(ch * LANE, (ch + 1) * LANE)
                part = self.summed[ch, pl.ds(index * (BLK // s.side), BLK // s.side)].reshape(BLK, LANE)
                self.sumb[at, cols] = (part + gate * self.pool[0, 0:1, cols]).astype(b16)
            return carry

        lax.fori_loop(0, s.rows // BLK, step, 0)

    def modulate(self):
        s = self.s
        self.mod[...] = mm(self.sumb[...], self.wh()) + self.row(4)

        def mix(at, lines):
            self.mixb[at, :] = (self.q[at, :] * self.mod[at, :]).astype(b16)

        self.blocks(mix)
        self.proj[...] = mm(self.mixb[...], self.wp()) + self.row(5)
        scale, gain, shift = self.row(6), self.row(7), self.row(8)
        upscale = self.row(10)

        def norm(at, lines):
            mid = self.image(self.x, lines) + scale * self.proj[at, :]
            self.mid[at, :] = mid
            centred = mid - lane_sum(mid) * (1.0 / s.c)
            r = lax.rsqrt(lane_sum(centred * centred) * (1.0 / s.c) + norm_eps)
            xh = centred * r
            self.xh2[at, :] = xh
            self.r2[at, :] = jnp.broadcast_to(r, (BLK, LANE))
            self.n2b[at, :] = (xh * gain + shift).astype(b16)
            d_shr = self.image(self.cot, lines) * self.wide_mask(at) * upscale
            self.dshrb[at, :] = d_shr.astype(b16)
            return (d_shr,)

        (g_b2,) = self.blocks(norm, 1)
        self.put(9, g_b2)

    def slope_tile(self, tile):
        s = self.s
        index, part = divmod(tile, s.nc)
        lanes = slice(part * LANE, (part + 1) * LANE)
        if index == 0:
            return self.dsum.at[part], (s.rows, LANE)
        if index == 1:
            return self.grad.at[:, :, lanes], (s.side, s.side, LANE)
        return (self.dn if index == 2 else self.shr).at[:, lanes], (s.rows, LANE)

    def feed(self, wide=256):
        s = self.s
        half = s.hid // 2
        for j in range(s.hid // wide):
            cols = slice(j * wide, (j + 1) * wide)
            h, at = divmod(j * wide, half)
            bias = []
            for start in range(j * wide, (j + 1) * wide, LANE):
                r, c = divmod(start, s.c)
                bias.append(self.v[11 + r : 12 + r, c : c + LANE])
            hid = mm(self.n2b[...], self.w1(h, at, wide)) + jnp.concatenate(bias, axis=1)
            act, slope = gelu_parts(hid)
            self.actb[:, cols] = act.astype(b16)
            for i in range(wide // LANE):
                ref, shape = self.slope_tile(j * wide // LANE + i)
                ref[...] = slope[:, i * LANE : (i + 1) * LANE].reshape(shape)

    def feed_back(self, wide=256):
        s = self.s
        for j in range(s.hid // wide):
            d_act = mm_t(self.dshrb[...], self.w2(j * wide, wide))
            for i in range(wide // LANE):
                ref, _ = self.slope_tile(j * wide // LANE + i)
                d_hid = d_act[:, i * LANE : (i + 1) * LANE] * ref[...].reshape(s.rows, LANE)
                start = j * wide + i * LANE
                self.dhidb[:, start : start + LANE] = d_hid.astype(b16)
                r, c = divmod(start, s.c)
                self.gv[11 + r : 12 + r, c : c + LANE] = jnp.sum(tall(d_hid), axis=0, keepdims=True)

    def shrink_grad(self):
        s = self.s
        for at in range(0, s.hid, s.c):
            self.put_g2(at, s.c, mm_g(self.actb[:, at : at + s.c], self.dshrb[...]))

    def expand_grad(self):
        s = self.s
        half = s.hid // 2
        for at in range(0, s.hid, s.c):
            self.put_g1(at // half, at % half, mm_g(self.n2b[...], self.dhidb[:, at : at + s.c]))

    def feed_out(self):
        s = self.s
        half = s.hid // 2
        self.shr[...] = mm(self.actb[...], self.w2(0, s.hid)) + self.row(9)
        self.dn[...] = mm_t(self.dhidb[:, :half], self.w1(0, 0, half)) + mm_t(
            self.dhidb[:, half:], self.w1(1, 0, half)
        )

    def middle(self):
        s = self.s
        gain, scale, upscale = self.row(7), self.row(6), self.row(10)

        def step(at, lines):
            shr, mid, proj, xh = self.shr[at, :], self.mid[at, :], self.proj[at, :], self.xh2[at, :]
            m = self.wide_mask(at)
            u = self.image(self.cot, lines) * m
            self.store(self.out, lines, (mid + upscale * shr) * m)
            d = self.dn[at, :]
            e = d * gain
            mean_e = lane_sum(e) * (1.0 / s.c)
            mean_x = lane_sum(e * xh) * (1.0 / s.c)
            d_mid = u + self.wide(self.r2, at) * (e - mean_e - xh * mean_x)
            self.dmid[at, :] = d_mid
            d_proj = scale * d_mid
            self.dprojb[at, :] = d_proj.astype(b16)
            return u * shr, d * xh, d, d_mid * proj, d_proj

        sums = self.blocks(step, 5)
        for index, total in zip((10, 7, 8, 6, 5), sums):
            self.put(index, total)
        self.dn[...] = mm_t(self.dprojb[...], self.wp())

        def split(at, lines):
            d = self.dn[at, :]
            d_q = d * self.mod[at, :]
            d_mod = d * self.q[at, :]
            self.dqb[at, :] = d_q.astype(b16)
            self.dmodb[at, :] = d_mod.astype(b16)
            return d_q, d_mod

        g_bq, g_bh = self.blocks(split, 2)
        self.put(2, g_bq)
        self.put(4, g_bh)
        d_sum = mm_t(self.dmodb[...], self.wh())
        for ch in range(s.nc):
            self.dsum[ch] = d_sum[:, ch * LANE : (ch + 1) * LANE]

    def middle_grads(self):
        self.put_gp(mm_g(self.mixb[...], self.dprojb[...]))
        self.put_gh(mm_g(self.sumb[...], self.dmodb[...]))

    def query_grad(self):
        self.put_gq(mm_g(self.n1b[...], self.dqb[...]))

    def focal_top(self):
        s = self.s

        def step(index, carry):
            at = pl.ds(pl.multiple_of(index * BLK, BLK), BLK)
            gate = self.gate[LEVELS, at, :]
            sums = [jnp.zeros((BLK, LANE), f32) for _ in range(GATES)]
            out = []
            for ch in range(s.nc):
                cols = slice(ch * LANE, (ch + 1) * LANE)
                d = self.dsum[ch, at, :]
                values = [
                    self.pads[l][ch, pl.ds(index * (BLK // s.side) + PAD, BLK // s.side), EDGE : EDGE + s.side, :]
                    for l in range(1, LEVELS + 1)
                ]
                for l in range(LEVELS):
                    sums[l] = sums[l] + d * values[l].reshape(BLK, LANE)
                sums[LEVELS] = sums[LEVELS] + d * self.pool[0, 0:1, cols]
                out.append(carry[ch] + tall(d * gate))
            for l in range(GATES):
                self.dgate[l, at, :] = jnp.broadcast_to(
                    jnp.sum(sums[l], axis=1, keepdims=True), (BLK, LANE)
                )
            return tuple(out)

        zero = jnp.zeros((8, LANE), f32)
        totals = lax.fori_loop(0, s.rows // BLK, step, (zero,) * s.nc)
        for ch in range(s.nc):
            cols = slice(ch * LANE, (ch + 1) * LANE)
            total = jnp.sum(totals[ch], axis=0, keepdims=True)
            self.pool[1, :, cols] = self.pool[1, :, cols] * total

        def last(index, carry):
            at = pl.ds(pl.multiple_of(index * BLK, BLK), BLK)
            gate = self.gate[LEVELS - 1, at, :]
            for ch in range(s.nc):
                cols = slice(ch * LANE, (ch + 1) * LANE)
                e = self.dsum[ch, at, :] * gate + self.pool[1, 0:1, cols]
                d = e.reshape(BLK // s.side, s.side, LANE) * self.gd[LEVELS - 1][ch, pl.ds(index * (BLK // s.side), BLK // s.side)]
                self.pads[LEVELS][ch, pl.ds(index * (BLK // s.side) + PAD, BLK // s.side), EDGE : EDGE + s.side, :] = d
            return carry

        lax.fori_loop(0, s.rows // BLK, last, 0)

    def level_back(self, l, chunks, block=4):
        s = self.s
        k = 2 * l + 3
        p = l + 1
        base = sum(s.taps[:l])
        offset = s.kernel_at + base
        source = self.pads[l + 1]
        inputs = self.pads[l]
        per = s.side // block

        def step(index, carry):
            ch = chunks[0] + lax.div(index, per)
            r0 = lax.rem(index, per) * block
            acc = [None] * block
            xs = [
                inputs[ch, r0 + PAD + o, EDGE : EDGE + s.side, :] for o in range(block)
            ]
            for dc in range(-p, p + 1):
                taps = [
                    self.vc[ch, pl.ds(offset + (dr + p) * k + dc + p, 1), :]
                    for dr in range(-p, p + 1)
                ]
                sums = [None] * k
                for a in range(-p, block + p):
                    d = source[ch, r0 + PAD + a, pl.ds(EDGE - dc, s.side), :]
                    for o in range(max(0, a - p), min(block, a + p + 1)):
                        dr = o - a
                        term = d * taps[dr + p]
                        acc[o] = term if acc[o] is None else acc[o] + term
                        part = tall(d * xs[o])
                        sums[dr + p] = part if sums[dr + p] is None else sums[dr + p] + part
                for dr in range(-p, p + 1):
                    tap = base + (dr + p) * k + dc + p
                    self.gacc[ch, tap] = self.gacc[ch, tap] + sums[dr + p]
            total = None
            for o in range(block):
                at = pl.ds(pl.multiple_of((r0 + o) * s.side, s.side), s.side)
                if l:
                    e = acc[o] + self.dsum[ch, at, :] * self.gate[l - 1, at, :]
                    self.pads[l][ch, r0 + o + PAD, EDGE : EDGE + s.side, :] = (
                        e * self.gd[l - 1][ch, r0 + o]
                    )
                else:
                    self.summed[ch, r0 + o] = acc[o] * self.mask[at, :]
            return carry

        lax.fori_loop(0, len(chunks) * per, step, 0)

    def context_grad(self, chunks):
        s = self.s

        def step(index, carry):
            at = pl.ds(pl.multiple_of(index * BLK, BLK), BLK)
            out = []
            for i, ch in enumerate(chunks):
                cols = slice(ch * LANE, (ch + 1) * LANE)
                lines = pl.ds(index * (BLK // s.side), BLK // s.side)
                d = self.summed[ch, lines].reshape(BLK, LANE)
                self.dctxb[at, cols] = d.astype(b16)
                out.append(carry[i] + tall(d))
            return tuple(out)

        zero = jnp.zeros((8, LANE), f32)
        totals = lax.fori_loop(0, s.rows // BLK, step, (zero,) * len(chunks))
        for i, ch in enumerate(chunks):
            cols = slice(ch * LANE, (ch + 1) * LANE)
            self.gv[3:4, cols] = jnp.sum(totals[i], axis=0, keepdims=True)
            self.gv[s.kernel_at : s.nvec, cols] = jnp.sum(self.gacc[ch], axis=1)
        lanes = slice(chunks[0] * LANE, (chunks[-1] + 1) * LANE)
        self.put_gc(chunks, mm_g(self.n1b[...], self.dctxb[:, lanes]))

    def last_back(self):
        s = self.s
        wc = self.wc(tuple(range(s.nc)))
        self.dn[...] = mm_t(self.dqb[...], self.wq()) + mm_t(self.dctxb[...], wc)
        gain, shift = self.row(0), self.row(1)
        weights = [self.row(s.gate_at + l) for l in range(GATES)]

        def step(at, lines):
            xh = self.xh1[at, :]
            n1 = xh * gain + shift
            d = self.dn[at, :]
            sums = []
            for l in range(GATES):
                dg = self.wide(self.dgate.at[l], at)
                d = d + dg * weights[l]
                sums.append(dg * n1)
            e = d * gain
            mean_e = lane_sum(e) * (1.0 / s.c)
            mean_x = lane_sum(e * xh) * (1.0 / s.c)
            d_in = self.dmid[at, :] + self.wide(self.r1, at) * (e - mean_e - xh * mean_x)
            self.store(self.grad, lines, d_in)
            return (d * xh, d) + tuple(sums)

        sums = self.blocks(step, 2 + GATES)
        for index, total in zip((0, 1) + tuple(s.gate_at + l for l in range(GATES)), sums):
            self.put(index, total)


MESH = pl.DeviceIdType.MESH
STEP = 10
beta_one = 0.9
beta_two = 0.95
adam_eps = 1e-08
weight_decay = 0.05
VMEM_BYTES = 63 * 2**20 + 2**19
GATHERED = "vabmes"
REDUCED = "sedmqtu"
DIRECT = "qtu"
NEAR = "va"
AT_ONCE = "vab"


class Plan:
    def __init__(self, n_grp, n_fs, s):
        self.X = n_grp // 2
        self.Y = 2 ** (int(math.log2(n_fs)) // 2)
        self.Z = n_fs // self.Y
        self.fs = n_fs
        self.s = s
        self.rows = s.c // n_fs
        self.rp = -(-self.rows // 16) * 16
        self.rows2 = s.hid // n_fs // 2
        self.rp2 = -(-self.rows2 // 16) * 16
        self.even = self.rp == self.rows and self.rp2 == self.rows2
        self.rv = self.rp // 2
        self.gather_cols = dict(v=LANE, a=LANE, b=2 * LANE, m=s.c, e=s.hid // 2, s=s.c)
        self.reduce_cols = dict(s=s.c, e=s.hid // 4, d=s.hid // 4, m=s.c, q=2 * LANE, t=LANE, u=LANE)

    def piece(self, name, cols):
        return (dict(s=self.rp2, v=self.rv).get(name, self.rp), cols[name])

    def whole(self, name, cols):
        if name in "sv":
            return (self.Z, self.Y, 2) + self.piece(name, cols)
        return (2, self.Z, self.Y) + self.piece(name, cols)


def gather_scratch(p, name):
    piece = p.piece(name, p.gather_cols)
    kind = f32 if name == "v" else b16
    return dict(
        cand=pltpu.VMEM((2,) + piece, kind),
        rx1=pltpu.VMEM(piece, kind),
        sel=pltpu.VMEM(piece, kind),
        rx2=pltpu.VMEM((p.X - 1, 2 if name in NEAR else 1) + piece, kind),
        full=pltpu.VMEM(p.whole(name, p.gather_cols), kind),
    )


def reduce_scratch(p, name):
    piece = p.piece(name, p.reduce_cols)
    out = dict(
        grad=pltpu.VMEM(p.whole(name, p.reduce_cols), b16),
        r1=pltpu.VMEM((p.Z, p.Y) + piece, b16),
        a3=pltpu.VMEM(piece, b16),
        a4=pltpu.VMEM(piece, f32),
        r4=pltpu.VMEM((p.X - 1, 2) + piece, b16),
        r5=pltpu.VMEM(piece, b16),
        fin=pltpu.VMEM((2,) + piece, f32),
    )
    if name in DIRECT:
        out["r3"] = pltpu.VMEM((p.fs - 1,) + piece, b16)
    else:
        out["r2"] = pltpu.VMEM((p.Y - 1, p.Z) + piece, b16)
        out["a2"] = pltpu.VMEM((p.Z,) + piece, b16)
        out["r3"] = pltpu.VMEM((p.Z - 1,) + piece, b16)
    return out


def sem_count(p):
    gather = 1 + 2 * (p.X - 1) + (p.Z - 1) + p.Z * (p.Y - 1) + p.fs
    reduce = 1 + max((p.Y - 1) + (p.Z - 1), p.fs - 1) + 2 * (p.X - 1) + 1
    return gather * len(GATHERED) + reduce * len(REDUCED)


class Links:
    def __init__(self, p, send_sem, recv_sem):
        self.p = p
        self.send_sem, self.recv_sem = send_sem, recv_sem
        self.used = 0
        self.sent = []
        self.g, self.f = lax.axis_index("grp"), lax.axis_index("fs")
        self.x, self.c = lax.div(self.g, 2), lax.rem(self.g, 2)
        self.z, self.y = lax.div(self.f, p.Y), lax.rem(self.f, p.Y)

    def sibling(self):
        return (self.x * 2 + 1 - self.c, self.f)

    def at_x(self, x, other_core=0):
        core = 1 - self.c if other_core else self.c
        return (x * 2 + core, self.f)

    def at_z(self, z):
        return (self.g, z * self.p.Y + self.y)

    def at_y(self, y):
        return (self.g, self.z * self.p.Y + y)

    def flip_z(self, bit):
        return self.z + bit - 2 * bit * lax.rem(lax.div(self.z, bit), 2)

    def signal_partners(self):
        p = self.p
        partners = (
            [self.sibling()]
            + [self.at_x(lax.rem(self.x + d, p.X), i) for d in range(1, p.X) for i in range(2)]
            + [(self.g, lax.rem(self.f + d, p.fs)) for d in range(1, p.fs)]
        )
        self.partners = len(partners)
        barrier = pltpu.get_barrier_semaphore()
        for partner in partners:
            pl.semaphore_signal(barrier, inc=1, device_id=partner, device_id_type=MESH)

    def wait_partners(self):
        pl.semaphore_wait(pltpu.get_barrier_semaphore(), self.partners)

    def send(self, source, target, partner, arriving=None):
        index = self.used
        self.used += 1

        def copy(src, dst):
            return pltpu.make_async_remote_copy(
                src_ref=src,
                dst_ref=dst,
                send_sem=self.send_sem.at[index],
                recv_sem=self.recv_sem.at[index],
                device_id=partner,
                device_id_type=MESH,
            )

        started = copy(source, target)
        started.start()
        self.sent.append(started)
        coming = copy(source, target if arriving is None else arriving)
        return coming.wait_recv

    def finish(self):
        for copy in self.sent:
            copy.wait_send()


class Gather:
    def __init__(self, name, links, refs):
        self.name, self.links, self.p = name, links, links.p
        self.near, self.direct = name in NEAR, name in AT_ONCE
        self.__dict__.update(refs)
        self.held, self.wait3, self.wait4, self.wait5 = [], [], [], []

    def piece(self, half, z, y):
        return self.full.at[z, y, half] if self.name in "sv" else self.full.at[half, z, y]

    def core_send(self, z, y):
        k = self.links
        here = self.piece(k.c, z, y)
        self.wait5.append(k.send(here, here, k.sibling(), self.piece(1 - k.c, z, y)))

    def one(self):
        k, p = self.links, self.p
        self.wait1 = k.send(self.cand.at[1 - k.c], self.rx1, k.sibling())
        if self.near:
            self.wait2 = []
            for d in range(1, p.X):
                x = lax.rem(k.x + d, p.X)
                for i, h in enumerate((k.c, 1 - k.c)):
                    self.wait2.append(k.send(self.cand.at[h], self.rx2.at[d - 1, i], k.at_x(x, i)))

    def two(self):
        k, p = self.links, self.p
        self.wait1()
        self.sel[...] = self.cand[k.c] + self.rx1[...]
        if not self.near:
            self.wait2 = [
                k.send(self.sel, self.rx2.at[d - 1, 0], k.at_x(lax.rem(k.x + d, p.X)))
                for d in range(1, p.X)
            ]

    def y_sends(self, z):
        k, p = self.links, self.p
        here = self.piece(k.c, z, k.y)
        for d in range(1, p.Y):
            other = lax.rem(k.y + p.Y - d, p.Y)
            partner = k.at_y(lax.rem(k.y + d, p.Y))
            wait = k.send(here, here, partner, self.piece(k.c, z, other))
            self.wait4.append((wait, z, other))

    def pair_round(self):
        k = self.links
        bit = self.p.Z >> (self.rounds + 1)
        partner = k.at_z(k.flip_z(bit))
        self.rounds += 1
        for z in self.held:
            other = z + bit - 2 * bit * lax.rem(lax.div(z, bit), 2)
            here = self.piece(k.c, z, k.y)
            wait = k.send(here, here, partner, self.piece(k.c, other, k.y))
            self.wait3.append((wait, other))

    def three(self):
        k, p = self.links, self.p
        for wait in self.wait2:
            wait()
        total = self.sel[...]
        for d in range(p.X - 1):
            for i in range(2 if self.near else 1):
                total = total + self.rx2[d, i]
        here = self.piece(k.c, k.z, k.y)
        here[...] = total
        self.held, self.rounds = [k.z], 0
        if self.direct:
            for d in range(1, p.Z):
                other = lax.rem(k.z + p.Z - d, p.Z)
                partner = k.at_z(lax.rem(k.z + d, p.Z))
                wait = k.send(here, here, partner, self.piece(k.c, other, k.y))
                self.wait3.append((wait, other))
        else:
            self.pair_round()

    def own(self):
        self.y_sends(self.links.z)
        self.core_send(self.links.z, self.links.y)

    def four(self):
        waits, self.wait3 = self.wait3, []
        for wait, z in waits:
            wait()
            self.held.append(z)
        if len(self.held) < self.p.Z:
            self.pair_round()
        for _, z in waits:
            self.y_sends(z)
            self.core_send(z, self.links.y)

    def five(self):
        while self.wait3:
            self.four()
        for wait, z, y in self.wait4:
            wait()
            self.core_send(z, y)

    def six(self):
        for wait in self.wait5:
            wait()


class Reduce:
    def __init__(self, name, links, refs):
        self.name, self.links, self.p = name, links, links.p
        self.direct = name in DIRECT
        self.__dict__.update(refs)

    def half(self, h):
        return self.grad.at[:, :, h] if self.name == "s" else self.grad.at[h]

    def one(self):
        k = self.links
        self.wait1 = k.send(self.half(1 - k.c), self.r1, k.sibling())

    def two(self):
        k, p = self.links, self.p
        self.wait1()
        mine = self.half(k.c)

        def add(index, carry):
            z, y = lax.div(index, p.Y), lax.rem(index, p.Y)
            self.r1[z, y] = self.r1[z, y] + mine[z, y]
            return carry

        lax.fori_loop(0, p.fs, add, 0)
        self.wait2 = []
        if self.direct:
            for d in range(1, p.fs):
                f = lax.rem(k.f + d, p.fs)
                source = self.r1.at[lax.div(f, p.Y), lax.rem(f, p.Y)]
                self.wait2.append(k.send(source, self.r3.at[d - 1], (k.g, f)))
            return
        for d in range(1, p.Y):
            other = lax.rem(k.y + d, p.Y)
            self.wait2.append(k.send(self.r1.at[:, other], self.r2.at[d - 1], k.at_y(other)))

    def three(self):
        k, p = self.links, self.p
        for wait in self.wait2:
            wait()
        self.wait3 = []
        if self.direct:
            total = self.r1[k.z, k.y].astype(f32)
            for d in range(p.fs - 1):
                total = total + self.r3[d].astype(f32)
            self.a4[...] = total
            return

        def add(z, carry):
            total = self.r1[z, k.y].astype(f32)
            for d in range(p.Y - 1):
                total = total + self.r2[d, z].astype(f32)
            self.a2[z] = total.astype(b16)
            return carry

        lax.fori_loop(0, p.Z, add, 0)
        self.bit, self.slot = 1, 0
        self.pair_round()

    def pair_round(self):
        k, p = self.links, self.p
        bit = self.bit
        partner = k.flip_z(bit)
        low_partner, own = lax.rem(partner, 2 * bit), lax.rem(k.z, 2 * bit)
        self.wait3 = []
        for step in range(p.Z // (2 * bit)):
            target = low_partner + 2 * bit * step
            mine = own + 2 * bit * step
            wait = k.send(self.a2.at[target], self.r3.at[self.slot], k.at_z(partner))
            self.wait3.append((wait, mine, self.slot))
            self.slot += 1
        self.bit = 2 * bit

    def four(self):
        for wait, z, slot in self.wait3:
            wait()
            total = self.a2[z].astype(f32) + self.r3[slot].astype(f32)
            if self.bit < self.p.Z:
                self.a2[z] = total.astype(b16)
            else:
                self.a4[...] = total
        self.wait3 = []
        if not self.direct and self.bit < self.p.Z:
            self.pair_round()

    def five(self):
        k, p = self.links, self.p
        while self.wait3:
            self.four()
        self.a3[...] = self.a4[...].astype(b16)
        self.wait4 = []
        for d in range(1, p.X):
            x = lax.rem(k.x + d, p.X)
            for i in range(2):
                self.wait4.append(k.send(self.a3, self.r4.at[d - 1, i], k.at_x(x, i)))
        self.wait4.append(k.send(self.a3, self.r5, k.sibling()))

    def six(self):
        k, p = self.links, self.p
        for wait in self.wait4:
            wait()
        for h, total, i in ((k.c, self.a4[...], 0), (1 - k.c, self.r5[...].astype(f32), 1)):
            for d in range(p.X - 1):
                total = total + self.r4[d, i].astype(f32)
            self.fin[h] = total


def spread_matrix(rows, rp, count):
    bits = int(math.log2(rp))
    shape = (count * rows, count * rp)
    a = lax.broadcasted_iota(jnp.int32, shape, 0)
    b = lax.broadcasted_iota(jnp.int32, shape, 1)
    i = lax.bitwise_and(b, rp - 1)
    hit = (a == lax.shift_right_logical(b, bits) * rows + i) & (i < rows)
    return jnp.where(hit, 1.0, 0.0).astype(b16)


def block_kernel(p, tree, *refs):
    s = p.s
    count, sides, owners = refs[:3]
    sources = dict(zip(("x", "cot", "focal", "modulate", "project", "expand", "shrink", "vector"), refs[3:11]))
    out_hbm, grad_hbm = refs[11:13]
    fin_hbm = dict(zip(REDUCED, refs[13:20]))
    own = jax.tree.unflatten(tree, refs[20:])
    k = Links(p, own["send_sem"], own["recv_sem"])
    land, local_sem = own["land"], own["local_sem"]
    local_used = []

    def local(source, target):
        copy = pltpu.make_async_copy(source, target, local_sem.at[len(local_used)])
        local_used.append(copy)
        copy.start()
        return copy

    loads = {}
    for name in ("focal", "vector", "modulate", "project", "x", "expand", "shrink", "cot"):
        loads[name] = local(sources[name].at[0], land[name])
    k.signal_partners()

    def mine(index):
        return jnp.where(owners[index] == k.g, 1.0, 0.0).astype(f32)

    def cut(values, rows, rp):
        if rows == rp:
            return values
        return jnp.concatenate([values, jnp.zeros((rp - rows, values.shape[1]), f32)], axis=0)

    def candidate(name, h, values):
        rows, rp = values.shape[0], p.piece(name, p.gather_cols)[0]
        own["g" + name]["cand"][h] = cut(values, rows, rp).astype(b16)

    gathers = {
        name: Gather(name, k, own["g" + name]) for name in GATHERED
    }
    gv, ga, gb, gm, ge, gs = (gathers[name] for name in GATHERED)
    reduces = {name: Reduce(name, k, own["r" + name]) for name in REDUCED}
    rs, re, rd, rm, rq, rt, ru = (reduces[name] for name in REDUCED)
    c, wide = s.c, s.hid // 2

    loads["focal"].wait()
    loads["vector"].wait()
    focal = land["focal"]
    values = cut(land["vector"][...] * mine(5), p.rows, p.rp)
    values = jnp.concatenate([values, jnp.zeros((p.rp, LANE - s.nvec), f32)], axis=1)
    for h in range(2):
        own["gv"]["cand"][h] = values[h * p.rv : (h + 1) * p.rv]
        at = c + h * LANE
        candidate("a", h, focal[:, at : at + LANE] * mine(0))
    k.wait_partners()
    gv.one()
    ga.one()
    candidate("b", 0, jnp.concatenate([focal[:, c + 2 * LANE :], focal[:, :LANE]], axis=1) * mine(0))
    candidate("b", 1, focal[:, LANE:c] * mine(0))
    gb.one()
    loads["modulate"].wait()
    loads["project"].wait()
    candidate("m", 0, land["modulate"][...] * mine(1))
    candidate("m", 1, land["project"][...] * mine(2))
    gm.one()
    gb.two()
    loads["expand"].wait()
    for h in range(2):
        candidate("e", h, land["expand"][:, h * wide : (h + 1) * wide] * mine(3))
    ge.one()
    loads["shrink"].wait()
    for h in range(2):
        candidate("s", h, land["shrink"][h * p.rows2 : (h + 1) * p.rows2, :] * mine(4))
    gs.one()

    if not p.even:
        own["map"][...] = spread_matrix(p.rows, p.rp, p.fs)

    def compact(values):
        return values if p.even else mm(own["map"][...], values).astype(b16)

    def spread(values):
        values = values.astype(b16)
        return values if p.even else mm_g(own["map"][...], values).astype(b16)

    def matrix(name, h, at, cols):
        part = own["g" + name]["full"][h, :, :, :, at : at + cols]
        return compact(part.reshape(p.fs * p.rp, cols))

    def take_context(chunks):
        parts = []
        if chunks[0] < 2:
            parts += [matrix("a", ch, 0, LANE) for ch in chunks if ch < 2]
        if chunks[-1] == 2:
            parts.append(matrix("b", 0, 0, LANE))
        return jnp.concatenate(parts, axis=1) if len(parts) > 1 else parts[0]

    def take_query():
        return jnp.concatenate([matrix("b", 0, LANE, LANE), matrix("b", 1, 0, 2 * LANE)], axis=1)

    def take_shrink(at, rows):
        if p.even:
            return own["gs"]["full"][...].reshape(s.hid, s.c)[at : at + rows]
        return own["w2n"][at : at + rows, :]

    def put(name, h, at, values):
        cols = values.shape[1]
        grads = spread(values).reshape(p.Z, p.Y, p.rp, cols)
        own["r" + name]["grad"][h, :, :, :, at : at + cols] = grads

    def put_query(values):
        put("q", 0, 0, values[:, : 2 * LANE])
        put("q", 1, 0, values[:, 2 * LANE :])

    def put_context(chunks, values):
        for i, ch in enumerate(chunks):
            name, h = (("t", 0), ("t", 1), ("u", 0))[ch]
            put(name, h, 0, values[:, i * LANE : (i + 1) * LANE])

    def put_shrink(at, rows, values):
        low = values.astype(b16)
        if not p.even:
            own["g2n"][at : at + rows, :] = low
            return
        start = at
        while start < at + rows:
            piece, inner = divmod(start, p.rp2)
            size = min(p.rp2 - inner, at + rows - start)
            (f, h), first = divmod(piece, 2), start - at
            own["rs"]["grad"][f // p.Y, f % p.Y, h, inner : inner + size, :] = low[first : first + size]
            start += size

    block = Compute(
        s,
        dict(
            x=land["x"],
            cot=land["cot"],
            v=own["v"],
            count=count[0, 0],
            sides=sides[0],
            out=own["out"],
            grad=own["grad"],
            gv=own["gvec"],
            wc=take_context,
            wq=take_query,
            wh=lambda: matrix("m", 0, 0, c),
            wp=lambda: matrix("m", 1, 0, c),
            w1=lambda h, at, cols: matrix("e", h, at, cols),
            w2=take_shrink,
            put_gq=put_query,
            put_gc=put_context,
            put_gh=lambda values: put("m", 0, 0, values),
            put_gp=lambda values: put("m", 1, 0, values),
            put_g1=lambda h, at, values: put("d" if at else "e", h, 0, values),
            put_g2=put_shrink,
        ),
        own["compute"],
    )

    stores = []

    def settle(name):
        reduces[name].six()
        stores.append(local(own["r" + name]["fin"], fin_hbm[name]))

    def prepare():
        loads["x"].wait()
        block.prepare()
        own["gvec"][s.nvec :, :] = jnp.zeros((LANE - s.nvec, s.c), f32)
        put("q", 1, LANE, jnp.zeros((s.c, LANE), f32))

    def take_vector():
        vector = own["gv"]["full"][...].reshape(p.fs * p.rp, LANE)
        if not p.even:
            vector = jnp.dot(own["map"][...].astype(f32), vector, precision=lax.Precision.HIGHEST)
        own["v"][...] = vector.T

    def modulate():
        loads["cot"].wait()
        block.modulate()

    def close_shrink():
        def close(f, carry):
            z, y = lax.div(f, p.Y), lax.rem(f, p.Y)
            parts = [own["gs"]["full"][z, y, h].astype(f32)[: p.rows2] for h in range(2)]
            at = pl.ds(pl.multiple_of(f * 2 * p.rows2, 2 * p.rows2), 2 * p.rows2)
            own["w2n"][at, :] = jnp.concatenate(parts, axis=0).astype(b16)
            return carry

        if not p.even:
            lax.fori_loop(0, p.fs, close, 0)

    def shrink_grad():
        block.shrink_grad()

        def open_up(f, carry):
            z, y = lax.div(f, p.Y), lax.rem(f, p.Y)
            at = pl.ds(pl.multiple_of(f * 2 * p.rows2, 2 * p.rows2), 2 * p.rows2)
            both = own["g2n"][at, :].astype(f32)
            for h in range(2):
                part = cut(both[h * p.rows2 : (h + 1) * p.rows2], p.rows2, p.rp2)
                own["rs"]["grad"][z, y, h] = part.astype(b16)
            return carry

        if not p.even:
            lax.fori_loop(0, p.fs, open_up, 0)

    def middle():
        block.middle()
        stores.append(local(own["out"], out_hbm.at[0]))

    def last_back():
        block.last_back()
        stores.append(local(own["grad"], grad_hbm.at[0]))

    def put_vector():
        grads = own["gvec"][...].T
        if not p.even:
            grads = mm_g(own["map"][...], grads.astype(b16))
        own["ru"]["grad"][1] = grads.astype(b16).reshape(p.Z, p.Y, p.rp, LANE)

    gm.two()
    ga.two()
    gv.two()
    gv.three()
    ga.three()
    ge.two()
    gb.three()
    gv.own()
    gm.three()
    ga.own()
    gs.two()
    gm.own()
    ge.three()
    gb.own()
    gv.four()
    ge.own()
    gs.three()
    ga.four()
    gv.five()
    gb.four()
    gv.six()
    prepare()
    ge.four()
    take_vector()
    gs.own()
    gm.four()
    ga.five()
    gb.five()
    block.first()
    ga.six()
    block.context((0, 1))
    block.level(0, (0, 1))
    gs.four()
    block.level(1, (0, 1))
    ge.four()
    gb.six()
    block.context((2,))
    block.level(2, (0, 1))
    gm.four()
    block.level(0, (2,))
    block.query()
    block.level(1, (2,))
    gs.four()
    ge.five()
    block.level(2, (2,))
    gm.five()
    ge.six()
    block.pooling()
    gm.six()
    modulate()
    gs.five()
    block.feed()
    gs.six()
    shrink_grad()
    rs.one()
    close_shrink()
    block.feed_back()
    block.expand_grad()
    rs.two()
    re.one()
    block.feed_out()
    middle()
    block.query_grad()
    block.middle_grads()
    rq.one()
    rm.one()
    block.focal_top()
    re.two()
    rm.two()
    rq.two()
    block.level_back(2, (0, 1))
    rs.three()
    block.level_back(1, (0, 1))
    rd.one()
    re.three()
    block.level_back(0, (0, 1))
    rd.two()
    block.context_grad((0, 1))
    rm.three()
    rt.one()
    rs.four()
    rt.two()
    block.level_back(2, (2,))
    block.level_back(1, (2,))
    block.level_back(0, (2,))
    rd.three()
    block.context_grad((2,))
    re.four()
    rq.three()
    last_back()
    rm.four()
    rs.five()
    put_vector()
    ru.one()
    rq.five()
    ru.two()
    rd.four()
    re.five()
    rt.three()
    rm.five()
    rt.five()
    ru.three()
    ru.five()
    rd.five()
    settle("e")
    settle("m")
    settle("s")
    settle("u")
    settle("t")
    settle("q")
    settle("d")
    k.finish()
    for store in stores:
        store.wait()


def adam_kernel(p, rates, tree, *refs):
    s = p.s
    owners = refs[0]
    fins = dict(zip(REDUCED, refs[1:8]))
    passed, olds = refs[8:10], refs[10:28]
    passed_out, news = refs[28:30], refs[30:48]
    own = jax.tree.unflatten(tree, refs[48:])
    sems = own["sem"]
    g = lax.axis_index("grp")
    used = []

    def local(source, target):
        copy = pltpu.make_async_copy(source, target, sems.at[len(used)])
        used.append(copy)
        copy.start()
        return copy

    wide = s.hid // 2
    groups = (
        (3, [(n, h, 0, p.rows, h * wide + i * s.c, s.c) for h in range(2) for i, n in enumerate("ed")]),
        (4, [("s", h, h * p.rows2, p.rows2, 0, s.c) for h in range(2)]),
        (1, [("m", 0, 0, p.rows, 0, s.c)]),
        (2, [("m", 1, 0, p.rows, 0, s.c)]),
        (
            0,
            [
                ("q", 0, 0, p.rows, 0, 2 * LANE),
                ("q", 1, 0, p.rows, 2 * LANE, LANE),
                ("t", 0, 0, p.rows, s.c, LANE),
                ("t", 1, 0, p.rows, s.c + LANE, LANE),
                ("u", 0, 0, p.rows, s.c + 2 * LANE, LANE),
            ],
        ),
        (5, [("u", 1, 0, p.rows, 0, s.nvec)]),
    )
    waits = {}
    for index, pieces in groups:
        waits[index] = []
        for name in dict.fromkeys(piece[0] for piece in pieces):
            if name not in waits:
                waits[name] = local(fins[name], own["fin"][name])
        for i in range(3):
            waits[index].append(local(olds[3 * index + i], own["old"][3 * index + i]))
    passing = [local(a, b) for a, b in zip(passed, own["passed"])]
    stores, arrived = [], set()
    for index, pieces in groups:
        scale = jnp.where(owners[index] == g, 1.0, 0.0).astype(f32)
        for wait in waits[index]:
            wait.wait()
        for name, h, row, rows, col, cols in pieces:
            if name not in arrived:
                arrived.add(name)
                waits[name].wait()
            at = (0, slice(row, row + rows), slice(col, col + cols))
            gradient = own["fin"][name][h, :rows, :cols]
            weight, first, second = (own["old"][3 * index + i][at] for i in range(3))
            first_new = beta_one * first + (1.0 - beta_one) * gradient
            second_new = beta_two * second + (1.0 - beta_two) * gradient * gradient
            first_hat = first_new / (1.0 - beta_one**STEP)
            second_hat = second_new / (1.0 - beta_two**STEP)
            weight_new = weight - rates[index] * (
                first_hat / (jnp.sqrt(second_hat) + adam_eps) + weight_decay * weight
            )
            for i, value in enumerate((weight_new, first_new, second_new)):
                own["new"][3 * index + i][at] = value * scale
        for i in range(3):
            stores.append(local(own["new"][3 * index + i], news[3 * index + i]))
    for wait, a, b in zip(passing, own["passed"], passed_out):
        wait.wait()
        stores.append(local(a, b))
    for store in stores:
        store.wait()


def solution(mesh):
    n_grp, n_fs = mesh.shape["grp"], mesh.shape["fs"]

    def shards(image_patches, cotangent, image_count, resolution, owner_list, *tensors):
        side, channels = image_patches.shape[1], image_patches.shape[3]
        hid = tensors[9].shape[2]
        s = Shape(side, channels, hid)
        p = Plan(n_grp, n_fs, s)
        grid = (side, side, channels)
        scratch = dict(
            compute=compute_scratch(s),
            land=dict(
                x=pltpu.VMEM(grid, b16),
                cot=pltpu.VMEM(grid, b16),
                focal=pltpu.VMEM((p.rows, 2 * channels), f32),
                modulate=pltpu.VMEM((p.rows, channels), f32),
                project=pltpu.VMEM((p.rows, channels), f32),
                expand=pltpu.VMEM((p.rows, hid), f32),
                shrink=pltpu.VMEM((2 * p.rows2, channels), f32),
                vector=pltpu.VMEM((p.rows, s.nvec), f32),
            ),
            out=pltpu.VMEM(grid, b16),
            grad=pltpu.VMEM(grid, f32),
            v=pltpu.VMEM((LANE, s.c), f32),
            gvec=pltpu.VMEM((LANE, s.c), f32),
            local_sem=pltpu.SemaphoreType.DMA((24,)),
            send_sem=pltpu.SemaphoreType.DMA((sem_count(p),)),
            recv_sem=pltpu.SemaphoreType.DMA((sem_count(p),)),
        )
        for name in GATHERED:
            scratch["g" + name] = gather_scratch(p, name)
        for name in REDUCED:
            scratch["r" + name] = reduce_scratch(p, name)
        if not p.even:
            scratch["map"] = pltpu.VMEM((s.c, p.fs * p.rp), b16)
            scratch["w2n"] = pltpu.VMEM((s.hid, s.c), b16)
            scratch["g2n"] = pltpu.VMEM((s.hid, s.c), b16)

        def flatten(scratch):
            return jax.tree.flatten(scratch, is_leaf=lambda v: not isinstance(v, (dict, list)))

        leaves, tree = flatten(scratch)
        anywhere = pl.BlockSpec(memory_space=pl.ANY)
        smem = pl.BlockSpec(memory_space=pltpu.SMEM)
        shape = jax.ShapeDtypeStruct
        fins = [shape((2,) + p.piece(name, p.reduce_cols), f32) for name in REDUCED]
        images = [shape(image_patches.shape, b16), shape(image_patches.shape, f32)]
        tensors = tensors[:15] + tuple(t.transpose(0, 2, 1) for t in tensors[15:])
        results = pl.pallas_call(
            lambda *refs: block_kernel(p, tree, *refs),
            out_shape=images + fins,
            in_specs=[smem] * 3 + [anywhere] * 8,
            out_specs=[anywhere] * 9,
            scratch_shapes=leaves,
            compiler_params=pltpu.CompilerParams(
                collective_id=0, has_side_effects=True, vmem_limit_bytes=VMEM_BYTES
            ),
            name="block",
        )(
            image_count,
            resolution,
            owner_list,
            image_patches,
            cotangent,
            *tensors[0:16:3],
        )
        wide_rate = 1.5 / math.sqrt(channels)
        rates = (wide_rate,) * 4 + (1.5 / math.sqrt(hid), 0.2)
        adam_leaves, adam_tree = flatten(
            dict(
                fin={name: pltpu.VMEM((2,) + p.piece(name, p.reduce_cols), f32) for name in REDUCED},
                old=[pltpu.VMEM(t.shape, f32) for t in tensors],
                new=[pltpu.VMEM(t.shape, f32) for t in tensors],
                passed=[pltpu.VMEM(t.shape, t.dtype) for t in images],
                sem=pltpu.SemaphoreType.DMA((56,)),
            )
        )
        news = pl.pallas_call(
            lambda *refs: adam_kernel(p, rates, adam_tree, *refs),
            out_shape=images + [shape(t.shape, f32) for t in tensors],
            in_specs=[smem] + [anywhere] * 27,
            out_specs=[anywhere] * 20,
            scratch_shapes=adam_leaves,
            compiler_params=pltpu.CompilerParams(vmem_limit_bytes=VMEM_BYTES),
            name="adam",
        )(owner_list, *results[2:], *results[:2], *tensors)
        return tuple(news[:17]) + tuple(t.transpose(0, 2, 1) for t in news[17:])

    images = P(("grp", "fs"), None, None, None)
    weights = (P("grp", "fs", None),) * 15 + (P("grp", None, "fs"),) * 3
    return jax.shard_map(
        shards,
        mesh=mesh,
        in_specs=(images, images, P("grp", "fs"), P(("grp", "fs")), P()) + weights,
        out_specs=(images, images) + weights,
        check_vma=False,
    )
```

time: 132 us -> 92.5 us (0.70)
  Pallas kernels: 127 us -> 90.2 us
  local copies, waits for them, and re-layouts: 2.23 us -> 0 us
    pallas_call x2, Pallas kernels: 127 us -> 90.2 us  [the longest x1 85.3 us: shards(): pl.pallas_call(lambda *refs: block_kernel(p, tree, *refs), out_shape=imag...]
    unnamed x6 -> x0, local copies, waits for them, and re-layouts: 2.23 us -> none
where the time goes in v2:
time: 92.5 us; the launch traced here: 92.3 us
  Pallas kernels  90.2 us (98%)
  between operations  2.12 us (2%)
    pallas_call x1, Pallas kernels, shards(): pl.pallas_call(lambda *refs: block_kernel(p, tree, *refs), out_shape=imag...  85.3 us
    pallas_call x1, Pallas kernels, shards(): pl.pallas_call(lambda *refs: adam_kernel(p, rates, adam_tree, *refs), out...  4.89 us

profile of v2, /device:TPU:0, one launch (start us, length us, event | category | flops | bytes accessed | tf_op | source)
XLA Modules:
  0.0 92.3 jit_solution(11868389287280596991)
XLA Ops:
  1.9 85.3 %block.1 = (bf16[1,24,24,384]{3,2,1,0:T(8,128)(2,1)}, f32[1,24,24,384]{3,2,1,0:T(8,128)}, f32[2,96,384]{2,1,0:T(8,128)}, f32[2,48,384]{2,1,0:T(8,128)}, f32[2,48...) custom-call(s32[1,1]{1,0:T(1,128)S(6)} %copy.43.refs_0_, ...), custom_call_target="tpu_custom_call" | custom-call | tf_op jit(solution)/shard_map/block/pallas_call | solution.py:1370
  87.2 4.9 %adam.1 = (bf16[1,24,24,384]{3,2,1,0:T(8,128)(2,1)}, f32[1,24,24,384]{3,2,1,0:T(8,128)}, f32[1,48,768]{2,1,0:T(8,128)}, f32[1,48,768]{2,1,0:T(8,128)}, f32[1,48,...) custom-call(s32[6]{0:T(128)} %refs_0_.2, ...), custom_call_target="tpu_custom_call" | custom-call | tf_op jit(solution)/shard_map/adam/pallas_call | solution.py:1399

commit v3 on v2

--- a/solution.py
+++ b/solution.py
@@ -17,7 +17,7 @@
 EDGE = 8
 SQRT_HALF = math.sqrt(0.5)
 INV_SQRT_2PI = 1.0 / math.sqrt(2.0 * math.pi)
-BLK = 192
+BLK = 576
 
 
 def gelu_parts(z):
@@ -69,7 +69,8 @@
         self.kernel_at = self.gate_at + GATES
         self.taps = [(2 * n + 3) ** 2 for n in range(LEVELS)]
         self.nvec = self.kernel_at + sum(self.taps)
-        self.padded = (self.nc, side + 2 * PAD, side + 2 * EDGE, LANE)
+        self.high = side + 2 * PAD + 1
+        self.padded = (self.nc, self.high, side + 2 * EDGE, LANE)
 
 
 def compute_scratch(s):
@@ -86,6 +87,7 @@
         q=pltpu.VMEM(flat, f32),
         pads=[pltpu.VMEM(s.padded, f32) for _ in range(LEVELS + 1)],
         gd=[pltpu.VMEM(grid, f32) for _ in range(LEVELS)],
+        sums=pltpu.VMEM((s.side,) + s.padded[2:], f32),
         summed=pltpu.VMEM(grid, f32),
         sumb=pltpu.VMEM(flat, b16),
         mod=pltpu.VMEM(flat, f32),
@@ -165,11 +167,14 @@
                     pad[ch, index, EDGE + s.side :, :] = jnp.zeros((EDGE, LANE), f32)
             return carry
 
-        lax.fori_loop(0, s.side + 2 * PAD, zero_plane, 0)
+        lax.fori_loop(0, s.high, zero_plane, 0)
         for pad in self.pads:
             for ch in range(s.nc):
-                for edge in list(range(PAD)) + list(range(PAD + s.side, s.side + 2 * PAD)):
+                for edge in list(range(PAD)) + list(range(PAD + s.side, s.high)):
                     pad[ch, edge, EDGE : EDGE + s.side, :] = jnp.zeros((s.side, LANE), f32)
+
+    def first_norm(self):
+        s = self.s
 
         def norm(at, lines):
             x = self.image(self.x, lines)
@@ -179,13 +184,6 @@
             self.r1[at, :] = jnp.broadcast_to(r, (BLK, LANE))
 
         self.blocks(norm)
-
-        def clear(index, carry):
-            for ch in range(s.nc):
-                self.gacc[ch, index] = jnp.zeros((8, LANE), f32)
-            return carry
-
-        lax.fori_loop(0, sum(s.taps), clear, 0)
 
     def first(self):
         s = self.s
@@ -216,42 +214,111 @@
     def query(self):
         self.q[...] = mm(self.n1b[...], self.wq()) + self.row(2)
 
-    def level(self, l, chunks, block=6):
+    def plane_sum(self, plane, count, at):
+        def row(n):
+            ref, base, stride = plane
+            return ref[base + stride * n]
+
+        for n in range(count):
+            self.sums[at + n] = row(2 * n + 1) + row(2 * n + 2)
+        return (self.sums, at, 1)
+
+    def direct_rows(self, plane, taps, rows, weights=None):
+        s = self.s
+        ref, base, stride = plane
+        out, grads = [None] * rows, {}
+        for dc, column in taps.items():
+            k = len(column)
+            sums = [None] * k
+            for a in range(rows + k - 1):
+                x = ref[base + stride * a, pl.ds(EDGE + dc, s.side), :]
+                for o in range(max(0, a - k + 1), min(rows, a + 1)):
+                    t = a - o
+                    term = x * column[t]
+                    out[o] = term if out[o] is None else out[o] + term
+                    if weights is not None:
+                        part = tall(x * weights[o])
+                        sums[t] = part if sums[t] is None else sums[t] + part
+            grads[dc] = sums
+        return out, grads
+
+    def fast_rows(self, plane, taps, rows, depth, weights=None, at=0):
+        length = len(next(iter(taps.values())))
+        if depth == 0 or length == 1:
+            return self.direct_rows(plane, taps, rows, weights)
+        if rows % 2:
+            ref, base, stride = plane
+            last = (ref, base + stride * (rows - 1), stride)
+            head = None if weights is None else weights[:-1]
+            out, grads = self.fast_rows(plane, taps, rows - 1, depth, head, at)
+            more, more_grads = self.direct_rows(last, taps, 1, None if weights is None else weights[-1:])
+            if weights is not None:
+                for dc in taps:
+                    grads[dc] = [x + y for x, y in zip(grads[dc], more_grads[dc])]
+            return out + more, grads
+        n = rows // 2
+        ref, base, stride = plane
+        even, odd = (ref, base, 2 * stride), (ref, base + stride, 2 * stride)
+        e_taps = {dc: column[0::2] for dc, column in taps.items()}
+        o_taps = {dc: column[1::2] for dc, column in taps.items()}
+        s_taps = {
+            dc: [x + o_taps[dc][i] if i < len(o_taps[dc]) else x for i, x in enumerate(column)]
+            for dc, column in e_taps.items()
+        }
+        count = n + (length + 1) // 2 - 1
+        summed = self.plane_sum(plane, count, at)
+        at = at + count
+        wa = wb = ws = None
+        if weights is not None:
+            we, wo = weights[0::2], weights[1::2]
+            wa = [we[0]] + [we[i] - wo[i - 1] for i in range(1, n)] + [0.0 - wo[n - 1]]
+            wb = [we[i] - wo[i] for i in range(n)]
+            ws = wo
+        a_out, a_grad = self.fast_rows(even, e_taps, n + 1, depth - 1, wa, at)
+        b_out, b_grad = self.fast_rows(odd, o_taps, n, depth - 1, wb, at)
+        s_out, s_grad = self.fast_rows(summed, s_taps, n, depth - 1, ws, at)
+        out, grads = [], {}
+        for i in range(n):
+            out += [a_out[i] + b_out[i], s_out[i] - a_out[i + 1] - b_out[i]]
+        if weights is not None:
+            for dc in taps:
+                column = []
+                for i in range(length):
+                    both = (a_grad if i % 2 == 0 else b_grad)[dc][i // 2]
+                    column.append(both + s_grad[dc][i // 2])
+                grads[dc] = column
+        return out, grads
+
+    def level(self, l, chunks, depth=1):
         s = self.s
         k = 2 * l + 3
         p = l + 1
         offset = s.kernel_at + sum(s.taps[:l])
-        source = self.pads[l]
-        per = s.side // block
-
-        def step(index, carry):
-            ch = chunks[0] + lax.div(index, per)
-            r0 = lax.rem(index, per) * block
-            acc = [None] * block
-            for dc in range(-p, p + 1):
-                taps = [
-                    self.vc[ch, pl.ds(offset + (dr + p) * k + dc + p, 1), :]
-                    for dr in range(-p, p + 1)
+
+        def step(ch, carry):
+            taps = {
+                dc: [
+                    self.vc[ch, pl.ds(offset + t * k + dc + p, 1), :]
+                    for t in range(k)
                 ]
-                for a in range(-p, block + p):
-                    x = source[ch, r0 + PAD + a, pl.ds(EDGE + dc, s.side), :]
-                    for o in range(max(0, a - p), min(block, a + p + 1)):
-                        term = x * taps[a - o + p]
-                        acc[o] = term if acc[o] is None else acc[o] + term
-            for o in range(block):
-                at = pl.ds(pl.multiple_of((r0 + o) * s.side, s.side), s.side)
+                for dc in range(-p, p + 1)
+            }
+            plane = (self.pads[l].at[ch], PAD - p, 1)
+            out, _ = self.fast_rows(plane, taps, s.side, depth)
+            for r in range(s.side):
+                at = slice(r * s.side, (r + 1) * s.side)
                 m = self.mask[at, :]
-                value, slope = gelu_parts(acc[o])
+                value, slope = gelu_parts(out[r])
                 value = value * m
-                self.gd[l][ch, r0 + o] = slope * m
-                self.pads[l + 1][ch, r0 + o + PAD, EDGE : EDGE + s.side, :] = value
+                self.gd[l][ch, r] = slope * m
+                self.pads[l + 1][ch, r + PAD, EDGE : EDGE + s.side, :] = value
                 term = value * self.gate[l, at, :]
                 if l:
-                    term = term + self.summed[ch, r0 + o]
-                self.summed[ch, r0 + o] = term
+                    term = term + self.summed[ch, r]
+                self.summed[ch, r] = term
             return carry
 
-        lax.fori_loop(0, len(chunks) * per, step, 0)
+        lax.fori_loop(chunks[0], chunks[-1] + 1, step, 0)
 
     def pooling(self):
         s = self.s
@@ -451,53 +518,37 @@
 
         lax.fori_loop(0, s.rows // BLK, last, 0)
 
-    def level_back(self, l, chunks, block=4):
+    def level_back(self, l, chunks, depth=2):
         s = self.s
         k = 2 * l + 3
         p = l + 1
         base = sum(s.taps[:l])
         offset = s.kernel_at + base
-        source = self.pads[l + 1]
-        inputs = self.pads[l]
-        per = s.side // block
-
-        def step(index, carry):
-            ch = chunks[0] + lax.div(index, per)
-            r0 = lax.rem(index, per) * block
-            acc = [None] * block
-            xs = [
-                inputs[ch, r0 + PAD + o, EDGE : EDGE + s.side, :] for o in range(block)
-            ]
-            for dc in range(-p, p + 1):
-                taps = [
-                    self.vc[ch, pl.ds(offset + (dr + p) * k + dc + p, 1), :]
-                    for dr in range(-p, p + 1)
+
+        def step(ch, carry):
+            taps = {
+                dc: [
+                    self.vc[ch, pl.ds(offset + (k - 1 - t) * k + p - dc, 1), :]
+                    for t in range(k)
                 ]
-                sums = [None] * k
-                for a in range(-p, block + p):
-                    d = source[ch, r0 + PAD + a, pl.ds(EDGE - dc, s.side), :]
-                    for o in range(max(0, a - p), min(block, a + p + 1)):
-                        dr = o - a
-                        term = d * taps[dr + p]
-                        acc[o] = term if acc[o] is None else acc[o] + term
-                        part = tall(d * xs[o])
-                        sums[dr + p] = part if sums[dr + p] is None else sums[dr + p] + part
-                for dr in range(-p, p + 1):
-                    tap = base + (dr + p) * k + dc + p
-                    self.gacc[ch, tap] = self.gacc[ch, tap] + sums[dr + p]
-            total = None
-            for o in range(block):
-                at = pl.ds(pl.multiple_of((r0 + o) * s.side, s.side), s.side)
+                for dc in range(-p, p + 1)
+            }
+            plane = (self.pads[l + 1].at[ch], PAD - p, 1)
+            inputs = [self.pads[l][ch, r + PAD, EDGE : EDGE + s.side, :] for r in range(s.side)]
+            out, grads = self.fast_rows(plane, taps, s.side, depth, inputs)
+            for dc, column in grads.items():
+                for t, value in enumerate(column):
+                    self.gacc[ch, base + (k - 1 - t) * k + p - dc] = value
+            for r in range(s.side):
+                at = slice(r * s.side, (r + 1) * s.side)
                 if l:
-                    e = acc[o] + self.dsum[ch, at, :] * self.gate[l - 1, at, :]
-                    self.pads[l][ch, r0 + o + PAD, EDGE : EDGE + s.side, :] = (
-                        e * self.gd[l - 1][ch, r0 + o]
-                    )
+                    e = out[r] + self.dsum[ch, at, :] * self.gate[l - 1, at, :]
+                    self.pads[l][ch, r + PAD, EDGE : EDGE + s.side, :] = e * self.gd[l - 1][ch, r]
                 else:
-                    self.summed[ch, r0 + o] = acc[o] * self.mask[at, :]
+                    self.summed[ch, r] = out[r] * self.mask[at, :]
             return carry
 
-        lax.fori_loop(0, len(chunks) * per, step, 0)
+        lax.fori_loop(chunks[0], chunks[-1] + 1, step, 0)
 
     def context_grad(self, chunks):
         s = self.s
@@ -522,7 +573,7 @@
         lanes = slice(chunks[0] * LANE, (chunks[-1] + 1) * LANE)
         self.put_gc(chunks, mm_g(self.n1b[...], self.dctxb[:, lanes]))
 
-    def last_back(self):
+    def last_sums(self):
         s = self.s
         wc = self.wc(tuple(range(s.nc)))
         self.dn[...] = mm_t(self.dqb[...], self.wq()) + mm_t(self.dctxb[...], wc)
@@ -538,16 +589,26 @@
                 dg = self.wide(self.dgate.at[l], at)
                 d = d + dg * weights[l]
                 sums.append(dg * n1)
-            e = d * gain
+            self.dn[at, :] = d
+            return (d * xh, d) + tuple(sums)
+
+        sums = self.blocks(step, 2 + GATES)
+        for index, total in zip((0, 1) + tuple(s.gate_at + l for l in range(GATES)), sums):
+            self.put(index, total)
+
+    def last_out(self):
+        s = self.s
+        gain = self.row(0)
+
+        def step(at, lines):
+            xh = self.xh1[at, :]
+            e = self.dn[at, :] * gain
             mean_e = lane_sum(e) * (1.0 / s.c)
             mean_x = lane_sum(e * xh) * (1.0 / s.c)
             d_in = self.dmid[at, :] + self.wide(self.r1, at) * (e - mean_e - xh * mean_x)
             self.store(self.grad, lines, d_in)
-            return (d * xh, d) + tuple(sums)
-
-        sums = self.blocks(step, 2 + GATES)
-        for index, total in zip((0, 1) + tuple(s.gate_at + l for l in range(GATES)), sums):
-            self.put(index, total)
+
+        self.blocks(step)
 
 
 MESH = pl.DeviceIdType.MESH
@@ -558,9 +619,11 @@
 weight_decay = 0.05
 VMEM_BYTES = 63 * 2**20 + 2**19
 GATHERED = "vabmes"
-REDUCED = "sedmqtu"
+REDUCED = "semqtu"
+PAIRS = "se"
 DIRECT = "qtu"
 NEAR = "va"
+HALVED = "es"
 AT_ONCE = "vab"
 
 
@@ -577,40 +640,61 @@
         self.rp2 = -(-self.rows2 // 16) * 16
         self.even = self.rp == self.rows and self.rp2 == self.rows2
         self.rv = self.rp // 2
-        self.gather_cols = dict(v=LANE, a=LANE, b=2 * LANE, m=s.c, e=s.hid // 2, s=s.c)
-        self.reduce_cols = dict(s=s.c, e=s.hid // 4, d=s.hid // 4, m=s.c, q=2 * LANE, t=LANE, u=LANE)
-
-    def piece(self, name, cols):
-        return (dict(s=self.rp2, v=self.rv).get(name, self.rp), cols[name])
-
-    def whole(self, name, cols):
+        self.gather_cols = dict(v=LANE, a=LANE, b=2 * LANE, m=s.c)
+        self.rs = self.rp2 // 2
+        self.reduce_cols = dict(s=s.c, e=s.hid // 4, m=s.c, q=2 * LANE, t=LANE, u=LANE)
+
+    def piece(self, name):
+        if name == "e":
+            return (2, self.rp, self.s.c)
+        if name == "s":
+            return (2, self.rs, self.s.c)
+        return (self.rv if name == "v" else self.rp, self.gather_cols[name])
+
+    def whole(self, name):
+        piece = self.piece(name)
+        if name == "e":
+            return (2, 2, self.Z, self.Y) + piece[1:]
         if name in "sv":
-            return (self.Z, self.Y, 2) + self.piece(name, cols)
-        return (2, self.Z, self.Y) + self.piece(name, cols)
+            return (self.Z, self.Y, 2) + piece
+        return (2, self.Z, self.Y) + piece
 
 
 def gather_scratch(p, name):
-    piece = p.piece(name, p.gather_cols)
+    piece = p.piece(name)
     kind = f32 if name == "v" else b16
+    passed = piece[1:] if name in HALVED and p.X == 2 else piece
     return dict(
         cand=pltpu.VMEM((2,) + piece, kind),
         rx1=pltpu.VMEM(piece, kind),
         sel=pltpu.VMEM(piece, kind),
-        rx2=pltpu.VMEM((p.X - 1, 2 if name in NEAR else 1) + piece, kind),
-        full=pltpu.VMEM(p.whole(name, p.gather_cols), kind),
+        rx2=pltpu.VMEM((p.X - 1, 2 if name in NEAR else 1) + passed, kind),
+        full=pltpu.VMEM(p.whole(name), kind),
     )
 
 
-def reduce_scratch(p, name):
-    piece = p.piece(name, p.reduce_cols)
+def reduce_piece(p, name):
+    return (p.rs if name == "s" else p.rp, p.reduce_cols[name])
+
+
+def fin_shape(p, name):
+    return (2, 2) + reduce_piece(p, name) if name in PAIRS else (2,) + reduce_piece(p, name)
+
+
+def grad_shape(p, name):
+    if name == "s":
+        return (p.Z, p.Y, 2, 2) + reduce_piece(p, name)
+    return ((2, 2) if name in PAIRS else (2,)) + (p.Z, p.Y) + reduce_piece(p, name)
+
+
+def steps_scratch(p, name):
+    piece = reduce_piece(p, name)
     out = dict(
-        grad=pltpu.VMEM(p.whole(name, p.reduce_cols), b16),
         r1=pltpu.VMEM((p.Z, p.Y) + piece, b16),
         a3=pltpu.VMEM(piece, b16),
         a4=pltpu.VMEM(piece, f32),
         r4=pltpu.VMEM((p.X - 1, 2) + piece, b16),
         r5=pltpu.VMEM(piece, b16),
-        fin=pltpu.VMEM((2,) + piece, f32),
     )
     if name in DIRECT:
         out["r3"] = pltpu.VMEM((p.fs - 1,) + piece, b16)
@@ -621,15 +705,28 @@
     return out
 
 
+def reduce_scratch(p, name):
+    out = dict(grad=pltpu.VMEM(grad_shape(p, name), b16), fin=pltpu.VMEM(fin_shape(p, name), f32))
+    if name not in PAIRS:
+        out["steps"] = steps_scratch(p, name)
+    elif p.X == 2:
+        out["steps"] = steps_scratch(p, name)
+        out["other"] = pltpu.VMEM((p.Z, p.Y) + reduce_piece(p, name), b16)
+        out["rx"] = pltpu.VMEM((p.Z, p.Y) + reduce_piece(p, name), b16)
+    else:
+        out["parts"] = [steps_scratch(p, name) for _ in range(2)]
+    return out
+
+
 def sem_count(p):
-    gather = 1 + 2 * (p.X - 1) + (p.Z - 1) + p.Z * (p.Y - 1) + p.fs
+    gather = 1 + 2 * (p.X - 1) + (p.Z - 1) + p.Z * (p.Y - 1) + 3 * p.fs
     reduce = 1 + max((p.Y - 1) + (p.Z - 1), p.fs - 1) + 2 * (p.X - 1) + 1
-    return gather * len(GATHERED) + reduce * len(REDUCED)
+    return gather * len(GATHERED) + reduce * (len(REDUCED) + len(PAIRS))
 
 
 class Links:
-    def __init__(self, p, send_sem, recv_sem):
-        self.p = p
+    def __init__(self, p, send_sem, recv_sem, column_sem):
+        self.p, self.column_sem = p, column_sem
         self.send_sem, self.recv_sem = send_sem, recv_sem
         self.used = 0
         self.sent = []
@@ -658,7 +755,8 @@
         partners = (
             [self.sibling()]
             + [self.at_x(lax.rem(self.x + d, p.X), i) for d in range(1, p.X) for i in range(2)]
-            + [(self.g, lax.rem(self.f + d, p.fs)) for d in range(1, p.fs)]
+            + [self.at_z(lax.rem(self.z + d, p.Z)) for d in range(1, p.Z)]
+            + [self.at_y(lax.rem(self.y + d, p.Y)) for d in range(1, p.Y)]
         )
         self.partners = len(partners)
         barrier = pltpu.get_barrier_semaphore()
@@ -667,6 +765,15 @@
 
     def wait_partners(self):
         pl.semaphore_wait(pltpu.get_barrier_semaphore(), self.partners)
+        self.heard = False
+        for d in range(1, self.p.Y):
+            partner = self.at_y(lax.rem(self.y + d, self.p.Y))
+            pl.semaphore_signal(self.column_sem, inc=1, device_id=partner, device_id_type=MESH)
+
+    def hear_columns(self):
+        if not self.heard:
+            pl.semaphore_wait(self.column_sem, self.p.Y - 1)
+            self.heard = True
 
     def send(self, source, target, partner, arriving=None):
         index = self.used
@@ -697,16 +804,26 @@
     def __init__(self, name, links, refs):
         self.name, self.links, self.p = name, links, links.p
         self.near, self.direct = name in NEAR, name in AT_ONCE
+        self.split = name in HALVED and links.p.X == 2
+        self.waitx = []
         self.__dict__.update(refs)
         self.held, self.wait3, self.wait4, self.wait5 = [], [], [], []
 
-    def piece(self, half, z, y):
+    def piece(self, half, z, y, x=None):
+        if self.split:
+            part = self.links.x if x is None else x
+            return self.full.at[z, y, half, part] if self.name == "s" else self.full.at[half, part, z, y]
+        if self.name == "e":
+            return self.full.at[half, :, z, y]
         return self.full.at[z, y, half] if self.name in "sv" else self.full.at[half, z, y]
 
     def core_send(self, z, y):
         k = self.links
         here = self.piece(k.c, z, y)
         self.wait5.append(k.send(here, here, k.sibling(), self.piece(1 - k.c, z, y)))
+        if self.split:
+            there = self.piece(k.c, z, y, 1 - k.x)
+            self.waitx.append((k.send(here, here, k.at_x(1 - k.x), there), z, y))
 
     def one(self):
         k, p = self.links, self.p
@@ -722,7 +839,9 @@
         k, p = self.links, self.p
         self.wait1()
         self.sel[...] = self.cand[k.c] + self.rx1[...]
-        if not self.near:
+        if self.split:
+            self.wait2 = [k.send(self.sel.at[1 - k.x], self.rx2.at[0, 0], k.at_x(1 - k.x))]
+        elif not self.near:
             self.wait2 = [
                 k.send(self.sel, self.rx2.at[d - 1, 0], k.at_x(lax.rem(k.x + d, p.X)))
                 for d in range(1, p.X)
@@ -752,7 +871,7 @@
         k, p = self.links, self.p
         for wait in self.wait2:
             wait()
-        total = self.sel[...]
+        total = self.sel[k.x] if self.split else self.sel[...]
         for d in range(p.X - 1):
             for i in range(2 if self.near else 1):
                 total = total + self.rx2[d, i]
@@ -790,19 +909,24 @@
             wait()
             self.core_send(z, y)
 
+    def cross(self):
+        k = self.links
+        for wait, z, y in self.waitx:
+            wait()
+            here = self.piece(k.c, z, y, 1 - k.x)
+            self.wait5.append(k.send(here, here, k.sibling(), self.piece(1 - k.c, z, y, 1 - k.x)))
+
     def six(self):
         for wait in self.wait5:
             wait()
 
 
 class Reduce:
-    def __init__(self, name, links, refs):
+    def __init__(self, name, links, refs, half, fin):
         self.name, self.links, self.p = name, links, links.p
         self.direct = name in DIRECT
         self.__dict__.update(refs)
-
-    def half(self, h):
-        return self.grad.at[:, :, h] if self.name == "s" else self.grad.at[h]
+        self.half, self.fin = half, fin
 
     def one(self):
         k = self.links
@@ -821,6 +945,7 @@
         lax.fori_loop(0, p.fs, add, 0)
         self.wait2 = []
         if self.direct:
+            k.hear_columns()
             for d in range(1, p.fs):
                 f = lax.rem(k.f + d, p.fs)
                 source = self.r1.at[lax.div(f, p.Y), lax.rem(f, p.Y)]
@@ -898,7 +1023,86 @@
         for h, total, i in ((k.c, self.a4[...], 0), (1 - k.c, self.r5[...].astype(f32), 1)):
             for d in range(p.X - 1):
                 total = total + self.r4[d, i].astype(f32)
-            self.fin[h] = total
+            self.fin(h)[...] = total
+
+
+class Pair(Reduce):
+    def __init__(self, name, links, refs):
+        grad, fin = refs["grad"], refs["fin"]
+
+        def half(h, part):
+            return grad.at[:, :, h, part] if name == "s" else grad.at[h, part]
+
+        self.parts = []
+        if "parts" in refs:
+            for part, steps in enumerate(refs["parts"]):
+                reduce = Reduce(
+                    name, links, steps, lambda h, part=part: half(h, part), lambda h, part=part: fin.at[h, part]
+                )
+                self.parts.append(reduce)
+            return
+        super().__init__(name, links, refs["steps"], half, fin)
+        self.rx, self.other, self.all_fin = refs["rx"], refs["other"], fin
+
+    def one(self):
+        if self.parts:
+            return [part.one() for part in self.parts]
+        k = self.links
+        self.wait1 = [
+            k.send(self.half(1 - k.c, 1 - k.x), self.other, k.sibling()),
+            k.send(self.half(1 - k.c, k.x), self.r1, k.sibling()),
+        ]
+
+    def add_pieces(self, total, term):
+        p = self.p
+
+        def add(index, carry):
+            z, y = lax.div(index, p.Y), lax.rem(index, p.Y)
+            total[z, y] = total[z, y] + term[z, y]
+            return carry
+
+        lax.fori_loop(0, p.fs, add, 0)
+
+    def two(self):
+        if self.parts:
+            return [part.two() for part in self.parts]
+        k = self.links
+        self.wait1[0]()
+        self.add_pieces(self.other, self.half(k.c, 1 - k.x))
+        self.waitx = k.send(self.other, self.rx, k.at_x(1 - k.x))
+        self.wait1[1]()
+        self.add_pieces(self.r1, self.half(k.c, k.x))
+
+    def across(self):
+        if self.parts:
+            return
+        k, p = self.links, self.p
+        self.waitx()
+        self.add_pieces(self.r1, self.rx)
+        self.wait2 = []
+        for d in range(1, p.Y):
+            other = lax.rem(k.y + d, p.Y)
+            self.wait2.append(k.send(self.r1.at[:, other], self.r2.at[d - 1], k.at_y(other)))
+
+    def three(self):
+        return [part.three() for part in self.parts] if self.parts else super().three()
+
+    def four(self):
+        return [part.four() for part in self.parts] if self.parts else super().four()
+
+    def five(self):
+        return [part.five() for part in self.parts] if self.parts else super().five()
+
+    def six(self):
+        if self.parts:
+            return [part.six() for part in self.parts]
+        k = self.links
+        for wait in self.wait4:
+            wait()
+        self.all_fin[k.c, k.x] = self.a4[...]
+        self.all_fin[1 - k.c, k.x] = self.r5[...].astype(f32)
+        self.all_fin[k.c, 1 - k.x] = self.r4[0, 0].astype(f32)
+        self.all_fin[1 - k.c, 1 - k.x] = self.r4[0, 1].astype(f32)
 
 
 def spread_matrix(rows, rp, count):
@@ -916,9 +1120,9 @@
     count, sides, owners = refs[:3]
     sources = dict(zip(("x", "cot", "focal", "modulate", "project", "expand", "shrink", "vector"), refs[3:11]))
     out_hbm, grad_hbm = refs[11:13]
-    fin_hbm = dict(zip(REDUCED, refs[13:20]))
-    own = jax.tree.unflatten(tree, refs[20:])
-    k = Links(p, own["send_sem"], own["recv_sem"])
+    fin_hbm = dict(zip(REDUCED, refs[13:19]))
+    own = jax.tree.unflatten(tree, refs[19:])
+    k = Links(p, own["send_sem"], own["recv_sem"], own["column_sem"])
     land, local_sem = own["land"], own["local_sem"]
     local_used = []
 
@@ -942,46 +1146,60 @@
         return jnp.concatenate([values, jnp.zeros((rp - rows, values.shape[1]), f32)], axis=0)
 
     def candidate(name, h, values):
-        rows, rp = values.shape[0], p.piece(name, p.gather_cols)[0]
-        own["g" + name]["cand"][h] = cut(values, rows, rp).astype(b16)
+        rows, rp = values.shape[0], p.rp2 if name == "s" else p.rp
+        low, target = cut(values, rows, rp).astype(b16), own["g" + name]["cand"]
+        if name == "e":
+            for part in range(2):
+                target[h, part] = low[:, part * c : (part + 1) * c]
+        elif name == "s":
+            for part in range(2):
+                target[h, part] = low[part * p.rs : (part + 1) * p.rs]
+        else:
+            target[h] = low
 
     gathers = {
         name: Gather(name, k, own["g" + name]) for name in GATHERED
     }
     gv, ga, gb, gm, ge, gs = (gathers[name] for name in GATHERED)
-    reduces = {name: Reduce(name, k, own["r" + name]) for name in REDUCED}
-    rs, re, rd, rm, rq, rt, ru = (reduces[name] for name in REDUCED)
+    reduces = {}
+    for name in REDUCED:
+        refs = own["r" + name]
+        if name in PAIRS:
+            reduces[name] = Pair(name, k, refs)
+        else:
+            reduces[name] = Reduce(
+                name, k, refs["steps"], lambda h, r=refs: r["grad"].at[h], lambda h, r=refs: r["fin"].at[h]
+            )
+    rs, re, rm, rq, rt, ru = (reduces[name] for name in REDUCED)
     c, wide = s.c, s.hid // 2
 
-    loads["focal"].wait()
-    loads["vector"].wait()
-    focal = land["focal"]
-    values = cut(land["vector"][...] * mine(5), p.rows, p.rp)
-    values = jnp.concatenate([values, jnp.zeros((p.rp, LANE - s.nvec), f32)], axis=1)
-    for h in range(2):
-        own["gv"]["cand"][h] = values[h * p.rv : (h + 1) * p.rv]
-        at = c + h * LANE
-        candidate("a", h, focal[:, at : at + LANE] * mine(0))
-    k.wait_partners()
-    gv.one()
-    ga.one()
-    candidate("b", 0, jnp.concatenate([focal[:, c + 2 * LANE :], focal[:, :LANE]], axis=1) * mine(0))
-    candidate("b", 1, focal[:, LANE:c] * mine(0))
-    gb.one()
-    loads["modulate"].wait()
-    loads["project"].wait()
-    candidate("m", 0, land["modulate"][...] * mine(1))
-    candidate("m", 1, land["project"][...] * mine(2))
-    gm.one()
-    gb.two()
-    loads["expand"].wait()
-    for h in range(2):
-        candidate("e", h, land["expand"][:, h * wide : (h + 1) * wide] * mine(3))
-    ge.one()
-    loads["shrink"].wait()
-    for h in range(2):
-        candidate("s", h, land["shrink"][h * p.rows2 : (h + 1) * p.rows2, :] * mine(4))
-    gs.one()
+    def prepare():
+        block.prepare()
+        own["gvec"][s.nvec :, :] = jnp.zeros((LANE - s.nvec, s.c), f32)
+        put("q", 1, LANE, jnp.zeros((s.c, LANE), f32))
+        loads["focal"].wait()
+        loads["vector"].wait()
+        values = cut(land["vector"][...] * mine(5), p.rows, p.rp)
+        values = jnp.concatenate([values, jnp.zeros((p.rp, LANE - s.nvec), f32)], axis=1)
+        focal = land["focal"]
+        for h in range(2):
+            own["gv"]["cand"][h] = values[h * p.rv : (h + 1) * p.rv]
+            at = c + h * LANE
+            candidate("a", h, focal[:, at : at + LANE] * mine(0))
+        candidate("b", 0, jnp.concatenate([focal[:, c + 2 * LANE :], focal[:, :LANE]], axis=1) * mine(0))
+        candidate("b", 1, focal[:, LANE:c] * mine(0))
+        loads["modulate"].wait()
+        loads["project"].wait()
+        candidate("m", 0, land["modulate"][...] * mine(1))
+        candidate("m", 1, land["project"][...] * mine(2))
+        loads["expand"].wait()
+        for h in range(2):
+            candidate("e", h, land["expand"][:, h * wide : (h + 1) * wide] * mine(3))
+        loads["shrink"].wait()
+        for h in range(2):
+            candidate("s", h, land["shrink"][h * p.rows2 : (h + 1) * p.rows2, :] * mine(4))
+        loads["x"].wait()
+        block.first_norm()
 
     if not p.even:
         own["map"][...] = spread_matrix(p.rows, p.rp, p.fs)
@@ -996,6 +1214,15 @@
     def matrix(name, h, at, cols):
         part = own["g" + name]["full"][h, :, :, :, at : at + cols]
         return compact(part.reshape(p.fs * p.rp, cols))
+
+    def take_expand(h, at, cols):
+        parts = []
+        for part in range(2):
+            first, last = max(at, part * c), min(at + cols, (part + 1) * c)
+            if first < last:
+                values = own["ge"]["full"][h, part, :, :, :, first - part * c : last - part * c]
+                parts.append(compact(values.reshape(p.fs * p.rp, last - first)))
+        return jnp.concatenate(parts, axis=1) if len(parts) > 1 else parts[0]
 
     def take_context(chunks):
         parts = []
@@ -1018,6 +1245,10 @@
         grads = spread(values).reshape(p.Z, p.Y, p.rp, cols)
         own["r" + name]["grad"][h, :, :, :, at : at + cols] = grads
 
+    def put_expand(h, at, values):
+        grads = spread(values).reshape(p.Z, p.Y, p.rp, values.shape[1])
+        own["re"]["grad"][h, 1 if at else 0] = grads
+
     def put_query(values):
         put("q", 0, 0, values[:, : 2 * LANE])
         put("q", 1, 0, values[:, 2 * LANE :])
@@ -1034,10 +1265,10 @@
             return
         start = at
         while start < at + rows:
-            piece, inner = divmod(start, p.rp2)
-            size = min(p.rp2 - inner, at + rows - start)
-            (f, h), first = divmod(piece, 2), start - at
-            own["rs"]["grad"][f // p.Y, f % p.Y, h, inner : inner + size, :] = low[first : first + size]
+            piece, inner = divmod(start, p.rs)
+            size = min(p.rs - inner, at + rows - start)
+            (f, h), part, first = divmod(piece // 2, 2), piece % 2, start - at
+            own["rs"]["grad"][f // p.Y, f % p.Y, h, part, inner : inner + size, :] = low[first : first + size]
             start += size
 
     block = Compute(
@@ -1055,13 +1286,13 @@
             wq=take_query,
             wh=lambda: matrix("m", 0, 0, c),
             wp=lambda: matrix("m", 1, 0, c),
-            w1=lambda h, at, cols: matrix("e", h, at, cols),
+            w1=take_expand,
             w2=take_shrink,
             put_gq=put_query,
             put_gc=put_context,
             put_gh=lambda values: put("m", 0, 0, values),
             put_gp=lambda values: put("m", 1, 0, values),
-            put_g1=lambda h, at, values: put("d" if at else "e", h, 0, values),
+            put_g1=put_expand,
             put_g2=put_shrink,
         ),
         own["compute"],
@@ -1072,12 +1303,6 @@
     def settle(name):
         reduces[name].six()
         stores.append(local(own["r" + name]["fin"], fin_hbm[name]))
-
-    def prepare():
-        loads["x"].wait()
-        block.prepare()
-        own["gvec"][s.nvec :, :] = jnp.zeros((LANE - s.nvec, s.c), f32)
-        put("q", 1, LANE, jnp.zeros((s.c, LANE), f32))
 
     def take_vector():
         vector = own["gv"]["full"][...].reshape(p.fs * p.rp, LANE)
@@ -1092,7 +1317,9 @@
     def close_shrink():
         def close(f, carry):
             z, y = lax.div(f, p.Y), lax.rem(f, p.Y)
-            parts = [own["gs"]["full"][z, y, h].astype(f32)[: p.rows2] for h in range(2)]
+            parts = [
+                own["gs"]["full"][z, y, h].astype(f32).reshape(p.rp2, s.c)[: p.rows2] for h in range(2)
+            ]
             at = pl.ds(pl.multiple_of(f * 2 * p.rows2, 2 * p.rows2), 2 * p.rows2)
             own["w2n"][at, :] = jnp.concatenate(parts, axis=0).astype(b16)
             return carry
@@ -1109,7 +1336,7 @@
             both = own["g2n"][at, :].astype(f32)
             for h in range(2):
                 part = cut(both[h * p.rows2 : (h + 1) * p.rows2], p.rows2, p.rp2)
-                own["rs"]["grad"][z, y, h] = part.astype(b16)
+                own["rs"]["grad"][z, y, h] = part.reshape(2, p.rs, s.c).astype(b16)
             return carry
 
         if not p.even:
@@ -1119,8 +1346,8 @@
         block.middle()
         stores.append(local(own["out"], out_hbm.at[0]))
 
-    def last_back():
-        block.last_back()
+    def last_out():
+        block.last_out()
         stores.append(local(own["grad"], grad_hbm.at[0]))
 
     def put_vector():
@@ -1129,117 +1356,124 @@
             grads = mm_g(own["map"][...], grads.astype(b16))
         own["ru"]["grad"][1] = grads.astype(b16).reshape(p.Z, p.Y, p.rp, LANE)
 
-    gm.two()
+    prepare()
+    k.wait_partners()
+    gv.one()
+    gb.one()
+    gs.one()
+    ge.one()
+    ga.one()
+    gm.one()
+    ge.two()
     ga.two()
     gv.two()
     gv.three()
+    gb.two()
     ga.three()
-    ge.two()
+    gm.two()
+    ge.three()
+    gs.two()
     gb.three()
+    ga.own()
+    gb.own()
     gv.own()
+    gv.four()
     gm.three()
-    ga.own()
-    gs.two()
+    ga.four()
+    gs.three()
+    ge.own()
+    gv.five()
+    ge.four()
+    gs.own()
     gm.own()
-    ge.three()
-    gb.own()
-    gv.four()
-    ge.own()
-    gs.three()
-    ga.four()
-    gv.five()
+    gv.six()
+    take_vector()
+    ga.five()
+    block.first()
     gb.four()
-    gv.six()
-    prepare()
-    ge.four()
-    take_vector()
-    gs.own()
-    gm.four()
-    ga.five()
-    gb.five()
-    block.first()
     ga.six()
     block.context((0, 1))
     block.level(0, (0, 1))
+    block.level(1, (0, 1))
+    gm.four()
+    block.level(2, (0, 1))
+    ge.four()
     gs.four()
-    block.level(1, (0, 1))
-    ge.four()
+    gb.five()
     gb.six()
     block.context((2,))
-    block.level(2, (0, 1))
-    gm.four()
     block.level(0, (2,))
     block.query()
+    gm.four()
+    ge.five()
+    gs.four()
     block.level(1, (2,))
-    gs.four()
-    ge.five()
     block.level(2, (2,))
     gm.five()
-    ge.six()
     block.pooling()
     gm.six()
+    gs.five()
+    ge.cross()
     modulate()
-    gs.five()
+    ge.six()
     block.feed()
-    gs.six()
+    gs.cross()
     shrink_grad()
     rs.one()
+    gs.six()
     close_shrink()
     block.feed_back()
     block.expand_grad()
     rs.two()
+    block.feed_out()
     re.one()
-    block.feed_out()
     middle()
     block.query_grad()
     block.middle_grads()
+    rm.one()
     rq.one()
-    rm.one()
     block.focal_top()
     re.two()
     rm.two()
     rq.two()
     block.level_back(2, (0, 1))
-    rs.three()
+    rs.across()
     block.level_back(1, (0, 1))
-    rd.one()
-    re.three()
     block.level_back(0, (0, 1))
-    rd.two()
+    rm.three()
     block.context_grad((0, 1))
-    rm.three()
     rt.one()
-    rs.four()
+    block.level_back(2, (2,))
     rt.two()
-    block.level_back(2, (2,))
     block.level_back(1, (2,))
     block.level_back(0, (2,))
-    rd.three()
+    re.across()
+    rm.four()
     block.context_grad((2,))
-    re.four()
     rq.three()
-    last_back()
-    rm.four()
-    rs.five()
+    block.last_sums()
+    rq.five()
+    rs.three()
     put_vector()
     ru.one()
-    rq.five()
+    last_out()
     ru.two()
-    rd.four()
+    rt.three()
+    re.three()
+    settle("q")
+    rm.five()
+    rs.four()
+    ru.three()
+    re.four()
+    settle("m")
+    ru.five()
+    rt.five()
+    rs.five()
     re.five()
-    rt.three()
-    rm.five()
-    rt.five()
-    ru.three()
-    ru.five()
-    rd.five()
+    settle("t")
+    settle("u")
+    settle("s")
     settle("e")
-    settle("m")
-    settle("s")
-    settle("u")
-    settle("t")
-    settle("q")
-    settle("d")
     k.finish()
     for store in stores:
         store.wait()
@@ -1248,10 +1482,10 @@
 def adam_kernel(p, rates, tree, *refs):
     s = p.s
     owners = refs[0]
-    fins = dict(zip(REDUCED, refs[1:8]))
-    passed, olds = refs[8:10], refs[10:28]
-    passed_out, news = refs[28:30], refs[30:48]
-    own = jax.tree.unflatten(tree, refs[48:])
+    fins = dict(zip(REDUCED, refs[1:7]))
+    passed, olds = refs[7:9], refs[9:27]
+    passed_out, news = refs[27:29], refs[29:47]
+    own = jax.tree.unflatten(tree, refs[47:])
     sems = own["sem"]
     g = lax.axis_index("grp")
     used = []
@@ -1264,8 +1498,15 @@
 
     wide = s.hid // 2
     groups = (
-        (3, [(n, h, 0, p.rows, h * wide + i * s.c, s.c) for h in range(2) for i, n in enumerate("ed")]),
-        (4, [("s", h, h * p.rows2, p.rows2, 0, s.c) for h in range(2)]),
+        (3, [("e", (h, i), 0, p.rows, h * wide + i * s.c, s.c) for h in range(2) for i in range(2)]),
+        (
+            4,
+            [
+                ("s", (h, i), h * p.rows2 + i * p.rs, min(p.rows2 - i * p.rs, p.rs), 0, s.c)
+                for h in range(2)
+                for i in range(2)
+            ],
+        ),
         (1, [("m", 0, 0, p.rows, 0, s.c)]),
         (2, [("m", 1, 0, p.rows, 0, s.c)]),
         (
@@ -1299,7 +1540,7 @@
                 arrived.add(name)
                 waits[name].wait()
             at = (0, slice(row, row + rows), slice(col, col + cols))
-            gradient = own["fin"][name][h, :rows, :cols]
+            gradient = own["fin"][name].at[h][:rows, :cols]
             weight, first, second = (own["old"][3 * index + i][at] for i in range(3))
             first_new = beta_one * first + (1.0 - beta_one) * gradient
             second_new = beta_two * second + (1.0 - beta_two) * gradient * gradient
@@ -1347,6 +1588,7 @@
             local_sem=pltpu.SemaphoreType.DMA((24,)),
             send_sem=pltpu.SemaphoreType.DMA((sem_count(p),)),
             recv_sem=pltpu.SemaphoreType.DMA((sem_count(p),)),
+            column_sem=pltpu.SemaphoreType.REGULAR,
         )
         for name in GATHERED:
             scratch["g" + name] = gather_scratch(p, name)
@@ -1364,14 +1606,14 @@
         anywhere = pl.BlockSpec(memory_space=pl.ANY)
         smem = pl.BlockSpec(memory_space=pltpu.SMEM)
         shape = jax.ShapeDtypeStruct
-        fins = [shape((2,) + p.piece(name, p.reduce_cols), f32) for name in REDUCED]
+        fins = [shape(fin_shape(p, name), f32) for name in REDUCED]
         images = [shape(image_patches.shape, b16), shape(image_patches.shape, f32)]
         tensors = tensors[:15] + tuple(t.transpose(0, 2, 1) for t in tensors[15:])
         results = pl.pallas_call(
             lambda *refs: block_kernel(p, tree, *refs),
             out_shape=images + fins,
             in_specs=[smem] * 3 + [anywhere] * 8,
-            out_specs=[anywhere] * 9,
+            out_specs=[anywhere] * 8,
             scratch_shapes=leaves,
             compiler_params=pltpu.CompilerParams(
                 collective_id=0, has_side_effects=True, vmem_limit_bytes=VMEM_BYTES
@@ -1389,7 +1631,7 @@
         rates = (wide_rate,) * 4 + (1.5 / math.sqrt(hid), 0.2)
         adam_leaves, adam_tree = flatten(
             dict(
-                fin={name: pltpu.VMEM((2,) + p.piece(name, p.reduce_cols), f32) for name in REDUCED},
+                fin={name: pltpu.VMEM(fin_shape(p, name), f32) for name in REDUCED},
                 old=[pltpu.VMEM(t.shape, f32) for t in tensors],
                 new=[pltpu.VMEM(t.shape, f32) for t in tensors],
                 passed=[pltpu.VMEM(t.shape, t.dtype) for t in images],
@@ -1399,7 +1641,7 @@
         news = pl.pallas_call(
             lambda *refs: adam_kernel(p, rates, adam_tree, *refs),
             out_shape=images + [shape(t.shape, f32) for t in tensors],
-            in_specs=[smem] + [anywhere] * 27,
+            in_specs=[smem] + [anywhere] * 26,
             out_specs=[anywhere] * 20,
             scratch_shapes=adam_leaves,
             compiler_params=pltpu.CompilerParams(vmem_limit_bytes=VMEM_BYTES),

time: 92.5 us -> 85.9 us (0.929)
  Pallas kernels: 90.2 us -> 83.5 us
    pallas_call x1, Pallas kernels: 85.3 us -> 78.7 us  [shards(): pl.pallas_call(lambda *refs: block_kernel(p, tree, *refs), out_shape=imag...]
where the time goes in v3:
time: 85.9 us; the launch traced here: 85.7 us
  Pallas kernels  83.5 us (97%)
  between operations  2.16 us (3%)
    pallas_call x1, Pallas kernels, shards(): pl.pallas_call(lambda *refs: block_kernel(p, tree, *refs), out_shape=imag...  78.7 us
    pallas_call x1, Pallas kernels, shards(): pl.pallas_call(lambda *refs: adam_kernel(p, rates, adam_tree, *refs), out...  4.82 us

profile of v3, /device:TPU:0, one launch (start us, length us, event | category | flops | bytes accessed | tf_op | source)
XLA Modules:
  0.0 85.7 jit_solution(10598850940815008008)
XLA Ops:
  1.9 78.7 %block.1 = (bf16[1,24,24,384]{3,2,1,0:T(8,128)(2,1)}, f32[1,24,24,384]{3,2,1,0:T(8,128)}, f32[2,2,48,384]{3,2,1,0:T(8,128)}, f32[2,2,48,384]{3,2,1,0:T(8,128)}, ...) custom-call(s32[1,1]{1,0:T(1,128)S(6)} %copy.43.refs_0_, ...), custom_call_target="tpu_custom_call" | custom-call | tf_op jit(solution)/shard_map/block/pallas_call | solution.py:1612
  80.6 4.8 %adam.1 = (bf16[1,24,24,384]{3,2,1,0:T(8,128)(2,1)}, f32[1,24,24,384]{3,2,1,0:T(8,128)}, f32[1,48,768]{2,1,0:T(8,128)}, f32[1,48,768]{2,1,0:T(8,128)}, f32[1,48,...) custom-call(s32[6]{0:T(128)} %refs_0_.2, ...), custom_call_target="tpu_custom_call" | custom-call | tf_op jit(solution)/shard_map/adam/pallas_call | solution.py:1641

commit v4 on v3

--- a/solution.py
+++ b/solution.py
@@ -17,20 +17,13 @@
 EDGE = 8
 SQRT_HALF = math.sqrt(0.5)
 INV_SQRT_2PI = 1.0 / math.sqrt(2.0 * math.pi)
+HALF_LOG2E = -0.5 / math.log(2.0)
 BLK = 576
 
 
 def gelu_parts(z):
-    az = jnp.abs(z)
-    t = 1.0 / (1.0 + (0.3275911 * SQRT_HALF) * az)
-    e = jnp.exp(z * z * -0.5)
-    poly = t * (
-        0.5 * 0.254829592
-        + t * (0.5 * -0.284496736 + t * (0.5 * 1.421413741 + t * (0.5 * -1.453152027 + t * (0.5 * 1.061405429))))
-    )
-    tail = poly * e
-    phi = jnp.where(z >= 0.0, 1.0 - tail, tail)
-    return z * phi, phi + z * e * INV_SQRT_2PI
+    phi = 0.5 + 0.5 * lax.erf(z * SQRT_HALF)
+    return z * phi, phi + (z * INV_SQRT_2PI) * jnp.exp2(z * z * HALF_LOG2E)
 
 
 def mm(a, b):
@@ -1474,6 +1467,7 @@
     settle("u")
     settle("s")
     settle("e")
+    k.hear_columns()
     k.finish()
     for store in stores:
         store.wait()

time: 85.9 us -> 84.8 us (0.987)
  Pallas kernels: 83.5 us -> 82.5 us
    pallas_call x1, Pallas kernels: 78.7 us -> 77.6 us  [shards(): pl.pallas_call(lambda *refs: block_kernel(p, tree, *refs), out_shape=imag...]
where the time goes in v4:
time: 84.8 us; the launch traced here: 84.6 us
  Pallas kernels  82.5 us (97%)
  between operations  2.16 us (3%)
    pallas_call x1, Pallas kernels, shards(): pl.pallas_call(lambda *refs: block_kernel(p, tree, *refs), out_shape=imag...  77.6 us
    pallas_call x1, Pallas kernels, shards(): pl.pallas_call(lambda *refs: adam_kernel(p, rates, adam_tree, *refs), out...  4.82 us

profile of v4, /device:TPU:0, one launch (start us, length us, event | category | flops | bytes accessed | tf_op | source)
XLA Modules:
  0.0 84.6 jit_solution(11572981337434659585)
XLA Ops:
  1.9 77.6 %block.1 = (bf16[1,24,24,384]{3,2,1,0:T(8,128)(2,1)}, f32[1,24,24,384]{3,2,1,0:T(8,128)}, f32[2,2,48,384]{3,2,1,0:T(8,128)}, f32[2,2,48,384]{3,2,1,0:T(8,128)}, ...) custom-call(s32[1,1]{1,0:T(1,128)S(6)} %copy.43.refs_0_, ...), custom_call_target="tpu_custom_call" | custom-call | tf_op jit(solution)/shard_map/block/pallas_call | solution.py:1606
  79.6 4.8 %adam.1 = (bf16[1,24,24,384]{3,2,1,0:T(8,128)(2,1)}, f32[1,24,24,384]{3,2,1,0:T(8,128)}, f32[1,48,768]{2,1,0:T(8,128)}, f32[1,48,768]{2,1,0:T(8,128)}, f32[1,48,...) custom-call(s32[6]{0:T(128)} %refs_0_.2, ...), custom_call_target="tpu_custom_call" | custom-call | tf_op jit(solution)/shard_map/adam/pallas_call | solution.py:1635
